TPU v7x, 128 devices: a whole 4x4x4 slice. The times are simulated.
128 devices in a mesh: row: 16 (over x, z), col: 8 (over y, core).
Axes of the slice: x: 4, y: 4, z: 4, core: 2. Of those that a mesh axis runs over, the one named last changes fastest.
Arguments:
- blocks: bfloat16 [16, 8, 96, 256, 256], P('row', 'col'), may hold values from -6 to 6
- sketch: bfloat16 [262144, 128], P('col'), may hold values from -6 to 6
- block_row: int32 [16, 8, 96], P('row', 'col'), may hold values from 0 to 127, as said below
- block_col: int32 [16, 8, 96], P('row', 'col'), may hold values from 0 to 127
- counts: int32 [16, 8], P('row', 'col'), may hold values from 12 to 96, as said below
Outputs:
- q_scaled: float32 [524288, 128], P(('row', 'col'))
- z_out: float32 [8, 32768, 128], P('col', 'row')
Inputs may be any that keep to these rules, and one draw needn't show every extreme that they name: `block_row`: block row of a slot among the 128 block rows of its device. `counts`: slots at or beyond a device's count are not part of the matrix.
All inputs are finite; a program needn't handle non-finite values.
Results may differ from a plain program's by a relative error of at most 0.0019.
Values may be sent and summed in bfloat16 or wider, within the bound.
No kernel may reach another device: no remote copies, remote signals or barrier semaphores. Data moves between devices by JAX's collectives and lax.ppermute only.
A program may use at most 192 MiB of HBM per device.

v0:
```python
import math

import jax
import jax.numpy as jnp
from jax import lax
from jax.experimental import pallas as pl
from jax.experimental.layout import Layout, with_layout_constraint
from jax.experimental.pallas import tpu as pltpu
from jax.sharding import PartitionSpec as P

B = 256
K = 128
BR = 128
BC = 128
NBLK = 96
CHUNK = 8
AHEAD = 28
GROUP = 4
BUFFERS = AHEAD + GROUP
VMEM_BYTES = 56 * 1024 * 1024
f32 = jnp.float32
f16 = jnp.float16


def ring(shift):
    return [(c, ((c // 2 + shift) % 4) * 2 + c % 2) for c in range(8)]


def along_x(shift):
    return [(r, ((r // 4 + shift) % 4) * 4 + r % 4) for r in range(16)]


def along_z(shift):
    return [(r, (r // 4) * 4 + (r % 4 + shift) % 4) for r in range(16)]


SHARE_ROWS = BR // 8 * B + 2 * K + 32
LOW_SCALE = 2.0**15

PAIR = [(c, c ^ 1) for c in range(8)]


def run_slots(parts, count, targets, order, bounds, begin, group, carry, total_sum, outs, out_sems):
    chunks = total_sum.shape[0] // CHUNK

    def chunk_of(s):
        return jnp.where(targets[s] < 0, chunks, targets[s] // CHUNK)

    for c in range(chunks + 1):
        bounds[c] = 0

    def tally(s, _):
        c = chunk_of(s)
        bounds[c] = bounds[c] + 1
        return 0

    lax.fori_loop(0, count, tally, 0)
    total = 0
    for c in range(chunks):
        here = bounds[c]
        bounds[c] = total
        total = total + here
    bounds[chunks] = total

    def place(s, _):
        c = chunk_of(s)
        at = bounds[c]
        order[at] = s
        bounds[c] = at + 1
        return 0

    lax.fori_loop(0, count, place, 0)

    def begin_later(j):
        @pl.when(j < total)
        def _():
            begin(j, 0)

    lax.fori_loop(0, jnp.minimum(total, AHEAD), begin, 0)

    def clear(t, _):
        total_sum[t] = jnp.zeros((B, K), f32)
        return 0

    lax.fori_loop(0, chunks * CHUNK, clear, 0)

    writes = [[] for _ in range(chunks)]
    first = 0
    for ring_at in range(len(outs) // len(parts)):
        for i, tiles in enumerate(parts):
            at = ring_at * len(parts) + i
            for piece in range(0, tiles, CHUNK):
                size = min(CHUNK, tiles)
                sem = sum(len(w) for w in writes)
                writes[first // CHUNK].append(
                    pltpu.make_async_copy(
                        total_sum.at[pl.ds(first, size)],
                        outs[at].at[pl.ds(piece, size)],
                        out_sems.at[sem],
                    )
                )
                first += size

    def write_done(done, chunk):
        def step(c):
            for i, pieces in enumerate(writes):

                @pl.when(c == i)
                def _():
                    for copy in pieces:
                        copy.start()

            return c + 1

        return lax.while_loop(
            lambda c: (c < chunks) & (bounds[jnp.minimum(c, chunks - 1)] <= done), step, chunk
        )

    def by_group(size, first):
        def step(g, state):
            chunk, carry = state
            at = first + g * size
            carry = group(begin_later, at, size, carry)
            return write_done(at + size, chunk), carry

        return step

    groups = total // GROUP
    state = write_done(0, 0), carry
    state = lax.fori_loop(0, groups, by_group(GROUP, 0), state)
    state = lax.fori_loop(0, total - groups * GROUP, by_group(1, groups * GROUP), state)
    for pieces in writes:
        for copy in pieces:
            copy.wait()
    return state[1]


def y_kernel(count, targets, cols, blocks, sketch, *rest):
    outs, stat, scratch = rest[:3], rest[3], rest[4:]
    total_sum, order, bounds, block_buf, sketch_buf, sems, out_sems = scratch

    def copies(j):
        s, at = order[j], lax.rem(j, BUFFERS)
        return (
            pltpu.make_async_copy(blocks.at[s], block_buf.at[at], sems.at[0, at]),
            pltpu.make_async_copy(sketch.at[cols[s]], sketch_buf.at[at], sems.at[1, at]),
        )

    def begin(j, _):
        for copy in copies(j):
            copy.start()
        return 0

    def group(begin_later, at, size, carry):
        largest, largest_block = carry
        for u in range(size):
            begin_later(at + u + AHEAD)
        for u in range(size):
            for copy in copies(at + u):
                copy.wait()
        for u in range(size):
            target = targets[order[at + u]]
            buffer = lax.rem(at + u, BUFFERS)
            tile = block_buf[buffer]
            value = total_sum[target] + jnp.dot(
                tile, sketch_buf[buffer], preferred_element_type=f32
            )
            total_sum[target] = value
            largest = jnp.maximum(largest, jnp.max(jnp.abs(value).reshape(B // 8, 8, K), axis=0))
            largest_block = jnp.maximum(
                largest_block, jnp.max(jnp.abs(tile).reshape(B // 16, 16, B), axis=0)
            )
        return largest, largest_block

    carry = jnp.zeros((8, K), f32), jnp.zeros((16, B), jnp.bfloat16)
    largest, largest_block = run_slots(
        Y_PARTS, count[0], targets, order, bounds, begin, group, carry, total_sum, outs, out_sems
    )
    stat[:4] = jnp.full((4, K), jnp.max(largest))
    stat[4:] = jnp.full((4, K), jnp.max(largest_block.astype(f32)))


Y_PARTS = (32, 16, 16)
Z_PARTS = (16, 16, 8, 8, 4, 4, 4, 4)


def sums_of(parts):
    return tuple(jax.ShapeDtypeStruct((n, B, K), f32) for n in parts)


def scratch_for(halves, parts, y_type):
    return [
        pltpu.VMEM((halves * 8 * CHUNK, B, K), f32),
        pltpu.SMEM((NBLK + 1,), jnp.int32),
        pltpu.SMEM((halves * 8 + 1,), jnp.int32),
        pltpu.VMEM((BUFFERS, B, B), jnp.bfloat16),
        pltpu.VMEM((BUFFERS, B, K), y_type),
        pltpu.SemaphoreType.DMA((2, BUFFERS)),
        pltpu.SemaphoreType.DMA((halves * 10,)),
    ]


def partial_rows(count, targets, cols, blocks, sketch):
    return pl.pallas_call(
        y_kernel,
        out_shape=sums_of(Y_PARTS) + (jax.ShapeDtypeStruct((8, K), f32),),
        in_specs=[pl.BlockSpec(memory_space=pltpu.SMEM)] * 3
        + [pl.BlockSpec(memory_space=pl.ANY)] * 2,
        out_specs=(pl.BlockSpec(memory_space=pl.ANY),) * 3
        + (pl.BlockSpec(memory_space=pltpu.VMEM),),
        scratch_shapes=scratch_for(1, Y_PARTS, jnp.bfloat16),
        compiler_params=pltpu.CompilerParams(vmem_limit_bytes=VMEM_BYTES),
        cost_estimate=pl.CostEstimate(
            flops=NBLK * B * B * K, bytes_accessed=60 * 1024 * 1024, transcendentals=0
        ),
        name="partial_rows",
    )(count, targets, cols, blocks, sketch)


def table_row(row):
    return pl.multiple_of((row >> 4) * SHARE_ROWS + (row & 15) * B, 16)


def share_kernel(gathered, gram, scales, buffer, sems):
    copies = [
        pltpu.make_async_copy(
            gathered.at[pl.ds(c * SHARE_ROWS + BR // 8 * B, 2 * K + 32)], buffer.at[c], sems.at[c]
        )
        for c in range(8)
    ]
    for copy in copies:
        copy.start()
    total = jnp.zeros((K, K), f32)
    for c, copy in enumerate(copies):
        copy.wait()
        scale = jnp.exp2(buffer[c, 2 * K : 2 * K + 32].astype(f32))
        scales[c * 16 : (c + 1) * 16] = scale[:16]
        high, low = buffer[c, :K].astype(f32), buffer[c, K : 2 * K].astype(f32)
        total += (high + low * (1.0 / LOW_SCALE)) * scale[16:17]
    gram[...] = total


def read_shares(gathered):
    return pl.pallas_call(
        share_kernel,
        out_shape=(jax.ShapeDtypeStruct((K, K), f32), jax.ShapeDtypeStruct((BR, K), f32)),
        in_specs=[pl.BlockSpec(memory_space=pl.ANY)],
        out_specs=(pl.BlockSpec(memory_space=pltpu.VMEM),) * 2,
        scratch_shapes=[
            pltpu.VMEM((8, 2 * K + 32, K), jnp.int16),
            pltpu.SemaphoreType.DMA((8,)),
        ],
        compiler_params=pltpu.CompilerParams(vmem_limit_bytes=VMEM_BYTES),
        name="read_shares",
    )(gathered)


def z_kernel(count, targets, rows, blocks, table, tile_scales, *rest):
    outs, scratch = rest[:16], rest[16:]
    total_sum, order, bounds, block_buf, y_buf, sems, out_sems = scratch

    def copies(j):
        s, at = order[j], lax.rem(j, BUFFERS)
        return (
            pltpu.make_async_copy(blocks.at[s], block_buf.at[at], sems.at[0, at]),
            pltpu.make_async_copy(
                table.at[pl.ds(table_row(rows[s]), B)], y_buf.at[at], sems.at[1, at]
            ),
        )

    def begin(j, _):
        for copy in copies(j):
            copy.start()
        return 0

    def group(begin_later, at, size, carry):
        for u in range(size):
            begin_later(at + u + AHEAD)
        for u in range(size):
            for copy in copies(at + u):
                copy.wait()
        for u in range(size):
            buffer = lax.rem(at + u, BUFFERS)
            value = y_buf[buffer].astype(f32)
            high = value.astype(jnp.bfloat16)
            low = (value - high.astype(f32)).astype(jnp.bfloat16)
            product = lax.dot_general(
                block_buf[buffer],
                jnp.concatenate([high, low], axis=1),
                (((0,), (0,)), ((), ())),
                preferred_element_type=f32,
            )
            slot = order[at + u]
            product = (product[:, :K] + product[:, K:]) * tile_scales[pl.ds(rows[slot], 1)]
            total_sum[targets[slot]] += product
        return carry

    run_slots(
        Z_PARTS, count[0], targets, order, bounds, begin, group, 0, total_sum, outs, out_sems
    )


def partial_cols(count, targets, rows, blocks, table, tile_scales):
    return pl.pallas_call(
        z_kernel,
        out_shape=sums_of(Z_PARTS * 2),
        in_specs=[pl.BlockSpec(memory_space=pltpu.SMEM)] * 3
        + [pl.BlockSpec(memory_space=pl.ANY)] * 2
        + [pl.BlockSpec(memory_space=pltpu.VMEM)],
        out_specs=(pl.BlockSpec(memory_space=pl.ANY),) * 16,
        scratch_shapes=scratch_for(2, Z_PARTS, jnp.int16),
        compiler_params=pltpu.CompilerParams(vmem_limit_bytes=VMEM_BYTES),
        cost_estimate=pl.CostEstimate(
            flops=NBLK * B * B * K * 4, bytes_accessed=42 * 1024 * 1024, transcendentals=0
        ),
        name="partial_cols",
    )(count, targets, rows, blocks, table, tile_scales)


def scales_for(bound):
    exponent = jnp.ceil(jnp.log2(jnp.maximum(bound, 1e-30))) - 15.0
    scale, inverse = lax.optimization_barrier((jnp.exp2(exponent), jnp.exp2(-exponent)))
    return scale[0, 0], inverse[0, 0]


def by_rows(value):
    return with_layout_constraint(value, Layout(tuple(range(value.ndim))))


def pack(value, scales):
    return by_rows((value * scales[1]).astype(f16))


def unpack(message, scales):
    return message.astype(f32) * scales[0]


PLACES = (6, 7, 4, 1, 0, 2, 3, 5)


HALF = CHUNK * B


def ring_first(messages, send):
    return lax.optimization_barrier((send(messages[0], 1), send(messages[1], -1)))


def ring_second(received, passing, send, scales, below, above):
    messages = lax.optimization_barrier(
        (
            pack(passing[0] + unpack(received[0][:HALF], below), scales),
            pack(passing[1] + unpack(received[1][:HALF], above), scales),
        )
    )
    sums = send(messages[0], 1), send(messages[1], -1)
    return lax.optimization_barrier((received, sums, messages))


def ring_total(received, sums, staying, scales, below, above):
    def total(which, start=0, stop=HALF):
        direct = received[1 - which][HALF + start : HALF + stop]
        return (
            staying[which][start // (stop - start)]
            + unpack(direct, below if which else above)
            + unpack(sums[which][start:stop], scales)
        )

    return total


def ring_exchange(parts, send, scales):
    messages = [pack(parts[r], scales) for r in (1, 3, 2)]
    up, down, across = (unpack(send(m, r), scales) for m, r in zip(messages, (1, 3, 2)))
    return parts[0] + up + down + across, messages


def exponent_of(largest):
    return jnp.floor(jnp.log2(jnp.maximum(largest, 1e-30))) - 14.0


def whole(value):
    return jnp.clip(jnp.round(value), -32767.0, 32767.0)


def after(value, other):
    return value + (0.0 * other[(0,) * other.ndim]).astype(value.dtype)


def ring_fold(value, send, op):
    across, below, above = send(value, 2), send(value, 1), send(value, -1)
    return op(op(value, across), op(below, above)), below, above


def body(blocks, sketch, block_row, block_col, counts):
    highest = lax.Precision.HIGHEST
    blocks = blocks[0, 0]
    rows, cols = block_row[0, 0], block_col[0, 0]
    count = counts[0, 0]
    row_at, col_at = lax.axis_index("row"), lax.axis_index("col")
    here_x, here_z = row_at // 4, row_at % 4
    here_y, core = col_at // 2, col_at % 2
    sketch_table = sketch.reshape(BC, B, K)

    def send_core(value):
        return lax.ppermute(value, "col", PAIR)

    def send_y(value, shift):
        return lax.ppermute(value, "col", ring(shift))

    def send_x(value, shift):
        return lax.ppermute(value, "row", along_x(shift))

    def send_z(value, shift):
        return lax.ppermute(value, "row", along_z(shift))

    live = jnp.arange(NBLK, dtype=jnp.int32) < count

    def chunk_of(rel, half):
        key = (rel & 3) * 2 + half
        chunk = PLACES[7]
        for k in range(7):
            chunk = jnp.where(key == k, PLACES[k], chunk)
        return chunk * CHUNK

    y_target = chunk_of((rows >> 5) - here_y, (rows >> 3) & 1) + (rows & 7)
    row_core = (rows >> 4) & 1
    rel_x, rel_z = ((cols >> 5) - here_x) & 3, ((cols >> 3) - here_z) & 3
    is_a = ((cols >> 2) & 1) == 0
    one, two = jnp.where(is_a, rel_x, rel_z), jnp.where(is_a, rel_z, rel_x)
    z_target = chunk_of(one, two >> 1) + (two & 1) * 4 + (cols & 3) + jnp.where(is_a, 0, 8 * CHUNK)
    other_target = jnp.where(live & (row_core != core), y_target, -1)
    own_target = jnp.where(live & (row_core == core), y_target, -1)
    z_target = jnp.where(live, z_target, -1)
    count = count[None]

    def flat(values):
        return [v.reshape(-1, K) for v in values]

    *other, other_stat = partial_rows(count, other_target, cols, blocks, sketch_table)
    *from_pair, pair_stat = [send_core(v) for v in (*other, other_stat)]
    *own, own_stat = partial_rows(count, own_target, cols, blocks, sketch_table)
    own, from_pair = flat(own), flat(from_pair)

    first_bound = own_stat + pair_stat
    scales = scales_for(first_bound[:1])
    own_first, pair_first = (v.reshape(2, 2 * HALF, K) for v in (own[0], from_pair[0]))
    first = [pack(own_first[i] + pair_first[i], scales) for i in range(2)]
    received = [send_y(first[0], 1), send_y(first[1], -1)]

    in_first = lax.broadcasted_iota(jnp.int32, (8, K), 0) < 4
    entries = jnp.maximum(own_stat, other_stat) * count[0].astype(f32)
    bounds, _ = lax.optimization_barrier((jnp.where(in_first, first_bound, entries), first))
    bounds, below, above = ring_fold(bounds, send_y, jnp.maximum)
    later, _ = lax.optimization_barrier(((own[1:], from_pair[1:]), bounds))
    parts = [
        [mine[at : at + HALF] + pair[at : at + HALF] for at in (0, HALF)] for mine, pair in zip(*later)
    ]
    passing, staying = lax.optimization_barrier(parts)
    around = scales_for(below[:1]), scales_for(above[:1])
    sum_scales = scales_for(bounds[:1] * 4.0)
    received, sums, messages = ring_second(received, passing, send_y, sum_scales, *around)
    y_part = ring_total(received, sums, [[v] for v in staying], sum_scales, *around)
    y_share = jnp.concatenate([y_part(0), y_part(1)], axis=0)

    bounds, _ = lax.optimization_barrier((bounds, messages))
    bounds = jnp.maximum(bounds, send_core(bounds))
    y_scales = scales_for(bounds[:1] * 4.0)
    bounds = ring_fold(ring_fold(bounds, send_x, jnp.maximum)[0], send_z, jnp.maximum)[0]
    z_scales = scales_for(bounds[:1] * bounds[4:5] * (4.0 * 16.0 * B))

    gram = jnp.dot(
        y_share.T, y_share, precision=lax.Precision.HIGH, preferred_element_type=f32
    )
    tiles = y_share.reshape(BR // 8, B, K)
    exponents = exponent_of(jnp.max(jnp.abs(tiles), axis=(1, 2)))
    gram_exponent = exponent_of(jnp.max(jnp.abs(gram)))
    codes = whole(tiles * jnp.exp2(-exponents)[:, None, None]).reshape(-1, K)
    gram = gram * jnp.exp2(-gram_exponent)
    high = whole(gram)
    low = whole((gram - high) * LOW_SCALE)
    scale_rows = jnp.concatenate([exponents, jnp.full((16,), gram_exponent)])
    scale_rows = jnp.broadcast_to(scale_rows[:, None], (32, K)).astype(jnp.int16)
    scale_rows = by_rows(lax.optimization_barrier(scale_rows))
    mine = [v.astype(jnp.int16) for v in (codes, high, low)]
    mine = jnp.concatenate([*mine, scale_rows], axis=0)
    mine, z_scales = lax.optimization_barrier((by_rows(mine), z_scales))
    gathered = lax.all_gather(mine, "col", axis=0, tiled=True)
    gram, tile_scales = read_shares(gathered)
    gram = ring_fold(gram, send_x, jnp.add)[0]
    partial = flat(partial_cols(count, z_target, rows, blocks, gathered, tile_scales))
    gram = ring_fold(gram, send_z, jnp.add)[0]

    rings = [(partial[:8], send_x, send_z), (partial[8:], send_z, send_x)]
    around = z_scales, z_scales
    scales_each = [z_scales, (z_scales[0], after(z_scales[1], gram))]
    messages = [
        [pack(v, scales) for v in values[:2]] for (values, _, _), scales in zip(rings, scales_each)
    ]
    received = [[send(m[0], 1), send(m[1], -1)] for m, (_, send, _) in zip(messages, rings)]
    lower_factor = jnp.linalg.cholesky(gram)
    seconds = [
        ring_second(r, values[2:4], send, z_scales, *around)
        for r, (values, send, _) in zip(received, rings)
    ]
    thirds = []
    for (direct, sums, _), (values, _, send) in zip(seconds, rings):
        total = ring_total(direct, sums, [values[4:6], values[6:]], z_scales, *around)
        quarters = [total(r // 2, r % 2 * 4 * B, (r % 2 + 1) * 4 * B) for r in range(4)]
        thirds.append(ring_exchange(quarters, send, z_scales))
    inverse = lax.linalg.triangular_solve(
        lower_factor, jnp.eye(K, dtype=f32), left_side=True, lower=True
    )
    basis_factor = after(inverse, seconds[1][2][1])
    q_share = jnp.dot(y_share, basis_factor.T, precision=highest, preferred_element_type=f32)
    z_raw = jnp.concatenate([z for z, _ in thirds], axis=0)
    z_share = jnp.dot(z_raw, inverse.T, precision=highest, preferred_element_type=f32)
    row_scale = math.sqrt(BR * B * lax.axis_size("row"))
    return (q_share * row_scale, z_share[None])


def solution(mesh):
    in_specs = (
        P("row", "col", None, None, None),
        P("col", None),
        P("row", "col", None),
        P("row", "col", None),
        P("row", "col"),
    )
    out_specs = (P(("row", "col"), None), P("col", "row", None))
    return jax.shard_map(body, mesh=mesh, in_specs=in_specs, out_specs=out_specs, check_vma=False)
```

profile of v0, /device:TPU:24, one launch (start us, length us, event | category | flops | bytes accessed | tf_op | source)
XLA Modules:
  0.0 247.8 jit_solution(12813557431420187876)
XLA Ops:
  3.7 12.2 %partial_rows.3 = (f32[32,256,128]{2,1,0:T(8,128)}, f32[16,256,128]{2,1,0:T(8,128)}, f32[16,256,128]{2,1,0:T(8,128)}, f32[8,128]{1,0:T(8,128)}) custom-call(s32[1]{0:T(128)} %bitcast.146.count, s32[96]{0:T(128)} %and_select_fusion.targets, s32[96]{0:T(128)} %bitcast.184, bf16[96,256,256]{2,1,0:T(8,128)(2,1)} %bitcast.152, bf16[128,256,128]{2,1,0:T(8,128)(2,1)} %bitcast.155), custom_call_target="tpu_custom_call" | custom-call | flops 805306368 | bytes 62914560 | tf_op jit(solution)/shard_map/partial_rows/pallas_call | solution.py:204
  17.0 12.5 %partial_rows.2 = (f32[32,256,128]{2,1,0:T(8,128)}, f32[16,256,128]{2,1,0:T(8,128)}, f32[16,256,128]{2,1,0:T(8,128)}, f32[8,128]{1,0:T(8,128)}) custom-call(s32[1]{0:T(128)} %bitcast.145.count, s32[96]{0:T(128)} %get-tuple-element.130.targets, s32[96]{0:T(128)} %bitcast.185, bf16[96,256,256]{2,1,0:T(8,128)(2,1)} %bitcast.153, bf16[128,256,128]{2,1,0:T(8,128)(2,1)} %bitcast.156), custom_call_target="tpu_custom_call" | custom-call | flops 805306368 | bytes 62914560 | tf_op jit(solution)/shard_map/partial_rows/pallas_call | solution.py:204
  30.4 4.5 %fusion.1 = (f16[16,256,128]{2,1,0:T(8,128)(2,1)S(1)}, f16[16,256,128]{2,1,0:T(8,128)(2,1)S(1)}) fusion(f32[32,256,128]{2,1,0:T(8,128)} %collective-permute-done.3, f32[32,256,128]{2,1,0:T(8,128)} %get-tuple-element.69, f32[]{:T(128)S(1)} %bitcast.195), kind=kLoop, calls=%fused_computation.4 | loop fusion | flops 3145728 | bytes 10485764 | tf_op jit(solution)/shard_map/convert_element_type | solution.py:331
  34.8 2.4 collective-permute-start.4
  40.9 2.4 collective-permute-start.7
  43.4 2.2 slice_add_fusion.2
  47.9 2.6 %collective-permute-start.14 = (f32[8,128]{1,0:T(8,128)S(1)}, f32[8,128]{1,0:T(8,128)S(1)}, u32[]{:S(2)}, u32[]{:S(2)}) collective-permute-start(f32[8,128]{1,0:T(8,128)S(1)} %max.84), channel_id=1, source_target_pairs={{0,96},{8,104},{16,112},{24,120},{32,0},{40,8},{48,16},{56,24},{64... | collective-permute-start | bytes 12296 | tf_op jit(solution)/shard_map/ppermute | solution.py:411
  52.1 5.7 %collective-permute-start.15 = (f32[8,128]{1,0:T(8,128)S(1)}, f32[8,128]{1,0:T(8,128)S(1)}, u32[]{:S(2)}, u32[]{:S(2)}) collective-permute-start(f32[8,128]{1,0:T(8,128)S(1)} %maximum_maximum_fusion.1), channel_id=1, source_target_pairs={{0,16},{8,24},{16,0},{24,8},{32,48},{40,56},{48,32},{56,40},{64,80... | collective-permute-start | bytes 12296 | tf_op jit(solution)/shard_map/ppermute | solution.py:414
  57.8 3.2 %collective-permute-start.17 = (f32[8,128]{1,0:T(8,128)S(1)}, f32[8,128]{1,0:T(8,128)S(1)}, u32[]{:S(2)}, u32[]{:S(2)}) collective-permute-start(f32[8,128]{1,0:T(8,128)S(1)} %maximum_maximum_fusion.1), channel_id=1, source_target_pairs={{0,24},{8,0},{16,8},{24,16},{32,56},{40,32},{48,40},{56,48},{64,88... | collective-permute-start | bytes 12296 | tf_op jit(solution)/shard_map/ppermute | solution.py:414
  61.1 4.2 %collective-permute-done.8 = f16[4096,128]{1,0:T(8,128)(2,1)S(1)} collective-permute-done((f16[4096,128]{1,0:T(8,128)(2,1)S(1)}, f16[4096,128]{1,0:T(8,128)(2,1)S(1)}, u32[]{:S(2)}, u32[]{:S(2)}) %collective-permute-start.8) | collective-permute-done | bytes 1048608 | tf_op jit(solution)/shard_map/ppermute | solution.py:408
  66.2 2.9 %collective-permute-start.9 = (f16[2048,128]{1,0:T(8,128)(2,1)S(1)}, f16[2048,128]{1,0:T(8,128)(2,1)S(1)}, u32[]{:S(2)}, u32[]{:S(2)}) collective-permute-start(f16[2048,128]{1,0:T(8,128)(2,1)S(1)} %multiply_convert_fusion.5), channel_id=1, source_target_pairs={{0,2},{1,3},{2,4},{3,5},{4,6},{5,7},{6,0},{7,1},{8,10},{9,11},{10,... | collective-permute-start | bytes 1572872 | tf_op jit(solution)/shard_map/ppermute | solution.py:408
  69.1 9.7 %collective-permute-done.10 = f16[2048,128]{1,0:T(8,128)(2,1)S(1)} collective-permute-done((f16[2048,128]{1,0:T(8,128)(2,1)S(1)}, f16[2048,128]{1,0:T(8,128)(2,1)S(1)}, u32[]{:S(2)}, u32[]{:S(2)}) %collective-permute-start.10) | collective-permute-done | bytes 524320 | tf_op jit(solution)/shard_map/ppermute | solution.py:408
  79.9 2.4 abs_reduce_fusion.1
  84.9 42.7 %all-gather.1.gathered.table = s16[35072,128]{1,0:T(8,128)(2,1)} all-gather(s16[4384,128]{1,0:T(8,128)(2,1)S(1)} %pad_add_fusion), channel_id=1, replica_groups=mesh['row'=16,'col'=8] {'col'}, dimensions={0}, use_global_device_ids=true | all-gather | bytes 10100736 | tf_op jit(solution)/shard_map/all_gather | solution.py:487
  131.5 3.2 %collective-permute-start.20 = (f32[128,128]{0,1:T(8,128)S(1)}, f32[128,128]{0,1:T(8,128)S(1)}, u32[]{:S(2)}, u32[]{:S(2)}) collective-permute-start(f32[128,128]{0,1:T(8,128)S(1)} %copy.13), channel_id=1, source_target_pairs={{0,96},{8,104},{16,112},{24,120},{32,0},{40,8},{48,16},{56,24},{64... | collective-permute-start | bytes 196616 | tf_op jit(solution)/shard_map/ppermute | solution.py:411
  134.8 16.8 %partial_cols.1 = (f32[16,256,128]{2,1,0:T(8,128)}, f32[16,256,128]{2,1,0:T(8,128)}, f32[8,256,128]{2,1,0:T(8,128)}, f32[8,256,128]{2,1,0:T(8,128)}, f32[4,256,1...) custom-call(s32[1]{0:T(128)} %bitcast.147.count, ...), custom_call_target="tpu_custom_call" | custom-call | flops 3221225472 | bytes 44040192 | tf_op jit(solution)/shard_map/partial_cols/pallas_call | solution.py:304
  151.6 3.0 %multiply_convert_fusion = f16[16,256,128]{2,1,0:T(8,128)(2,1)} fusion(f32[16,256,128]{2,1,0:T(8,128)} %get-tuple-element.104, f32[]{:T(128)S(1)} %bitcast.163), kind=kLoop, calls=%fused_computation.9 | loop fusion | flops 1048576 | bytes 3145732 | tf_op jit(solution)/shard_map/convert_element_type | solution.py:331
  154.7 9.1 %collective-permute-start.21 = (f32[128,128]{0,1:T(8,128)S(1)}, f32[128,128]{0,1:T(8,128)S(1)}, u32[]{:S(2)}, u32[]{:S(2)}) collective-permute-start(f32[128,128]{0,1:T(8,128)S(1)} %add_add_fusion.1), channel_id=1, source_target_pairs={{0,16},{8,24},{16,0},{24,8},{32,48},{40,56},{48,32},{56,40},{64,80... | collective-permute-start | bytes 196616 | tf_op jit(solution)/shard_map/ppermute | solution.py:414
  163.7 3.2 %collective-permute-start.23 = (f32[128,128]{0,1:T(8,128)S(1)}, f32[128,128]{0,1:T(8,128)S(1)}, u32[]{:S(2)}, u32[]{:S(2)}) collective-permute-start(f32[128,128]{0,1:T(8,128)S(1)} %add_add_fusion.1), channel_id=1, source_target_pairs={{0,24},{8,0},{16,8},{24,16},{32,56},{40,32},{48,40},{56,48},{64,88... | collective-permute-start | bytes 196616 | tf_op jit(solution)/shard_map/ppermute | solution.py:414
  170.5 3.0 %multiply_convert_fusion.2 = f16[16,256,128]{2,1,0:T(8,128)(2,1)} fusion(f32[16,256,128]{2,1,0:T(8,128)} %get-tuple-element.95, f32[]{:T(128)S(6)} %add.225), kind=kLoop, calls=%fused_computation.11 | loop fusion | flops 1048576 | bytes 3145732 | tf_op jit(solution)/shard_map/convert_element_type | solution.py:331
  173.5 3.2 %collective-permute-start.25 = (f16[4096,128]{1,0:T(8,128)(2,1)}, f16[4096,128]{1,0:T(8,128)(2,1)}, u32[]{:S(2)}, u32[]{:S(2)}) collective-permute-start(f16[4096,128]{1,0:T(8,128)(2,1)} %bitcast.24), channel_id=1, source_target_pairs={{0,24},{8,0},{16,8},{24,16},{32,56},{40,32},{48,40},{56,48},{64,88... | collective-permute-start | bytes 3145736 | tf_op jit(solution)/shard_map/ppermute | solution.py:414
  178.1 11.7 %cholesky.17 = f32[128,128]{1,0:T(8,128)S(1)} custom-call(f32[128,128]{1,0:T(8,128)S(1)} %fusion.45), custom_call_target="Cholesky" | custom-call | tf_op jit(solution)/shard_map/jit(cholesky)/cholesky | solution.py:500
  191.2 9.8 %custom-call.6 = f32[1,128,128]{1,2,0:T(8,128)S(1)} custom-call(f32[1,128,128]{2,1,0:T(8,128)S(1)} %fusion.42), custom_call_target="InvertDiagBlocksLowerTriangular" | custom-call | tf_op jit(solution)/shard_map/triangular_solve | solution.py:510
  203.3 3.2 %collective-permute-start.31 = (f16[2048,128]{1,0:T(8,128)(2,1)S(1)}, f16[2048,128]{1,0:T(8,128)(2,1)S(1)}, u32[]{:S(2)}, u32[]{:S(2)}) collective-permute-start(f16[2048,128]{1,0:T(8,128)(2,1)S(1)} %fusion.8), channel_id=1, source_target_pairs={{0,96},{8,104},{16,112},{24,120},{32,0},{40,8},{48,16},{56,24},{64... | collective-permute-start | bytes 1572872 | tf_op jit(solution)/shard_map/ppermute | solution.py:411
  209.6 3.3 %collective-permute-start.27 = (f16[2048,128]{1,0:T(8,128)(2,1)S(1)}, f16[2048,128]{1,0:T(8,128)(2,1)S(1)}, u32[]{:S(2)}, u32[]{:S(2)}) collective-permute-start(f16[2048,128]{1,0:T(8,128)(2,1)S(1)} %fusion.12), channel_id=1, source_target_pairs={{0,24},{8,0},{16,8},{24,16},{32,56},{40,32},{48,40},{56,48},{64,88... | collective-permute-start | bytes 1572872 | tf_op jit(solution)/shard_map/ppermute | solution.py:414
  212.9 3.3 %collective-permute-done.30 = f16[2048,128]{1,0:T(8,128)(2,1)S(1)} collective-permute-done((f16[2048,128]{1,0:T(8,128)(2,1)S(1)}, f16[2048,128]{1,0:T(8,128)(2,1)S(1)}, u32[]{:S(2)}, u32[]{:S(2)}) %collective-permute-start.30) | collective-permute-done | bytes 524320 | tf_op jit(solution)/shard_map/ppermute | solution.py:411
  216.2 2.0 fusion.37
  219.4 3.2 %collective-permute-start.33 = (f16[1024,128]{1,0:T(8,128)(2,1)}, f16[1024,128]{1,0:T(8,128)(2,1)}, u32[]{:S(2)}, u32[]{:S(2)}) collective-permute-start(f16[1024,128]{1,0:T(8,128)(2,1)} %get-tuple-element.138), channel_id=1, source_target_pairs={{0,24},{8,0},{16,8},{24,16},{32,56},{40,32},{48,40},{56,48},{64,88... | collective-permute-start | bytes 786440 | tf_op jit(solution)/shard_map/ppermute | solution.py:414
  226.7 2.2 fusion.21
  228.9 3.2 %collective-permute-start.36 = (f16[1024,128]{1,0:T(8,128)(2,1)}, f16[1024,128]{1,0:T(8,128)(2,1)}, u32[]{:S(2)}, u32[]{:S(2)}) collective-permute-start(f16[1024,128]{1,0:T(8,128)(2,1)} %get-tuple-element.140), channel_id=1, source_target_pairs={{0,96},{8,104},{16,112},{24,120},{32,0},{40,8},{48,16},{56,24},{64... | collective-permute-start | bytes 786440 | tf_op jit(solution)/shard_map/ppermute | solution.py:411
  233.3 3.1 %convolution_multiply_fusion = f32[4096,128]{1,0:T(8,128)} fusion(f32[2048,128]{1,0:T(8,128)S(1)} %multiply_add_fusion, f32[2048,128]{1,0:T(8,128)S(1)} %multiply_add_fusion.1, f32[128,128]{1,0:T(8,128)S(1)} %fusion.43, f32[]{:T(128)S(6)} %convert.9), kind=kOutput, calls=%fused_computation | convolution fusion | flops 806371328 | bytes 4259844 | tf_op jit(solution)/shard_map/dot_general | solution.py:514
  239.0 5.4 %collective-permute-done.37 = f16[1024,128]{1,0:T(8,128)(2,1)S(1)} collective-permute-done((f16[1024,128]{1,0:T(8,128)(2,1)S(1)}, f16[1024,128]{1,0:T(8,128)(2,1)S(1)}, u32[]{:S(2)}, u32[]{:S(2)}) %collective-permute-start.37) | collective-permute-done | bytes 262176 | tf_op jit(solution)/shard_map/ppermute | solution.py:411
  (156 shorter events, 42.2 us)
Async XLA Ops:
  15.9 14.4 %collective-permute-start.3 = (f32[32,256,128]{2,1,0:T(8,128)}, f32[32,256,128]{2,1,0:T(8,128)}, u32[]{:S(2)}, u32[]{:S(2)}) collective-permute-start(f32[32,256,128]{2,1,0:T(8,128)} %get-tuple-element.70), channel_id=1, source_target_pairs={{0,1},{1,0},{2,3},{3,2},{4,5},{5,4},{6,7},{7,6},{8,9},{9,8},{10,11... | collective-permute-start | bytes 12582920 | tf_op jit(solution)/shard_map/ppermute | solution.py:405
  16.0 27.4 %collective-permute-start = (f32[16,256,128]{2,1,0:T(8,128)}, f32[16,256,128]{2,1,0:T(8,128)S(1)}, u32[]{:S(2)}, u32[]{:S(2)}) collective-permute-start(f32[16,256,128]{2,1,0:T(8,128)} %get-tuple-element.65), channel_id=1, source_target_pairs={{0,1},{1,0},{2,3},{3,2},{4,5},{5,4},{6,7},{7,6},{8,9},{9,8},{10,11... | collective-permute-start | bytes 6291464 | tf_op jit(solution)/shard_map/ppermute | solution.py:405
  16.5 26.9 %collective-permute-start.1 = (f32[16,256,128]{2,1,0:T(8,128)}, f32[16,256,128]{2,1,0:T(8,128)}, u32[]{:S(2)}, u32[]{:S(2)}) collective-permute-start(f32[16,256,128]{2,1,0:T(8,128)} %get-tuple-element.66), channel_id=1, source_target_pairs={{0,1},{1,0},{2,3},{3,2},{4,5},{5,4},{6,7},{7,6},{8,9},{9,8},{10,11... | collective-permute-start | bytes 6291464 | tf_op jit(solution)/shard_map/ppermute | solution.py:405
  16.6 13.0 %collective-permute-start.2 = (f32[8,128]{1,0:T(8,128)}, f32[8,128]{1,0:T(8,128)S(1)}, u32[]{:S(2)}, u32[]{:S(2)}) collective-permute-start(f32[8,128]{1,0:T(8,128)} %get-tuple-element.68), channel_id=1, source_target_pairs={{0,1},{1,0},{2,3},{3,2},{4,5},{5,4},{6,7},{7,6},{8,9},{9,8},{10,11... | collective-permute-start | bytes 12296 | tf_op jit(solution)/shard_map/ppermute | solution.py:405
  40.0 25.2 %collective-permute-start.8 = (f16[4096,128]{1,0:T(8,128)(2,1)S(1)}, f16[4096,128]{1,0:T(8,128)(2,1)S(1)}, u32[]{:S(2)}, u32[]{:S(2)}) collective-permute-start(f16[4096,128]{1,0:T(8,128)(2,1)S(1)} %bitcast.161), channel_id=1, source_target_pairs={{0,6},{1,7},{2,0},{3,1},{4,2},{5,3},{6,4},{7,5},{8,14},{9,15},{10,... | collective-permute-start | bytes 3145736 | tf_op jit(solution)/shard_map/ppermute | solution.py:408
  40.9 24.6 %collective-permute-start.7 = (f16[4096,128]{1,0:T(8,128)(2,1)S(1)}, f16[4096,128]{1,0:T(8,128)(2,1)S(1)}, u32[]{:S(2)}, u32[]{:S(2)}) collective-permute-start(f16[4096,128]{1,0:T(8,128)(2,1)S(1)} %bitcast.160), channel_id=1, source_target_pairs={{0,2},{1,3},{2,4},{3,5},{4,6},{5,7},{6,0},{7,1},{8,10},{9,11},{10,... | collective-permute-start | bytes 3145736 | tf_op jit(solution)/shard_map/ppermute | solution.py:408
  46.1 6.0 %collective-permute-start.13 = (f32[8,128]{1,0:T(8,128)S(1)}, f32[8,128]{1,0:T(8,128)S(1)}, u32[]{:S(2)}, u32[]{:S(2)}) collective-permute-start(f32[8,128]{1,0:T(8,128)S(1)} %max.84), channel_id=1, source_target_pairs={{0,32},{8,40},{16,48},{24,56},{32,64},{40,72},{48,80},{56,88},{64,... | collective-permute-start | bytes 12296 | tf_op jit(solution)/shard_map/ppermute | solution.py:411
  52.1 16.9 %collective-permute-start.15 = (f32[8,128]{1,0:T(8,128)S(1)}, f32[8,128]{1,0:T(8,128)S(1)}, u32[]{:S(2)}, u32[]{:S(2)}) collective-permute-start(f32[8,128]{1,0:T(8,128)S(1)} %maximum_maximum_fusion.1), channel_id=1, source_target_pairs={{0,16},{8,24},{16,0},{24,8},{32,48},{40,56},{48,32},{56,40},{64,80... | collective-permute-start | bytes 12296 | tf_op jit(solution)/shard_map/ppermute | solution.py:414
  57.8 11.2 %collective-permute-start.16 = (f32[8,128]{1,0:T(8,128)S(1)}, f32[8,128]{1,0:T(8,128)S(1)}, u32[]{:S(2)}, u32[]{:S(2)}) collective-permute-start(f32[8,128]{1,0:T(8,128)S(1)} %maximum_maximum_fusion.1), channel_id=1, source_target_pairs={{0,8},{8,16},{16,24},{24,0},{32,40},{40,48},{48,56},{56,32},{64,72... | collective-permute-start | bytes 12296 | tf_op jit(solution)/shard_map/ppermute | solution.py:414
  57.8 11.2 %collective-permute-start.17 = (f32[8,128]{1,0:T(8,128)S(1)}, f32[8,128]{1,0:T(8,128)S(1)}, u32[]{:S(2)}, u32[]{:S(2)}) collective-permute-start(f32[8,128]{1,0:T(8,128)S(1)} %maximum_maximum_fusion.1), channel_id=1, source_target_pairs={{0,24},{8,0},{16,8},{24,16},{32,56},{40,32},{48,40},{56,48},{64,88... | collective-permute-start | bytes 12296 | tf_op jit(solution)/shard_map/ppermute | solution.py:414
  65.7 13.1 %collective-permute-start.10 = (f16[2048,128]{1,0:T(8,128)(2,1)S(1)}, f16[2048,128]{1,0:T(8,128)(2,1)S(1)}, u32[]{:S(2)}, u32[]{:S(2)}) collective-permute-start(f16[2048,128]{1,0:T(8,128)(2,1)S(1)} %multiply_convert_fusion.4), channel_id=1, source_target_pairs={{0,6},{1,7},{2,0},{3,1},{4,2},{5,3},{6,4},{7,5},{8,14},{9,15},{10,... | collective-permute-start | bytes 1572872 | tf_op jit(solution)/shard_map/ppermute | solution.py:408
  66.2 12.7 %collective-permute-start.9 = (f16[2048,128]{1,0:T(8,128)(2,1)S(1)}, f16[2048,128]{1,0:T(8,128)(2,1)S(1)}, u32[]{:S(2)}, u32[]{:S(2)}) collective-permute-start(f16[2048,128]{1,0:T(8,128)(2,1)S(1)} %multiply_convert_fusion.5), channel_id=1, source_target_pairs={{0,2},{1,3},{2,4},{3,5},{4,6},{5,7},{6,0},{7,1},{8,10},{9,11},{10,... | collective-permute-start | bytes 1572872 | tf_op jit(solution)/shard_map/ppermute | solution.py:408
  130.4 24.2 %collective-permute-start.18 = (f32[128,128]{0,1:T(8,128)S(1)}, f32[128,128]{0,1:T(8,128)S(1)}, u32[]{:S(2)}, u32[]{:S(2)}) collective-permute-start(f32[128,128]{0,1:T(8,128)S(1)} %copy.13), channel_id=1, source_target_pairs={{0,64},{8,72},{16,80},{24,88},{32,96},{40,104},{48,112},{56,120},{... | collective-permute-start | bytes 196616 | tf_op jit(solution)/shard_map/ppermute | solution.py:411
  131.5 23.1 %collective-permute-start.19 = (f32[128,128]{0,1:T(8,128)S(1)}, f32[128,128]{0,1:T(8,128)S(1)}, u32[]{:S(2)}, u32[]{:S(2)}) collective-permute-start(f32[128,128]{0,1:T(8,128)S(1)} %copy.13), channel_id=1, source_target_pairs={{0,32},{8,40},{16,48},{24,56},{32,64},{40,72},{48,80},{56,88},{64,... | collective-permute-start | bytes 196616 | tf_op jit(solution)/shard_map/ppermute | solution.py:411
  131.5 23.1 %collective-permute-start.20 = (f32[128,128]{0,1:T(8,128)S(1)}, f32[128,128]{0,1:T(8,128)S(1)}, u32[]{:S(2)}, u32[]{:S(2)}) collective-permute-start(f32[128,128]{0,1:T(8,128)S(1)} %copy.13), channel_id=1, source_target_pairs={{0,96},{8,104},{16,112},{24,120},{32,0},{40,8},{48,16},{56,24},{64... | collective-permute-start | bytes 196616 | tf_op jit(solution)/shard_map/ppermute | solution.py:411
  154.6 46.6 %collective-permute-start.29 = (f16[4096,128]{1,0:T(8,128)(2,1)}, f16[4096,128]{1,0:T(8,128)(2,1)}, u32[]{:S(2)}, u32[]{:S(2)}) collective-permute-start(f16[4096,128]{1,0:T(8,128)(2,1)} %bitcast.30), channel_id=1, source_target_pairs={{0,96},{8,104},{16,112},{24,120},{32,0},{40,8},{48,16},{56,24},{64... | collective-permute-start | bytes 3145736 | tf_op jit(solution)/shard_map/ppermute | solution.py:411
  154.7 13.6 %collective-permute-start.21 = (f32[128,128]{0,1:T(8,128)S(1)}, f32[128,128]{0,1:T(8,128)S(1)}, u32[]{:S(2)}, u32[]{:S(2)}) collective-permute-start(f32[128,128]{0,1:T(8,128)S(1)} %add_add_fusion.1), channel_id=1, source_target_pairs={{0,16},{8,24},{16,0},{24,8},{32,48},{40,56},{48,32},{56,40},{64,80... | collective-permute-start | bytes 196616 | tf_op jit(solution)/shard_map/ppermute | solution.py:414
  163.7 5.5 %collective-permute-start.22 = (f32[128,128]{0,1:T(8,128)S(1)}, f32[128,128]{0,1:T(8,128)S(1)}, u32[]{:S(2)}, u32[]{:S(2)}) collective-permute-start(f32[128,128]{0,1:T(8,128)S(1)} %add_add_fusion.1), channel_id=1, source_target_pairs={{0,8},{8,16},{16,24},{24,0},{32,40},{40,48},{48,56},{56,32},{64,72... | collective-permute-start | bytes 196616 | tf_op jit(solution)/shard_map/ppermute | solution.py:414
  163.7 5.5 %collective-permute-start.23 = (f32[128,128]{0,1:T(8,128)S(1)}, f32[128,128]{0,1:T(8,128)S(1)}, u32[]{:S(2)}, u32[]{:S(2)}) collective-permute-start(f32[128,128]{0,1:T(8,128)S(1)} %add_add_fusion.1), channel_id=1, source_target_pairs={{0,24},{8,0},{16,8},{24,16},{32,56},{40,32},{48,40},{56,48},{64,88... | collective-permute-start | bytes 196616 | tf_op jit(solution)/shard_map/ppermute | solution.py:414
  168.3 34.7 %collective-permute-start.28 = (f16[4096,128]{1,0:T(8,128)(2,1)}, f16[4096,128]{1,0:T(8,128)(2,1)S(1)}, u32[]{:S(2)}, u32[]{:S(2)}) collective-permute-start(f16[4096,128]{1,0:T(8,128)(2,1)} %bitcast.29), channel_id=1, source_target_pairs={{0,32},{8,40},{16,48},{24,56},{32,64},{40,72},{48,80},{56,88},{64,... | collective-permute-start | bytes 3145736 | tf_op jit(solution)/shard_map/ppermute | solution.py:411
  173.5 33.0 %collective-permute-start.25 = (f16[4096,128]{1,0:T(8,128)(2,1)}, f16[4096,128]{1,0:T(8,128)(2,1)}, u32[]{:S(2)}, u32[]{:S(2)}) collective-permute-start(f16[4096,128]{1,0:T(8,128)(2,1)} %bitcast.24), channel_id=1, source_target_pairs={{0,24},{8,0},{16,8},{24,16},{32,56},{40,32},{48,40},{56,48},{64,88... | collective-permute-start | bytes 3145736 | tf_op jit(solution)/shard_map/ppermute | solution.py:414
  178.0 30.0 %collective-permute-start.24 = (f16[4096,128]{1,0:T(8,128)(2,1)}, f16[4096,128]{1,0:T(8,128)(2,1)}, u32[]{:S(2)}, u32[]{:S(2)}) collective-permute-start(f16[4096,128]{1,0:T(8,128)(2,1)} %bitcast.23), channel_id=1, source_target_pairs={{0,8},{8,16},{16,24},{24,0},{32,40},{40,48},{48,56},{56,32},{64,72... | collective-permute-start | bytes 3145736 | tf_op jit(solution)/shard_map/ppermute | solution.py:414
  203.2 12.9 %collective-permute-start.30 = (f16[2048,128]{1,0:T(8,128)(2,1)S(1)}, f16[2048,128]{1,0:T(8,128)(2,1)S(1)}, u32[]{:S(2)}, u32[]{:S(2)}) collective-permute-start(f16[2048,128]{1,0:T(8,128)(2,1)S(1)} %fusion.10), channel_id=1, source_target_pairs={{0,32},{8,40},{16,48},{24,56},{32,64},{40,72},{48,80},{56,88},{64,... | collective-permute-start | bytes 1572872 | tf_op jit(solution)/shard_map/ppermute | solution.py:411
  203.3 12.9 %collective-permute-start.31 = (f16[2048,128]{1,0:T(8,128)(2,1)S(1)}, f16[2048,128]{1,0:T(8,128)(2,1)S(1)}, u32[]{:S(2)}, u32[]{:S(2)}) collective-permute-start(f16[2048,128]{1,0:T(8,128)(2,1)S(1)} %fusion.8), channel_id=1, source_target_pairs={{0,96},{8,104},{16,112},{24,120},{32,0},{40,8},{48,16},{56,24},{64... | collective-permute-start | bytes 1572872 | tf_op jit(solution)/shard_map/ppermute | solution.py:411
  209.5 15.1 %collective-permute-start.26 = (f16[2048,128]{1,0:T(8,128)(2,1)S(1)}, f16[2048,128]{1,0:T(8,128)(2,1)S(1)}, u32[]{:S(2)}, u32[]{:S(2)}) collective-permute-start(f16[2048,128]{1,0:T(8,128)(2,1)S(1)} %fusion.14), channel_id=1, source_target_pairs={{0,8},{8,16},{16,24},{24,0},{32,40},{40,48},{48,56},{56,32},{64,72... | collective-permute-start | bytes 1572872 | tf_op jit(solution)/shard_map/ppermute | solution.py:414
  209.6 15.0 %collective-permute-start.27 = (f16[2048,128]{1,0:T(8,128)(2,1)S(1)}, f16[2048,128]{1,0:T(8,128)(2,1)S(1)}, u32[]{:S(2)}, u32[]{:S(2)}) collective-permute-start(f16[2048,128]{1,0:T(8,128)(2,1)S(1)} %fusion.12), channel_id=1, source_target_pairs={{0,24},{8,0},{16,8},{24,16},{32,56},{40,32},{48,40},{56,48},{64,88... | collective-permute-start | bytes 1572872 | tf_op jit(solution)/shard_map/ppermute | solution.py:414
  218.2 18.2 %collective-permute-start.32 = (f16[1024,128]{1,0:T(8,128)(2,1)}, f16[1024,128]{1,0:T(8,128)(2,1)S(1)}, u32[]{:S(2)}, u32[]{:S(2)}) collective-permute-start(f16[1024,128]{1,0:T(8,128)(2,1)} %fusion.37), channel_id=1, source_target_pairs={{0,8},{8,16},{16,24},{24,0},{32,40},{40,48},{48,56},{56,32},{64,72... | collective-permute-start | bytes 786440 | tf_op jit(solution)/shard_map/ppermute | solution.py:414
  219.4 17.4 %collective-permute-start.33 = (f16[1024,128]{1,0:T(8,128)(2,1)}, f16[1024,128]{1,0:T(8,128)(2,1)}, u32[]{:S(2)}, u32[]{:S(2)}) collective-permute-start(f16[1024,128]{1,0:T(8,128)(2,1)} %get-tuple-element.138), channel_id=1, source_target_pairs={{0,24},{8,0},{16,8},{24,16},{32,56},{40,32},{48,40},{56,48},{64,88... | collective-permute-start | bytes 786440 | tf_op jit(solution)/shard_map/ppermute | solution.py:414
  222.6 14.2 %collective-permute-start.34 = (f16[1024,128]{1,0:T(8,128)(2,1)}, f16[1024,128]{1,0:T(8,128)(2,1)}, u32[]{:S(2)}, u32[]{:S(2)}) collective-permute-start(f16[1024,128]{1,0:T(8,128)(2,1)} %get-tuple-element.139), channel_id=1, source_target_pairs={{0,16},{8,24},{16,0},{24,8},{32,48},{40,56},{48,32},{56,40},{64,80... | collective-permute-start | bytes 786440 | tf_op jit(solution)/shard_map/ppermute | solution.py:414
  226.6 11.6 %collective-permute-start.35 = (f16[1024,128]{1,0:T(8,128)(2,1)}, f16[1024,128]{1,0:T(8,128)(2,1)}, u32[]{:S(2)}, u32[]{:S(2)}) collective-permute-start(f16[1024,128]{1,0:T(8,128)(2,1)} %fusion.24), channel_id=1, source_target_pairs={{0,32},{8,40},{16,48},{24,56},{32,64},{40,72},{48,80},{56,88},{64,... | collective-permute-start | bytes 786440 | tf_op jit(solution)/shard_map/ppermute | solution.py:411
  228.9 10.2 %collective-permute-start.36 = (f16[1024,128]{1,0:T(8,128)(2,1)}, f16[1024,128]{1,0:T(8,128)(2,1)}, u32[]{:S(2)}, u32[]{:S(2)}) collective-permute-start(f16[1024,128]{1,0:T(8,128)(2,1)} %get-tuple-element.140), channel_id=1, source_target_pairs={{0,96},{8,104},{16,112},{24,120},{32,0},{40,8},{48,16},{56,24},{64... | collective-permute-start | bytes 786440 | tf_op jit(solution)/shard_map/ppermute | solution.py:411
  236.5 8.0 %collective-permute-start.37 = (f16[1024,128]{1,0:T(8,128)(2,1)S(1)}, f16[1024,128]{1,0:T(8,128)(2,1)S(1)}, u32[]{:S(2)}, u32[]{:S(2)}) collective-permute-start(f16[1024,128]{1,0:T(8,128)(2,1)S(1)} %copy-done.19), channel_id=1, source_target_pairs={{0,64},{8,72},{16,80},{24,88},{32,96},{40,104},{48,112},{56,120},{... | collective-permute-start | bytes 786440 | tf_op jit(solution)/shard_map/ppermute | solution.py:411
  (28 other events, 209.7 us)
where the time goes:
time: 248 us
  starting transfers between devices  60.5 us (24%)
  other arithmetic  60.2 us (24%)
  Pallas kernels  43.4 us (18%)
  blocking collectives  42.7 us (17%)
  waiting for transfers between devices  26.9 us (11%)
  matrix products  7.74 us (3%)
  between operations  4.02 us (2%)
    all_gather x1, blocking collectives, body(): gathered = lax.all_gather(mine, 'col', axis=0, tiled=True)  42.7 us
    ppermute x13, starting transfers between devices, send_z(): return lax.ppermute(value, 'row', along_z(shift))  32.2 us
    convert_element_type x15, other arithmetic, pack(): return by_rows((value * scales[1]).astype(f16))  25.8 us
    pallas_call x2, Pallas kernels, partial_rows(): pl.pallas_call(y_kernel, out_shape=sums_of(Y_PARTS) + (jax.ShapeDtypeStru...  24.7 us
    pallas_call x1, Pallas kernels, partial_cols(): pl.pallas_call(z_kernel, out_shape=sums_of(Z_PARTS * 2), in_specs=[pl.Blo...  16.8 us
    ppermute x13, starting transfers between devices, send_x(): return lax.ppermute(value, 'row', along_x(shift))  16.1 us
    ppermute x7, waiting for transfers between devices, send_y(): return lax.ppermute(value, 'col', ring(shift))  14.1 us
    another operation x3, other arithmetic, body(): lower_factor = jnp.linalg.cholesky(gram)  12.5 us
  transfers between devices with their start and end apart: 38, of which 10 were waited for; matrix products, arithmetic and copies ran while one was open for 23% of the time, Pallas kernels for 12%

commit v1 on v0

--- a/solution.py
+++ b/solution.py
@@ -369,9 +369,9 @@
 
 
 def ring_exchange(parts, send, scales):
-    messages = [pack(parts[r], scales) for r in (1, 3, 2)]
-    up, down, across = (unpack(send(m, r), scales) for m, r in zip(messages, (1, 3, 2)))
-    return parts[0] + up + down + across, messages
+    received = [send(pack(parts[r], scales), r) for r in (1, 3, 2)]
+    up, down, across = (unpack(message, scales) for message in received)
+    return parts[0] + up + down + across, received
 
 
 def exponent_of(largest):
@@ -392,7 +392,6 @@
 
 
 def body(blocks, sketch, block_row, block_col, counts):
-    highest = lax.Precision.HIGHEST
     blocks = blocks[0, 0]
     rows, cols = block_row[0, 0], block_col[0, 0]
     count = counts[0, 0]
@@ -486,9 +485,9 @@
     mine, z_scales = lax.optimization_barrier((by_rows(mine), z_scales))
     gathered = lax.all_gather(mine, "col", axis=0, tiled=True)
     gram, tile_scales = read_shares(gathered)
-    gram = ring_fold(gram, send_x, jnp.add)[0]
+    gram = ring_fold(by_rows(gram), send_x, jnp.add)[0]
     partial = flat(partial_cols(count, z_target, rows, blocks, gathered, tile_scales))
-    gram = ring_fold(gram, send_z, jnp.add)[0]
+    gram = by_rows(ring_fold(gram, send_z, jnp.add)[0])
 
     rings = [(partial[:8], send_x, send_z), (partial[8:], send_z, send_x)]
     around = z_scales, z_scales
@@ -502,18 +501,22 @@
         ring_second(r, values[2:4], send, z_scales, *around)
         for r, (values, send, _) in zip(received, rings)
     ]
+    inverse = lax.linalg.triangular_solve(
+        lower_factor, jnp.eye(K, dtype=f32), left_side=True, lower=True
+    )
     thirds = []
     for (direct, sums, _), (values, _, send) in zip(seconds, rings):
         total = ring_total(direct, sums, [values[4:6], values[6:]], z_scales, *around)
         quarters = [total(r // 2, r % 2 * 4 * B, (r % 2 + 1) * 4 * B) for r in range(4)]
         thirds.append(ring_exchange(quarters, send, z_scales))
-    inverse = lax.linalg.triangular_solve(
-        lower_factor, jnp.eye(K, dtype=f32), left_side=True, lower=True
-    )
-    basis_factor = after(inverse, seconds[1][2][1])
-    q_share = jnp.dot(y_share, basis_factor.T, precision=highest, preferred_element_type=f32)
+    basis_factor = after(inverse, thirds[0][1][0])
+    q_share = jnp.dot(
+        y_share, basis_factor.T, precision=lax.Precision.HIGH, preferred_element_type=f32
+    )
     z_raw = jnp.concatenate([z for z, _ in thirds], axis=0)
-    z_share = jnp.dot(z_raw, inverse.T, precision=highest, preferred_element_type=f32)
+    z_share = jnp.dot(
+        z_raw, inverse.T, precision=lax.Precision.HIGH, preferred_element_type=f32
+    )
     row_scale = math.sqrt(BR * B * lax.axis_size("row"))
     return (q_share * row_scale, z_share[None])
 

time: 248 us -> 244 us (0.984); the launches traced: 248 us -> 241 us
  starting transfers between devices: 60.5 us -> 50.8 us
  waiting for transfers between devices: 26.9 us -> 31.7 us
    ppermute x13, starting transfers between devices: 32.2 us -> 20.1 us  [send_z(): return lax.ppermute(value, 'row', along_z(shift))]
    ppermute x7, waiting for transfers between devices: 14.1 us -> 18.5 us  [send_y(): return lax.ppermute(value, 'col', ring(shift))]
    ppermute x13, starting transfers between devices: 16.1 us -> 20.3 us  [send_x(): return lax.ppermute(value, 'row', along_x(shift))]
    ppermute x13, waiting for transfers between devices: 1.78 us -> 4.66 us  [send_z(): return lax.ppermute(value, 'row', along_z(shift))]
    ppermute x13, waiting for transfers between devices: 11 us -> 8.55 us  [send_x(): return lax.ppermute(value, 'row', along_x(shift))]
  transfers between devices with their start and end apart: 38 -> 38, of which waited for: 10 -> 10; matrix products, arithmetic and copies ran while one was open for 23% -> 24% of each run, Pallas kernels for 12% -> 13%
where the time goes in v1:
time: 244 us; the launch traced here: 241 us
  other arithmetic  59.6 us (24%)
  starting transfers between devices  50.8 us (21%)
  Pallas kernels  44.5 us (18%)
  blocking collectives  42.7 us (18%)
  waiting for transfers between devices  31.7 us (13%)
  matrix products  6.54 us (3%)
  between operations  4.01 us (2%)
    all_gather x1, blocking collectives, body(): gathered = lax.all_gather(mine, 'col', axis=0, tiled=True)  42.7 us
    pallas_call x2, Pallas kernels, partial_rows(): pl.pallas_call(y_kernel, out_shape=sums_of(Y_PARTS) + (jax.ShapeDtypeStru...  24.9 us
    convert_element_type x15, other arithmetic, pack(): return by_rows((value * scales[1]).astype(f16))  24.9 us
    ppermute x13, starting transfers between devices, send_x(): return lax.ppermute(value, 'row', along_x(shift))  20.3 us
    ppermute x13, starting transfers between devices, send_z(): return lax.ppermute(value, 'row', along_z(shift))  20.1 us
    ppermute x7, waiting for transfers between devices, send_y(): return lax.ppermute(value, 'col', ring(shift))  18.5 us
    pallas_call x1, Pallas kernels, partial_cols(): pl.pallas_call(z_kernel, out_shape=sums_of(Z_PARTS * 2), in_specs=[pl.Blo...  17.7 us
    another operation x3, other arithmetic, body(): lower_factor = jnp.linalg.cholesky(gram)  12.4 us
  transfers between devices with their start and end apart: 38, of which 10 were waited for; matrix products, arithmetic and copies ran while one was open for 24% of the time, Pallas kernels for 13%

profile of v1, /device:TPU:24, one launch (start us, length us, event | category | flops | bytes accessed | tf_op | source)
XLA Modules:
  0.0 241.2 jit_solution(2238772360375368437)
XLA Ops:
  3.7 12.3 %partial_rows.3 = (f32[32,256,128]{2,1,0:T(8,128)}, f32[16,256,128]{2,1,0:T(8,128)}, f32[16,256,128]{2,1,0:T(8,128)}, f32[8,128]{1,0:T(8,128)}) custom-call(s32[1]{0:T(128)} %bitcast.146.count, s32[96]{0:T(128)} %and_select_fusion.targets, s32[96]{0:T(128)} %bitcast.184, bf16[96,256,256]{2,1,0:T(8,128)(2,1)} %bitcast.152, bf16[128,256,128]{2,1,0:T(8,128)(2,1)} %bitcast.155), custom_call_target="tpu_custom_call" | custom-call | flops 805306368 | bytes 62914560 | tf_op jit(solution)/shard_map/partial_rows/pallas_call | solution.py:204
  17.1 12.7 %partial_rows.2 = (f32[32,256,128]{2,1,0:T(8,128)}, f32[16,256,128]{2,1,0:T(8,128)}, f32[16,256,128]{2,1,0:T(8,128)}, f32[8,128]{1,0:T(8,128)}) custom-call(s32[1]{0:T(128)} %bitcast.145.count, s32[96]{0:T(128)} %get-tuple-element.128.targets, s32[96]{0:T(128)} %bitcast.185, bf16[96,256,256]{2,1,0:T(8,128)(2,1)} %bitcast.153, bf16[128,256,128]{2,1,0:T(8,128)(2,1)} %bitcast.156), custom_call_target="tpu_custom_call" | custom-call | flops 805306368 | bytes 62914560 | tf_op jit(solution)/shard_map/partial_rows/pallas_call | solution.py:204
  30.6 4.5 %fusion.1 = (f16[16,256,128]{2,1,0:T(8,128)(2,1)S(1)}, f16[16,256,128]{2,1,0:T(8,128)(2,1)S(1)}) fusion(f32[32,256,128]{2,1,0:T(8,128)} %collective-permute-done.3, f32[32,256,128]{2,1,0:T(8,128)} %get-tuple-element.68, f32[]{:T(128)S(1)} %bitcast.195), kind=kLoop, calls=%fused_computation.4 | loop fusion | flops 3145728 | bytes 10485764 | tf_op jit(solution)/shard_map/convert_element_type | solution.py:331
  35.2 2.6 %collective-permute-start.5 = (f32[8,128]{1,0:T(8,128)S(1)}, f32[8,128]{1,0:T(8,128)S(1)}, u32[]{:S(2)}, u32[]{:S(2)}) collective-permute-start(f32[8,128]{1,0:T(8,128)S(1)} %get-tuple-element.70), channel_id=1, source_target_pairs={{0,2},{1,3},{2,4},{3,5},{4,6},{5,7},{6,0},{7,1},{8,10},{9,11},{10,... | collective-permute-start | bytes 12296 | tf_op jit(solution)/shard_map/ppermute | solution.py:407
  40.3 3.2 %collective-permute-start.7 = (f16[4096,128]{1,0:T(8,128)(2,1)S(1)}, f16[4096,128]{1,0:T(8,128)(2,1)S(1)}, u32[]{:S(2)}, u32[]{:S(2)}) collective-permute-start(f16[4096,128]{1,0:T(8,128)(2,1)S(1)} %bitcast.160), channel_id=1, source_target_pairs={{0,2},{1,3},{2,4},{3,5},{4,6},{5,7},{6,0},{7,1},{8,10},{9,11},{10,... | collective-permute-start | bytes 3145736 | tf_op jit(solution)/shard_map/ppermute | solution.py:407
  43.6 2.2 slice_add_fusion.2
  47.8 2.6 %collective-permute-start.14 = (f32[8,128]{1,0:T(8,128)S(1)}, f32[8,128]{1,0:T(8,128)S(1)}, u32[]{:S(2)}, u32[]{:S(2)}) collective-permute-start(f32[8,128]{1,0:T(8,128)S(1)} %max.84), channel_id=1, source_target_pairs={{0,96},{8,104},{16,112},{24,120},{32,0},{40,8},{48,16},{56,24},{64... | collective-permute-start | bytes 12296 | tf_op jit(solution)/shard_map/ppermute | solution.py:410
  52.6 4.2 %collective-permute-start.16 = (f32[8,128]{1,0:T(8,128)S(1)}, f32[8,128]{1,0:T(8,128)S(1)}, u32[]{:S(2)}, u32[]{:S(2)}) collective-permute-start(f32[8,128]{1,0:T(8,128)S(1)} %maximum_maximum_fusion.1), channel_id=1, source_target_pairs={{0,8},{8,16},{16,24},{24,0},{32,40},{40,48},{48,56},{56,32},{64,72... | collective-permute-start | bytes 12296 | tf_op jit(solution)/shard_map/ppermute | solution.py:413
  56.8 2.6 %collective-permute-start.17 = (f32[8,128]{1,0:T(8,128)S(1)}, f32[8,128]{1,0:T(8,128)S(1)}, u32[]{:S(2)}, u32[]{:S(2)}) collective-permute-start(f32[8,128]{1,0:T(8,128)S(1)} %maximum_maximum_fusion.1), channel_id=1, source_target_pairs={{0,24},{8,0},{16,8},{24,16},{32,56},{40,32},{48,40},{56,48},{64,88... | collective-permute-start | bytes 12296 | tf_op jit(solution)/shard_map/ppermute | solution.py:413
  59.4 6.4 %collective-permute-done.8 = f16[4096,128]{1,0:T(8,128)(2,1)S(1)} collective-permute-done((f16[4096,128]{1,0:T(8,128)(2,1)S(1)}, f16[4096,128]{1,0:T(8,128)(2,1)S(1)}, u32[]{:S(2)}, u32[]{:S(2)}) %collective-permute-start.8) | collective-permute-done | bytes 1048608 | tf_op jit(solution)/shard_map/ppermute | solution.py:407
  66.6 3.0 %collective-permute-start.9 = (f16[2048,128]{1,0:T(8,128)(2,1)S(1)}, f16[2048,128]{1,0:T(8,128)(2,1)S(1)}, u32[]{:S(2)}, u32[]{:S(2)}) collective-permute-start(f16[2048,128]{1,0:T(8,128)(2,1)S(1)} %multiply_convert_fusion.5), channel_id=1, source_target_pairs={{0,2},{1,3},{2,4},{3,5},{4,6},{5,7},{6,0},{7,1},{8,10},{9,11},{10,... | collective-permute-start | bytes 1572872 | tf_op jit(solution)/shard_map/ppermute | solution.py:407
  69.7 10.1 %collective-permute-done.10 = f16[2048,128]{1,0:T(8,128)(2,1)S(1)} collective-permute-done((f16[2048,128]{1,0:T(8,128)(2,1)S(1)}, f16[2048,128]{1,0:T(8,128)(2,1)S(1)}, u32[]{:S(2)}, u32[]{:S(2)}) %collective-permute-start.10) | collective-permute-done | bytes 524320 | tf_op jit(solution)/shard_map/ppermute | solution.py:407
  80.9 2.4 abs_reduce_fusion.1
  85.9 42.7 %all-gather.1.gathered.table = s16[35072,128]{1,0:T(8,128)(2,1)} all-gather(s16[4384,128]{1,0:T(8,128)(2,1)S(1)} %pad_add_fusion), channel_id=1, replica_groups=mesh['row'=16,'col'=8] {'col'}, dimensions={0}, use_global_device_ids=true | all-gather | bytes 10100736 | tf_op jit(solution)/shard_map/all_gather | solution.py:486
  131.7 2.6 %collective-permute-start.20 = (f32[128,128]{1,0:T(8,128)}, f32[128,128]{1,0:T(8,128)S(1)}, u32[]{:S(2)}, u32[]{:S(2)}) collective-permute-start(f32[128,128]{1,0:T(8,128)} %get-tuple-element.90), channel_id=1, source_target_pairs={{0,96},{8,104},{16,112},{24,120},{32,0},{40,8},{48,16},{56,24},{64... | collective-permute-start | bytes 196616 | tf_op jit(solution)/shard_map/ppermute | solution.py:410
  134.3 17.7 %partial_cols.1 = (f32[16,256,128]{2,1,0:T(8,128)}, f32[16,256,128]{2,1,0:T(8,128)}, f32[8,256,128]{2,1,0:T(8,128)}, f32[8,256,128]{2,1,0:T(8,128)}, f32[4,256,1...) custom-call(s32[1]{0:T(128)} %bitcast.147.count, ...), custom_call_target="tpu_custom_call" | custom-call | flops 3221225472 | bytes 44040192 | tf_op jit(solution)/shard_map/partial_cols/pallas_call | solution.py:304
  152.0 3.0 %multiply_convert_fusion.2 = f16[16,256,128]{2,1,0:T(8,128)(2,1)} fusion(f32[16,256,128]{2,1,0:T(8,128)} %get-tuple-element.95, f32[]{:T(128)S(1)} %bitcast.163), kind=kLoop, calls=%fused_computation.11 | loop fusion | flops 1048576 | bytes 3145732 | tf_op jit(solution)/shard_map/convert_element_type | solution.py:331
  155.2 3.2 %collective-permute-start.23 = (f32[128,128]{1,0:T(8,128)S(1)}, f32[128,128]{1,0:T(8,128)S(1)}, u32[]{:S(2)}, u32[]{:S(2)}) collective-permute-start(f32[128,128]{1,0:T(8,128)S(1)} %add_add_fusion.1), channel_id=1, source_target_pairs={{0,24},{8,0},{16,8},{24,16},{32,56},{40,32},{48,40},{56,48},{64,88... | collective-permute-start | bytes 196616 | tf_op jit(solution)/shard_map/ppermute | solution.py:413
  159.7 2.0 collective-permute-start.24
  163.3 3.0 %multiply_convert_fusion = f16[16,256,128]{2,1,0:T(8,128)(2,1)} fusion(f32[16,256,128]{2,1,0:T(8,128)} %get-tuple-element.110, f32[]{:T(128)S(6)} %add.240), kind=kLoop, calls=%fused_computation.9 | loop fusion | flops 1048576 | bytes 3145732 | tf_op jit(solution)/shard_map/convert_element_type | solution.py:331
  166.3 2.1 collective-permute-start.32
  169.6 11.7 %cholesky.17 = f32[128,128]{1,0:T(8,128)S(1)} custom-call(f32[128,128]{1,0:T(8,128)S(1)} %fusion.45), custom_call_target="Cholesky" | custom-call | tf_op jit(solution)/shard_map/jit(cholesky)/cholesky | solution.py:499
  182.7 9.8 %custom-call.6 = f32[1,128,128]{1,2,0:T(8,128)S(1)} custom-call(f32[1,128,128]{2,1,0:T(8,128)S(1)} %fusion.42), custom_call_target="InvertDiagBlocksLowerTriangular" | custom-call | tf_op jit(solution)/shard_map/triangular_solve | solution.py:504
  196.0 2.1 collective-permute-start.26
  198.1 2.0 collective-permute-start.27
  202.5 2.8 %collective-permute-start.34 = (f16[2048,128]{1,0:T(8,128)(2,1)S(1)}, f16[2048,128]{1,0:T(8,128)(2,1)S(1)}, u32[]{:S(2)}, u32[]{:S(2)}) collective-permute-start(f16[2048,128]{1,0:T(8,128)(2,1)S(1)} %fusion.8), channel_id=1, source_target_pairs={{0,24},{8,0},{16,8},{24,16},{32,56},{40,32},{48,40},{56,48},{64,88... | collective-permute-start | bytes 1572872 | tf_op jit(solution)/shard_map/ppermute | solution.py:413
  205.3 5.3 %collective-permute-done.26 = f16[2048,128]{1,0:T(8,128)(2,1)S(1)} collective-permute-done((f16[2048,128]{1,0:T(8,128)(2,1)S(1)}, f16[2048,128]{1,0:T(8,128)(2,1)S(1)}, u32[]{:S(2)}, u32[]{:S(2)}) %collective-permute-start.26) | collective-permute-done | bytes 524320 | tf_op jit(solution)/shard_map/ppermute | solution.py:410
  211.2 2.2 fusion.34
  213.4 3.0 %collective-permute-start.29 = (f16[1024,128]{1,0:T(8,128)(2,1)}, f16[1024,128]{1,0:T(8,128)(2,1)}, u32[]{:S(2)}, u32[]{:S(2)}) collective-permute-start(f16[1024,128]{1,0:T(8,128)(2,1)} %get-tuple-element.136), channel_id=1, source_target_pairs={{0,24},{8,0},{16,8},{24,16},{32,56},{40,32},{48,40},{56,48},{64,88... | collective-permute-start | bytes 786440 | tf_op jit(solution)/shard_map/ppermute | solution.py:413
  224.9 4.5 %collective-permute-done.28 = f16[1024,128]{1,0:T(8,128)(2,1)S(1)} collective-permute-done((f16[1024,128]{1,0:T(8,128)(2,1)S(1)}, f16[1024,128]{1,0:T(8,128)(2,1)S(1)}, u32[]{:S(2)}, u32[]{:S(2)}) %collective-permute-start.28) | collective-permute-done | bytes 262176 | tf_op jit(solution)/shard_map/ppermute | solution.py:413
  229.4 2.6 %collective-permute-start.37 = (f16[1024,128]{1,0:T(8,128)(2,1)}, f16[1024,128]{1,0:T(8,128)(2,1)S(1)}, u32[]{:S(2)}, u32[]{:S(2)}) collective-permute-start(f16[1024,128]{1,0:T(8,128)(2,1)} %get-tuple-element.139), channel_id=1, source_target_pairs={{0,64},{8,72},{16,80},{24,88},{32,96},{40,104},{48,112},{56,120},{... | collective-permute-start | bytes 786440 | tf_op jit(solution)/shard_map/ppermute | solution.py:410
  234.9 2.3 convolution_multiply_fusion
  (153 shorter events, 44.0 us)
Async XLA Ops:
  15.9 14.6 %collective-permute-start.3 = (f32[32,256,128]{2,1,0:T(8,128)}, f32[32,256,128]{2,1,0:T(8,128)}, u32[]{:S(2)}, u32[]{:S(2)}) collective-permute-start(f32[32,256,128]{2,1,0:T(8,128)} %get-tuple-element.69), channel_id=1, source_target_pairs={{0,1},{1,0},{2,3},{3,2},{4,5},{5,4},{6,7},{7,6},{8,9},{9,8},{10,11... | collective-permute-start | bytes 12582920 | tf_op jit(solution)/shard_map/ppermute | solution.py:404
  16.0 27.6 %collective-permute-start = (f32[16,256,128]{2,1,0:T(8,128)}, f32[16,256,128]{2,1,0:T(8,128)S(1)}, u32[]{:S(2)}, u32[]{:S(2)}) collective-permute-start(f32[16,256,128]{2,1,0:T(8,128)} %get-tuple-element.64), channel_id=1, source_target_pairs={{0,1},{1,0},{2,3},{3,2},{4,5},{5,4},{6,7},{7,6},{8,9},{9,8},{10,11... | collective-permute-start | bytes 6291464 | tf_op jit(solution)/shard_map/ppermute | solution.py:404
  16.5 27.1 %collective-permute-start.1 = (f32[16,256,128]{2,1,0:T(8,128)}, f32[16,256,128]{2,1,0:T(8,128)}, u32[]{:S(2)}, u32[]{:S(2)}) collective-permute-start(f32[16,256,128]{2,1,0:T(8,128)} %get-tuple-element.65), channel_id=1, source_target_pairs={{0,1},{1,0},{2,3},{3,2},{4,5},{5,4},{6,7},{7,6},{8,9},{9,8},{10,11... | collective-permute-start | bytes 6291464 | tf_op jit(solution)/shard_map/ppermute | solution.py:404
  16.6 13.1 %collective-permute-start.2 = (f32[8,128]{1,0:T(8,128)}, f32[8,128]{1,0:T(8,128)S(1)}, u32[]{:S(2)}, u32[]{:S(2)}) collective-permute-start(f32[8,128]{1,0:T(8,128)} %get-tuple-element.67), channel_id=1, source_target_pairs={{0,1},{1,0},{2,3},{3,2},{4,5},{5,4},{6,7},{7,6},{8,9},{9,8},{10,11... | collective-permute-start | bytes 12296 | tf_op jit(solution)/shard_map/ppermute | solution.py:404
  37.8 5.7 %collective-permute-start.6 = (f32[8,128]{1,0:T(8,128)S(1)}, f32[8,128]{1,0:T(8,128)S(1)}, u32[]{:S(2)}, u32[]{:S(2)}) collective-permute-start(f32[8,128]{1,0:T(8,128)S(1)} %get-tuple-element.70), channel_id=1, source_target_pairs={{0,6},{1,7},{2,0},{3,1},{4,2},{5,3},{6,4},{7,5},{8,14},{9,15},{10,... | collective-permute-start | bytes 12296 | tf_op jit(solution)/shard_map/ppermute | solution.py:407
  40.3 25.6 %collective-permute-start.8 = (f16[4096,128]{1,0:T(8,128)(2,1)S(1)}, f16[4096,128]{1,0:T(8,128)(2,1)S(1)}, u32[]{:S(2)}, u32[]{:S(2)}) collective-permute-start(f16[4096,128]{1,0:T(8,128)(2,1)S(1)} %bitcast.161), channel_id=1, source_target_pairs={{0,6},{1,7},{2,0},{3,1},{4,2},{5,3},{6,4},{7,5},{8,14},{9,15},{10,... | collective-permute-start | bytes 3145736 | tf_op jit(solution)/shard_map/ppermute | solution.py:407
  40.3 25.8 %collective-permute-start.7 = (f16[4096,128]{1,0:T(8,128)(2,1)S(1)}, f16[4096,128]{1,0:T(8,128)(2,1)S(1)}, u32[]{:S(2)}, u32[]{:S(2)}) collective-permute-start(f16[4096,128]{1,0:T(8,128)(2,1)S(1)} %bitcast.160), channel_id=1, source_target_pairs={{0,2},{1,3},{2,4},{3,5},{4,6},{5,7},{6,0},{7,1},{8,10},{9,11},{10,... | collective-permute-start | bytes 3145736 | tf_op jit(solution)/shard_map/ppermute | solution.py:407
  52.0 17.7 %collective-permute-start.15 = (f32[8,128]{1,0:T(8,128)S(1)}, f32[8,128]{1,0:T(8,128)S(1)}, u32[]{:S(2)}, u32[]{:S(2)}) collective-permute-start(f32[8,128]{1,0:T(8,128)S(1)} %maximum_maximum_fusion.1), channel_id=1, source_target_pairs={{0,16},{8,24},{16,0},{24,8},{32,48},{40,56},{48,32},{56,40},{64,80... | collective-permute-start | bytes 12296 | tf_op jit(solution)/shard_map/ppermute | solution.py:413
  52.6 17.0 %collective-permute-start.16 = (f32[8,128]{1,0:T(8,128)S(1)}, f32[8,128]{1,0:T(8,128)S(1)}, u32[]{:S(2)}, u32[]{:S(2)}) collective-permute-start(f32[8,128]{1,0:T(8,128)S(1)} %maximum_maximum_fusion.1), channel_id=1, source_target_pairs={{0,8},{8,16},{16,24},{24,0},{32,40},{40,48},{48,56},{56,32},{64,72... | collective-permute-start | bytes 12296 | tf_op jit(solution)/shard_map/ppermute | solution.py:413
  56.8 12.9 %collective-permute-start.17 = (f32[8,128]{1,0:T(8,128)S(1)}, f32[8,128]{1,0:T(8,128)S(1)}, u32[]{:S(2)}, u32[]{:S(2)}) collective-permute-start(f32[8,128]{1,0:T(8,128)S(1)} %maximum_maximum_fusion.1), channel_id=1, source_target_pairs={{0,24},{8,0},{16,8},{24,16},{32,56},{40,32},{48,40},{56,48},{64,88... | collective-permute-start | bytes 12296 | tf_op jit(solution)/shard_map/ppermute | solution.py:413
  66.3 13.5 %collective-permute-start.10 = (f16[2048,128]{1,0:T(8,128)(2,1)S(1)}, f16[2048,128]{1,0:T(8,128)(2,1)S(1)}, u32[]{:S(2)}, u32[]{:S(2)}) collective-permute-start(f16[2048,128]{1,0:T(8,128)(2,1)S(1)} %multiply_convert_fusion.4), channel_id=1, source_target_pairs={{0,6},{1,7},{2,0},{3,1},{4,2},{5,3},{6,4},{7,5},{8,14},{9,15},{10,... | collective-permute-start | bytes 1572872 | tf_op jit(solution)/shard_map/ppermute | solution.py:407
  66.6 13.1 %collective-permute-start.9 = (f16[2048,128]{1,0:T(8,128)(2,1)S(1)}, f16[2048,128]{1,0:T(8,128)(2,1)S(1)}, u32[]{:S(2)}, u32[]{:S(2)}) collective-permute-start(f16[2048,128]{1,0:T(8,128)(2,1)S(1)} %multiply_convert_fusion.5), channel_id=1, source_target_pairs={{0,2},{1,3},{2,4},{3,5},{4,6},{5,7},{6,0},{7,1},{8,10},{9,11},{10,... | collective-permute-start | bytes 1572872 | tf_op jit(solution)/shard_map/ppermute | solution.py:407
  130.4 24.6 %collective-permute-start.18 = (f32[128,128]{1,0:T(8,128)}, f32[128,128]{1,0:T(8,128)S(1)}, u32[]{:S(2)}, u32[]{:S(2)}) collective-permute-start(f32[128,128]{1,0:T(8,128)} %get-tuple-element.90), channel_id=1, source_target_pairs={{0,64},{8,72},{16,80},{24,88},{32,96},{40,104},{48,112},{56,120},{... | collective-permute-start | bytes 196616 | tf_op jit(solution)/shard_map/ppermute | solution.py:410
  131.0 24.0 %collective-permute-start.19 = (f32[128,128]{1,0:T(8,128)}, f32[128,128]{1,0:T(8,128)S(1)}, u32[]{:S(2)}, u32[]{:S(2)}) collective-permute-start(f32[128,128]{1,0:T(8,128)} %get-tuple-element.90), channel_id=1, source_target_pairs={{0,32},{8,40},{16,48},{24,56},{32,64},{40,72},{48,80},{56,88},{64,... | collective-permute-start | bytes 196616 | tf_op jit(solution)/shard_map/ppermute | solution.py:410
  131.7 23.3 %collective-permute-start.20 = (f32[128,128]{1,0:T(8,128)}, f32[128,128]{1,0:T(8,128)S(1)}, u32[]{:S(2)}, u32[]{:S(2)}) collective-permute-start(f32[128,128]{1,0:T(8,128)} %get-tuple-element.90), channel_id=1, source_target_pairs={{0,96},{8,104},{16,112},{24,120},{32,0},{40,8},{48,16},{56,24},{64... | collective-permute-start | bytes 196616 | tf_op jit(solution)/shard_map/ppermute | solution.py:410
  155.0 37.8 %collective-permute-start.25 = (f16[4096,128]{1,0:T(8,128)(2,1)}, f16[4096,128]{1,0:T(8,128)(2,1)}, u32[]{:S(2)}, u32[]{:S(2)}) collective-permute-start(f16[4096,128]{1,0:T(8,128)(2,1)} %bitcast.24), channel_id=1, source_target_pairs={{0,96},{8,104},{16,112},{24,120},{32,0},{40,8},{48,16},{56,24},{64... | collective-permute-start | bytes 3145736 | tf_op jit(solution)/shard_map/ppermute | solution.py:410
  155.1 6.7 %collective-permute-start.21 = (f32[128,128]{1,0:T(8,128)S(1)}, f32[128,128]{1,0:T(8,128)S(1)}, u32[]{:S(2)}, u32[]{:S(2)}) collective-permute-start(f32[128,128]{1,0:T(8,128)S(1)} %add_add_fusion.1), channel_id=1, source_target_pairs={{0,16},{8,24},{16,0},{24,8},{32,48},{40,56},{48,32},{56,40},{64,80... | collective-permute-start | bytes 196616 | tf_op jit(solution)/shard_map/ppermute | solution.py:413
  155.2 6.7 %collective-permute-start.22 = (f32[128,128]{1,0:T(8,128)S(1)}, f32[128,128]{1,0:T(8,128)S(1)}, u32[]{:S(2)}, u32[]{:S(2)}) collective-permute-start(f32[128,128]{1,0:T(8,128)S(1)} %add_add_fusion.1), channel_id=1, source_target_pairs={{0,8},{8,16},{16,24},{24,0},{32,40},{40,48},{48,56},{56,32},{64,72... | collective-permute-start | bytes 196616 | tf_op jit(solution)/shard_map/ppermute | solution.py:413
  155.2 6.6 %collective-permute-start.23 = (f32[128,128]{1,0:T(8,128)S(1)}, f32[128,128]{1,0:T(8,128)S(1)}, u32[]{:S(2)}, u32[]{:S(2)}) collective-permute-start(f32[128,128]{1,0:T(8,128)S(1)} %add_add_fusion.1), channel_id=1, source_target_pairs={{0,24},{8,0},{16,8},{24,16},{32,56},{40,32},{48,40},{56,48},{64,88... | collective-permute-start | bytes 196616 | tf_op jit(solution)/shard_map/ppermute | solution.py:413
  159.7 34.7 %collective-permute-start.24 = (f16[4096,128]{1,0:T(8,128)(2,1)}, f16[4096,128]{1,0:T(8,128)(2,1)}, u32[]{:S(2)}, u32[]{:S(2)}) collective-permute-start(f16[4096,128]{1,0:T(8,128)(2,1)} %bitcast.23), channel_id=1, source_target_pairs={{0,32},{8,40},{16,48},{24,56},{32,64},{40,72},{48,80},{56,88},{64,... | collective-permute-start | bytes 3145736 | tf_op jit(solution)/shard_map/ppermute | solution.py:410
  166.3 33.8 %collective-permute-start.32 = (f16[4096,128]{1,0:T(8,128)(2,1)}, f16[4096,128]{1,0:T(8,128)(2,1)}, u32[]{:S(2)}, u32[]{:S(2)}) collective-permute-start(f16[4096,128]{1,0:T(8,128)(2,1)} %bitcast.34), channel_id=1, source_target_pairs={{0,24},{8,0},{16,8},{24,16},{32,56},{40,32},{48,40},{56,48},{64,88... | collective-permute-start | bytes 3145736 | tf_op jit(solution)/shard_map/ppermute | solution.py:413
  169.6 32.0 %collective-permute-start.31 = (f16[4096,128]{1,0:T(8,128)(2,1)}, f16[4096,128]{1,0:T(8,128)(2,1)S(1)}, u32[]{:S(2)}, u32[]{:S(2)}) collective-permute-start(f16[4096,128]{1,0:T(8,128)(2,1)} %bitcast.33), channel_id=1, source_target_pairs={{0,8},{8,16},{16,24},{24,0},{32,40},{40,48},{48,56},{56,32},{64,72... | collective-permute-start | bytes 3145736 | tf_op jit(solution)/shard_map/ppermute | solution.py:413
  196.0 14.6 %collective-permute-start.26 = (f16[2048,128]{1,0:T(8,128)(2,1)S(1)}, f16[2048,128]{1,0:T(8,128)(2,1)S(1)}, u32[]{:S(2)}, u32[]{:S(2)}) collective-permute-start(f16[2048,128]{1,0:T(8,128)(2,1)S(1)} %fusion.14), channel_id=1, source_target_pairs={{0,32},{8,40},{16,48},{24,56},{32,64},{40,72},{48,80},{56,88},{64,... | collective-permute-start | bytes 1572872 | tf_op jit(solution)/shard_map/ppermute | solution.py:410
  198.1 13.1 %collective-permute-start.27 = (f16[2048,128]{1,0:T(8,128)(2,1)S(1)}, f16[2048,128]{1,0:T(8,128)(2,1)S(1)}, u32[]{:S(2)}, u32[]{:S(2)}) collective-permute-start(f16[2048,128]{1,0:T(8,128)(2,1)S(1)} %fusion.12), channel_id=1, source_target_pairs={{0,96},{8,104},{16,112},{24,120},{32,0},{40,8},{48,16},{56,24},{64... | collective-permute-start | bytes 1572872 | tf_op jit(solution)/shard_map/ppermute | solution.py:410
  201.9 16.6 %collective-permute-start.33 = (f16[2048,128]{1,0:T(8,128)(2,1)S(1)}, f16[2048,128]{1,0:T(8,128)(2,1)S(1)}, u32[]{:S(2)}, u32[]{:S(2)}) collective-permute-start(f16[2048,128]{1,0:T(8,128)(2,1)S(1)} %fusion.10), channel_id=1, source_target_pairs={{0,8},{8,16},{16,24},{24,0},{32,40},{40,48},{48,56},{56,32},{64,72... | collective-permute-start | bytes 1572872 | tf_op jit(solution)/shard_map/ppermute | solution.py:413
  202.5 16.0 %collective-permute-start.34 = (f16[2048,128]{1,0:T(8,128)(2,1)S(1)}, f16[2048,128]{1,0:T(8,128)(2,1)S(1)}, u32[]{:S(2)}, u32[]{:S(2)}) collective-permute-start(f16[2048,128]{1,0:T(8,128)(2,1)S(1)} %fusion.8), channel_id=1, source_target_pairs={{0,24},{8,0},{16,8},{24,16},{32,56},{40,32},{48,40},{56,48},{64,88... | collective-permute-start | bytes 1572872 | tf_op jit(solution)/shard_map/ppermute | solution.py:413
  213.4 19.8 %collective-permute-start.29 = (f16[1024,128]{1,0:T(8,128)(2,1)}, f16[1024,128]{1,0:T(8,128)(2,1)}, u32[]{:S(2)}, u32[]{:S(2)}) collective-permute-start(f16[1024,128]{1,0:T(8,128)(2,1)} %get-tuple-element.136), channel_id=1, source_target_pairs={{0,24},{8,0},{16,8},{24,16},{32,56},{40,32},{48,40},{56,48},{64,88... | collective-permute-start | bytes 786440 | tf_op jit(solution)/shard_map/ppermute | solution.py:413
  216.3 16.8 %collective-permute-start.30 = (f16[1024,128]{1,0:T(8,128)(2,1)S(1)}, f16[1024,128]{1,0:T(8,128)(2,1)}, u32[]{:S(2)}, u32[]{:S(2)}) collective-permute-start(f16[1024,128]{1,0:T(8,128)(2,1)S(1)} %get-tuple-element.137), channel_id=1, source_target_pairs={{0,16},{8,24},{16,0},{24,8},{32,48},{40,56},{48,32},{56,40},{64,80... | collective-permute-start | bytes 786440 | tf_op jit(solution)/shard_map/ppermute | solution.py:413
  218.1 11.4 %collective-permute-start.28 = (f16[1024,128]{1,0:T(8,128)(2,1)S(1)}, f16[1024,128]{1,0:T(8,128)(2,1)S(1)}, u32[]{:S(2)}, u32[]{:S(2)}) collective-permute-start(f16[1024,128]{1,0:T(8,128)(2,1)S(1)} %fusion.41), channel_id=1, source_target_pairs={{0,8},{8,16},{16,24},{24,0},{32,40},{40,48},{48,56},{56,32},{64,72... | collective-permute-start | bytes 786440 | tf_op jit(solution)/shard_map/ppermute | solution.py:413
  220.5 16.8 %collective-permute-start.35 = (f16[1024,128]{1,0:T(8,128)(2,1)}, f16[1024,128]{1,0:T(8,128)(2,1)}, u32[]{:S(2)}, u32[]{:S(2)}) collective-permute-start(f16[1024,128]{1,0:T(8,128)(2,1)} %fusion.24), channel_id=1, source_target_pairs={{0,32},{8,40},{16,48},{24,56},{32,64},{40,72},{48,80},{56,88},{64,... | collective-permute-start | bytes 786440 | tf_op jit(solution)/shard_map/ppermute | solution.py:410
  223.4 13.8 %collective-permute-start.36 = (f16[1024,128]{1,0:T(8,128)(2,1)}, f16[1024,128]{1,0:T(8,128)(2,1)S(1)}, u32[]{:S(2)}, u32[]{:S(2)}) collective-permute-start(f16[1024,128]{1,0:T(8,128)(2,1)} %get-tuple-element.138), channel_id=1, source_target_pairs={{0,96},{8,104},{16,112},{24,120},{32,0},{40,8},{48,16},{56,24},{64... | collective-permute-start | bytes 786440 | tf_op jit(solution)/shard_map/ppermute | solution.py:410
  229.4 8.9 %collective-permute-start.37 = (f16[1024,128]{1,0:T(8,128)(2,1)}, f16[1024,128]{1,0:T(8,128)(2,1)S(1)}, u32[]{:S(2)}, u32[]{:S(2)}) collective-permute-start(f16[1024,128]{1,0:T(8,128)(2,1)} %get-tuple-element.139), channel_id=1, source_target_pairs={{0,64},{8,72},{16,80},{24,88},{32,96},{40,104},{48,112},{56,120},{... | collective-permute-start | bytes 786440 | tf_op jit(solution)/shard_map/ppermute | solution.py:410
  (27 other events, 204.8 us)

commit v2 on v1

--- a/solution.py
+++ b/solution.py
@@ -136,7 +136,7 @@
 
 
 def y_kernel(count, targets, cols, blocks, sketch, *rest):
-    outs, stat, scratch = rest[:3], rest[3], rest[4:]
+    outs, stat, scratch = rest[:2], rest[2], rest[3:]
     total_sum, order, bounds, block_buf, sketch_buf, sems, out_sems = scratch
 
     def copies(j):
@@ -180,7 +180,7 @@
     stat[4:] = jnp.full((4, K), jnp.max(largest_block.astype(f32)))
 
 
-Y_PARTS = (32, 16, 16)
+Y_PARTS = (32, 32)
 Z_PARTS = (16, 16, 8, 8, 4, 4, 4, 4)
 
 
@@ -206,7 +206,7 @@
         out_shape=sums_of(Y_PARTS) + (jax.ShapeDtypeStruct((8, K), f32),),
         in_specs=[pl.BlockSpec(memory_space=pltpu.SMEM)] * 3
         + [pl.BlockSpec(memory_space=pl.ANY)] * 2,
-        out_specs=(pl.BlockSpec(memory_space=pl.ANY),) * 3
+        out_specs=(pl.BlockSpec(memory_space=pl.ANY),) * 2
         + (pl.BlockSpec(memory_space=pltpu.VMEM),),
         scratch_shapes=scratch_for(1, Y_PARTS, jnp.bfloat16),
         compiler_params=pltpu.CompilerParams(vmem_limit_bytes=VMEM_BYTES),
@@ -450,9 +450,10 @@
     entries = jnp.maximum(own_stat, other_stat) * count[0].astype(f32)
     bounds, _ = lax.optimization_barrier((jnp.where(in_first, first_bound, entries), first))
     bounds, below, above = ring_fold(bounds, send_y, jnp.maximum)
-    later, _ = lax.optimization_barrier(((own[1:], from_pair[1:]), bounds))
+    later, _ = lax.optimization_barrier(((own[1], from_pair[1]), bounds))
     parts = [
-        [mine[at : at + HALF] + pair[at : at + HALF] for at in (0, HALF)] for mine, pair in zip(*later)
+        [later[0][at : at + HALF] + later[1][at : at + HALF] for at in (start, start + HALF)]
+        for start in (0, 2 * HALF)
     ]
     passing, staying = lax.optimization_barrier(parts)
     around = scales_for(below[:1]), scales_for(above[:1])
@@ -501,6 +502,7 @@
         ring_second(r, values[2:4], send, z_scales, *around)
         for r, (values, send, _) in zip(received, rings)
     ]
+    lower_factor = after(lower_factor, seconds[0][2][1])
     inverse = lax.linalg.triangular_solve(
         lower_factor, jnp.eye(K, dtype=f32), left_side=True, lower=True
     )

time: 244 us -> 248 us (1.016)
  starting transfers between devices: 50.8 us -> 55.8 us
  other arithmetic: 59.6 us -> 64.6 us
  waiting for transfers between devices: 31.7 us -> 27 us
  Pallas kernels: 44.5 us -> 41.4 us
  blocking collectives: 42.7 us -> 40 us
    ppermute x13, starting transfers between devices: 20.1 us -> 27.7 us  [send_z(): return lax.ppermute(value, 'row', along_z(shift))]
    ppermute x13, starting transfers between devices: 20.3 us -> 16.4 us  [send_x(): return lax.ppermute(value, 'row', along_x(shift))]
    convert_element_type x15, other arithmetic: 24.9 us -> 28.6 us  [pack(): return by_rows((value * scales[1]).astype(f16))]
    ppermute x13, waiting for transfers between devices: 4.66 us -> 1.36 us  [send_z(): return lax.ppermute(value, 'row', along_z(shift))]
    all_gather x1, blocking collectives: 42.7 us -> 40 us  [body(): gathered = lax.all_gather(mine, 'col', axis=0, tiled=True)]
  transfers between devices with their start and end apart: 38 -> 37, of which waited for: 10 -> 11; matrix products, arithmetic and copies ran while one was open for 24% -> 26% of each run, Pallas kernels for 13% -> 12%
where the time goes in v2:
time: 248 us; the launch traced here: 243 us
  other arithmetic  64.6 us (26%)
  starting transfers between devices  55.8 us (22%)
  Pallas kernels  41.4 us (17%)
  blocking collectives  40 us (16%)
  waiting for transfers between devices  27 us (11%)
  matrix products  7.38 us (3%)
  between operations  4.51 us (2%)
  local copies, waits for them, and re-layouts  2.58 us (1%)
    all_gather x1, blocking collectives, body(): gathered = lax.all_gather(mine, 'col', axis=0, tiled=True)  40 us
    convert_element_type x15, other arithmetic, pack(): return by_rows((value * scales[1]).astype(f16))  28.6 us
    ppermute x13, starting transfers between devices, send_z(): return lax.ppermute(value, 'row', along_z(shift))  27.7 us
    pallas_call x2, Pallas kernels, partial_rows(): pl.pallas_call(y_kernel, out_shape=sums_of(Y_PARTS) + (jax.ShapeDtypeStru...  23.1 us
    ppermute x7, waiting for transfers between devices, send_y(): return lax.ppermute(value, 'col', ring(shift))  19 us
    pallas_call x1, Pallas kernels, partial_cols(): pl.pallas_call(z_kernel, out_shape=sums_of(Z_PARTS * 2), in_specs=[pl.Blo...  16.5 us
    ppermute x13, starting transfers between devices, send_x(): return lax.ppermute(value, 'row', along_x(shift))  16.4 us
    another operation x3, other arithmetic, body(): lower_factor = jnp.linalg.cholesky(gram)  12.4 us
  transfers between devices with their start and end apart: 37, of which 11 were waited for; matrix products, arithmetic and copies ran while one was open for 26% of the time, Pallas kernels for 12%

profile of v2, /device:TPU:24, one launch (start us, length us, event | category | flops | bytes accessed | tf_op | source)
XLA Modules:
  0.0 243.3 jit_solution(1549002363460187771)
XLA Ops:
  3.7 10.9 %partial_rows.3 = (f32[32,256,128]{2,1,0:T(8,128)}, f32[32,256,128]{2,1,0:T(8,128)}, f32[8,128]{1,0:T(8,128)}) custom-call(s32[1]{0:T(128)} %bitcast.146.count, s32[96]{0:T(128)} %and_select_fusion.targets, s32[96]{0:T(128)} %bitcast.182, bf16[96,256,256]{2,1,0:T(8,128)(2,1)} %bitcast.152, bf16[128,256,128]{2,1,0:T(8,128)(2,1)} %bitcast.155), custom_call_target="tpu_custom_call" | custom-call | flops 805306368 | bytes 62914560 | tf_op jit(solution)/shard_map/partial_rows/pallas_call | solution.py:204
  17.1 12.2 %partial_rows.2 = (f32[32,256,128]{2,1,0:T(8,128)}, f32[32,256,128]{2,1,0:T(8,128)}, f32[8,128]{1,0:T(8,128)}) custom-call(s32[1]{0:T(128)} %bitcast.145.count, s32[96]{0:T(128)} %get-tuple-element.122.targets, s32[96]{0:T(128)} %bitcast.183, bf16[96,256,256]{2,1,0:T(8,128)(2,1)} %bitcast.153, bf16[128,256,128]{2,1,0:T(8,128)(2,1)} %bitcast.156), custom_call_target="tpu_custom_call" | custom-call | flops 805306368 | bytes 62914560 | tf_op jit(solution)/shard_map/partial_rows/pallas_call | solution.py:204
  30.1 4.5 %fusion.1 = (f16[16,256,128]{2,1,0:T(8,128)(2,1)S(1)}, f16[16,256,128]{2,1,0:T(8,128)(2,1)S(1)}) fusion(f32[32,256,128]{2,1,0:T(8,128)} %collective-permute-done.2, f32[32,256,128]{2,1,0:T(8,128)} %get-tuple-element.63, f32[]{:T(128)S(1)} %bitcast.192), kind=kLoop, calls=%fused_computation.4 | loop fusion | flops 3145728 | bytes 10485764 | tf_op jit(solution)/shard_map/convert_element_type | solution.py:331
  35.4 3.1 %collective-permute-start.4 = (f32[8,128]{1,0:T(8,128)S(1)}, f32[8,128]{1,0:T(8,128)S(1)}, u32[]{:S(2)}, u32[]{:S(2)}) collective-permute-start(f32[8,128]{1,0:T(8,128)S(1)} %get-tuple-element.65), channel_id=1, source_target_pairs={{0,2},{1,3},{2,4},{3,5},{4,6},{5,7},{6,0},{7,1},{8,10},{9,11},{10,... | collective-permute-start | bytes 12296 | tf_op jit(solution)/shard_map/ppermute | solution.py:407
  39.8 2.6 %collective-permute-start.6 = (f16[4096,128]{1,0:T(8,128)(2,1)S(1)}, f16[4096,128]{1,0:T(8,128)(2,1)S(1)}, u32[]{:S(2)}, u32[]{:S(2)}) collective-permute-start(f16[4096,128]{1,0:T(8,128)(2,1)S(1)} %bitcast.158), channel_id=1, source_target_pairs={{0,2},{1,3},{2,4},{3,5},{4,6},{5,7},{6,0},{7,1},{8,10},{9,11},{10,... | collective-permute-start | bytes 3145736 | tf_op jit(solution)/shard_map/ppermute | solution.py:407
  43.3 2.8 %slice_add_fusion.2 = (f32[2048,128]{1,0:T(8,128)S(1)}, f32[2048,128]{1,0:T(8,128)S(1)}, f32[2048,128]{1,0:T(8,128)S(1)}, f32[2048,128]{1,0:T(8,128)S(1)}) fusion(f32[8192,128]{1,0:T(8,128)} %bitcast.7, f32[8192,128]{1,0:T(8,128)S(1)} %bitcast.157), kind=kLoop, calls=%fused_computation.35 | loop fusion | flops 1048576 | bytes 12582912 | tf_op jit(solution)/shard_map/add | solution.py:455
  46.4 3.2 %collective-permute-start.13 = (f32[8,128]{1,0:T(8,128)S(1)}, f32[8,128]{1,0:T(8,128)S(1)}, u32[]{:S(2)}, u32[]{:S(2)}) collective-permute-start(f32[8,128]{1,0:T(8,128)S(1)} %max.84), channel_id=1, source_target_pairs={{0,96},{8,104},{16,112},{24,120},{32,0},{40,8},{48,16},{56,24},{64... | collective-permute-start | bytes 12296 | tf_op jit(solution)/shard_map/ppermute | solution.py:410
  51.4 6.3 %collective-permute-start.14 = (f32[8,128]{1,0:T(8,128)S(1)}, f32[8,128]{1,0:T(8,128)S(1)}, u32[]{:S(2)}, u32[]{:S(2)}) collective-permute-start(f32[8,128]{1,0:T(8,128)S(1)} %maximum_maximum_fusion.1), channel_id=1, source_target_pairs={{0,16},{8,24},{16,0},{24,8},{32,48},{40,56},{48,32},{56,40},{64,80... | collective-permute-start | bytes 12296 | tf_op jit(solution)/shard_map/ppermute | solution.py:413
  57.7 3.2 %collective-permute-start.16 = (f32[8,128]{1,0:T(8,128)S(1)}, f32[8,128]{1,0:T(8,128)S(1)}, u32[]{:S(2)}, u32[]{:S(2)}) collective-permute-start(f32[8,128]{1,0:T(8,128)S(1)} %maximum_maximum_fusion.1), channel_id=1, source_target_pairs={{0,24},{8,0},{16,8},{24,16},{32,56},{40,32},{48,40},{56,48},{64,88... | collective-permute-start | bytes 12296 | tf_op jit(solution)/shard_map/ppermute | solution.py:413
  60.9 4.2 %collective-permute-done.7 = f16[4096,128]{1,0:T(8,128)(2,1)S(1)} collective-permute-done((f16[4096,128]{1,0:T(8,128)(2,1)S(1)}, f16[4096,128]{1,0:T(8,128)(2,1)S(1)}, u32[]{:S(2)}, u32[]{:S(2)}) %collective-permute-start.7) | collective-permute-done | bytes 1048608 | tf_op jit(solution)/shard_map/ppermute | solution.py:407
  65.6 2.7 %collective-permute-start.8 = (f16[2048,128]{1,0:T(8,128)(2,1)S(1)}, f16[2048,128]{1,0:T(8,128)(2,1)S(1)}, u32[]{:S(2)}, u32[]{:S(2)}) collective-permute-start(f16[2048,128]{1,0:T(8,128)(2,1)S(1)} %multiply_convert_fusion.5), channel_id=1, source_target_pairs={{0,2},{1,3},{2,4},{3,5},{4,6},{5,7},{6,0},{7,1},{8,10},{9,11},{10,... | collective-permute-start | bytes 1572872 | tf_op jit(solution)/shard_map/ppermute | solution.py:407
  68.4 9.9 %collective-permute-done.8 = f16[2048,128]{1,0:T(8,128)(2,1)S(1)} collective-permute-done((f16[2048,128]{1,0:T(8,128)(2,1)S(1)}, f16[2048,128]{1,0:T(8,128)(2,1)S(1)}, u32[]{:S(2)}, u32[]{:S(2)}) %collective-permute-start.8) | collective-permute-done | bytes 524320 | tf_op jit(solution)/shard_map/ppermute | solution.py:407
  78.3 3.2 %collective-permute-done.9 = f16[2048,128]{1,0:T(8,128)(2,1)S(1)} collective-permute-done((f16[2048,128]{1,0:T(8,128)(2,1)S(1)}, f16[2048,128]{1,0:T(8,128)(2,1)S(1)}, u32[]{:S(2)}, u32[]{:S(2)}) %collective-permute-start.9) | collective-permute-done | bytes 524320 | tf_op jit(solution)/shard_map/ppermute | solution.py:407
  82.6 2.4 abs_reduce_fusion.1
  87.6 40.0 %all-gather.1.gathered.table = s16[35072,128]{1,0:T(8,128)(2,1)} all-gather(s16[4384,128]{1,0:T(8,128)(2,1)S(1)} %pad_add_fusion), channel_id=1, replica_groups=mesh['row'=16,'col'=8] {'col'}, dimensions={0}, use_global_device_ids=true | all-gather | bytes 10100736 | tf_op jit(solution)/shard_map/all_gather | solution.py:487
  129.6 3.2 %collective-permute-start.19 = (f32[128,128]{1,0:T(8,128)}, f32[128,128]{1,0:T(8,128)S(1)}, u32[]{:S(2)}, u32[]{:S(2)}) collective-permute-start(f32[128,128]{1,0:T(8,128)} %get-tuple-element.83), channel_id=1, source_target_pairs={{0,96},{8,104},{16,112},{24,120},{32,0},{40,8},{48,16},{56,24},{64... | collective-permute-start | bytes 196616 | tf_op jit(solution)/shard_map/ppermute | solution.py:410
  132.9 16.5 %partial_cols.1 = (f32[16,256,128]{2,1,0:T(8,128)}, f32[16,256,128]{2,1,0:T(8,128)}, f32[8,256,128]{2,1,0:T(8,128)}, f32[8,256,128]{2,1,0:T(8,128)}, f32[4,256,1...) custom-call(s32[1]{0:T(128)} %bitcast.147.count, ...), custom_call_target="tpu_custom_call" | custom-call | flops 3221225472 | bytes 44040192 | tf_op jit(solution)/shard_map/partial_cols/pallas_call | solution.py:304
  149.4 3.0 %multiply_convert_fusion.2 = f16[16,256,128]{2,1,0:T(8,128)(2,1)} fusion(f32[16,256,128]{2,1,0:T(8,128)} %get-tuple-element.87, f32[]{:T(128)S(1)} %bitcast.161), kind=kLoop, calls=%fused_computation.11 | loop fusion | flops 1048576 | bytes 3145732 | tf_op jit(solution)/shard_map/convert_element_type | solution.py:331
  152.4 7.5 %collective-permute-start.20 = (f32[128,128]{1,0:T(8,128)S(1)}, f32[128,128]{1,0:T(8,128)S(1)}, u32[]{:S(2)}, u32[]{:S(2)}) collective-permute-start(f32[128,128]{1,0:T(8,128)S(1)} %add_add_fusion.1), channel_id=1, source_target_pairs={{0,16},{8,24},{16,0},{24,8},{32,48},{40,56},{48,32},{56,40},{64,80... | collective-permute-start | bytes 196616 | tf_op jit(solution)/shard_map/ppermute | solution.py:413
  159.9 3.2 %collective-permute-start.22 = (f32[128,128]{1,0:T(8,128)S(1)}, f32[128,128]{1,0:T(8,128)S(1)}, u32[]{:S(2)}, u32[]{:S(2)}) collective-permute-start(f32[128,128]{1,0:T(8,128)S(1)} %add_add_fusion.1), channel_id=1, source_target_pairs={{0,24},{8,0},{16,8},{24,16},{32,56},{40,32},{48,40},{56,48},{64,88... | collective-permute-start | bytes 196616 | tf_op jit(solution)/shard_map/ppermute | solution.py:413
  167.6 3.0 %multiply_convert_fusion = f16[16,256,128]{2,1,0:T(8,128)(2,1)} fusion(f32[16,256,128]{2,1,0:T(8,128)} %get-tuple-element.104, f32[]{:T(128)S(6)} %add.248), kind=kLoop, calls=%fused_computation.9 | loop fusion | flops 1048576 | bytes 3145732 | tf_op jit(solution)/shard_map/convert_element_type | solution.py:331
  170.6 2.3 collective-permute-start.31
  174.1 11.7 %cholesky.17 = f32[128,128]{1,0:T(8,128)S(1)} custom-call(f32[128,128]{1,0:T(8,128)S(1)} %fusion.44), custom_call_target="Cholesky" | custom-call | tf_op jit(solution)/shard_map/jit(cholesky)/cholesky | solution.py:500
  191.6 2.9 %collective-permute-start.26 = (f16[2048,128]{1,0:T(8,128)(2,1)S(1)}, f16[2048,128]{1,0:T(8,128)(2,1)S(1)}, u32[]{:S(2)}, u32[]{:S(2)}) collective-permute-start(f16[2048,128]{1,0:T(8,128)(2,1)S(1)} %fusion.12), channel_id=1, source_target_pairs={{0,96},{8,104},{16,112},{24,120},{32,0},{40,8},{48,16},{56,24},{64... | collective-permute-start | bytes 1572872 | tf_op jit(solution)/shard_map/ppermute | solution.py:410
  194.5 2.3 fusion.8
  199.2 3.2 %collective-permute-start.33 = (f16[2048,128]{1,0:T(8,128)(2,1)}, f16[2048,128]{1,0:T(8,128)(2,1)}, u32[]{:S(2)}, u32[]{:S(2)}) collective-permute-start(f16[2048,128]{1,0:T(8,128)(2,1)} %fusion.8), channel_id=1, source_target_pairs={{0,24},{8,0},{16,8},{24,16},{32,56},{40,32},{48,40},{56,48},{64,88... | collective-permute-start | bytes 1572872 | tf_op jit(solution)/shard_map/ppermute | solution.py:413
  204.2 2.2 fusion.34
  212.2 10.4 %custom-call.6 = f32[1,128,128]{1,2,0:T(8,128)} custom-call(f32[1,128,128]{2,1,0:T(8,128)S(1)} %select_bitcast_fusion), custom_call_target="InvertDiagBlocksLowerTriangular" | custom-call | tf_op jit(solution)/shard_map/triangular_solve | solution.py:506
  223.7 2.1 fusion.24
  226.3 2.5 %fusion.21 = (f16[1024,128]{1,0:T(8,128)(2,1)}, f16[1024,128]{1,0:T(8,128)(2,1)}) fusion(f32[4,256,128]{2,1,0:T(8,128)} %get-tuple-element.112, f16[2048,128]{1,0:T(8,128)(2,1)} %collective-permute-done.33, f16[4096,128]{1,0:T(8,128)(2,1)S(1)} %collective-permute-done.30, f32[]{:T(128)S(1)} %bitcast.171, f32[]{:T(128)S(1)} %bitcast.179, ...), kind=kLoop, calls=%fused_computation.47 | loop fusion | flops 2097152 | bytes 2621448 | tf_op jit(solution)/shard_map/convert_element_type | solution.py:331
  228.8 2.8 %collective-permute-start.35 = (f16[1024,128]{1,0:T(8,128)(2,1)}, f16[1024,128]{1,0:T(8,128)(2,1)}, u32[]{:S(2)}, u32[]{:S(2)}) collective-permute-start(f16[1024,128]{1,0:T(8,128)(2,1)} %get-tuple-element.132), channel_id=1, source_target_pairs={{0,96},{8,104},{16,112},{24,120},{32,0},{40,8},{48,16},{56,24},{64... | collective-permute-start | bytes 786440 | tf_op jit(solution)/shard_map/ppermute | solution.py:410
  236.3 2.3 convolution_multiply_fusion
  (137 shorter events, 46.4 us)
Async XLA Ops:
  14.6 15.5 %collective-permute-start.2 = (f32[32,256,128]{2,1,0:T(8,128)}, f32[32,256,128]{2,1,0:T(8,128)}, u32[]{:S(2)}, u32[]{:S(2)}) collective-permute-start(f32[32,256,128]{2,1,0:T(8,128)} %get-tuple-element.64), channel_id=1, source_target_pairs={{0,1},{1,0},{2,3},{3,2},{4,5},{5,4},{6,7},{7,6},{8,9},{9,8},{10,11... | collective-permute-start | bytes 12582920 | tf_op jit(solution)/shard_map/ppermute | solution.py:404
  16.6 26.8 %collective-permute-start = (f32[32,256,128]{2,1,0:T(8,128)}, f32[32,256,128]{2,1,0:T(8,128)}, u32[]{:S(2)}, u32[]{:S(2)}) collective-permute-start(f32[32,256,128]{2,1,0:T(8,128)} %get-tuple-element.60), channel_id=1, source_target_pairs={{0,1},{1,0},{2,3},{3,2},{4,5},{5,4},{6,7},{7,6},{8,9},{9,8},{10,11... | collective-permute-start | bytes 12582920 | tf_op jit(solution)/shard_map/ppermute | solution.py:404
  16.7 12.6 %collective-permute-start.1 = (f32[8,128]{1,0:T(8,128)}, f32[8,128]{1,0:T(8,128)S(1)}, u32[]{:S(2)}, u32[]{:S(2)}) collective-permute-start(f32[8,128]{1,0:T(8,128)} %get-tuple-element.62), channel_id=1, source_target_pairs={{0,1},{1,0},{2,3},{3,2},{4,5},{5,4},{6,7},{7,6},{8,9},{9,8},{10,11... | collective-permute-start | bytes 12296 | tf_op jit(solution)/shard_map/ppermute | solution.py:404
  34.6 5.2 %collective-permute-start.3 = (f32[8,128]{1,0:T(8,128)S(1)}, f32[8,128]{1,0:T(8,128)S(1)}, u32[]{:S(2)}, u32[]{:S(2)}) collective-permute-start(f32[8,128]{1,0:T(8,128)S(1)} %get-tuple-element.65), channel_id=1, source_target_pairs={{0,4},{1,5},{2,6},{3,7},{4,0},{5,1},{6,2},{7,3},{8,12},{9,13},{10,... | collective-permute-start | bytes 12296 | tf_op jit(solution)/shard_map/ppermute | solution.py:407
  35.4 7.0 %collective-permute-start.4 = (f32[8,128]{1,0:T(8,128)S(1)}, f32[8,128]{1,0:T(8,128)S(1)}, u32[]{:S(2)}, u32[]{:S(2)}) collective-permute-start(f32[8,128]{1,0:T(8,128)S(1)} %get-tuple-element.65), channel_id=1, source_target_pairs={{0,2},{1,3},{2,4},{3,5},{4,6},{5,7},{6,0},{7,1},{8,10},{9,11},{10,... | collective-permute-start | bytes 12296 | tf_op jit(solution)/shard_map/ppermute | solution.py:407
  39.1 26.0 %collective-permute-start.7 = (f16[4096,128]{1,0:T(8,128)(2,1)S(1)}, f16[4096,128]{1,0:T(8,128)(2,1)S(1)}, u32[]{:S(2)}, u32[]{:S(2)}) collective-permute-start(f16[4096,128]{1,0:T(8,128)(2,1)S(1)} %bitcast.159), channel_id=1, source_target_pairs={{0,6},{1,7},{2,0},{3,1},{4,2},{5,3},{6,4},{7,5},{8,14},{9,15},{10,... | collective-permute-start | bytes 3145736 | tf_op jit(solution)/shard_map/ppermute | solution.py:407
  39.8 25.5 %collective-permute-start.6 = (f16[4096,128]{1,0:T(8,128)(2,1)S(1)}, f16[4096,128]{1,0:T(8,128)(2,1)S(1)}, u32[]{:S(2)}, u32[]{:S(2)}) collective-permute-start(f16[4096,128]{1,0:T(8,128)(2,1)S(1)} %bitcast.158), channel_id=1, source_target_pairs={{0,2},{1,3},{2,4},{3,5},{4,6},{5,7},{6,0},{7,1},{8,10},{9,11},{10,... | collective-permute-start | bytes 3145736 | tf_op jit(solution)/shard_map/ppermute | solution.py:407
  51.4 16.9 %collective-permute-start.14 = (f32[8,128]{1,0:T(8,128)S(1)}, f32[8,128]{1,0:T(8,128)S(1)}, u32[]{:S(2)}, u32[]{:S(2)}) collective-permute-start(f32[8,128]{1,0:T(8,128)S(1)} %maximum_maximum_fusion.1), channel_id=1, source_target_pairs={{0,16},{8,24},{16,0},{24,8},{32,48},{40,56},{48,32},{56,40},{64,80... | collective-permute-start | bytes 12296 | tf_op jit(solution)/shard_map/ppermute | solution.py:413
  57.7 10.6 %collective-permute-start.15 = (f32[8,128]{1,0:T(8,128)S(1)}, f32[8,128]{1,0:T(8,128)S(1)}, u32[]{:S(2)}, u32[]{:S(2)}) collective-permute-start(f32[8,128]{1,0:T(8,128)S(1)} %maximum_maximum_fusion.1), channel_id=1, source_target_pairs={{0,8},{8,16},{16,24},{24,0},{32,40},{40,48},{48,56},{56,32},{64,72... | collective-permute-start | bytes 12296 | tf_op jit(solution)/shard_map/ppermute | solution.py:413
  57.7 10.6 %collective-permute-start.16 = (f32[8,128]{1,0:T(8,128)S(1)}, f32[8,128]{1,0:T(8,128)S(1)}, u32[]{:S(2)}, u32[]{:S(2)}) collective-permute-start(f32[8,128]{1,0:T(8,128)S(1)} %maximum_maximum_fusion.1), channel_id=1, source_target_pairs={{0,24},{8,0},{16,8},{24,16},{32,56},{40,32},{48,40},{56,48},{64,88... | collective-permute-start | bytes 12296 | tf_op jit(solution)/shard_map/ppermute | solution.py:413
  65.6 12.7 %collective-permute-start.8 = (f16[2048,128]{1,0:T(8,128)(2,1)S(1)}, f16[2048,128]{1,0:T(8,128)(2,1)S(1)}, u32[]{:S(2)}, u32[]{:S(2)}) collective-permute-start(f16[2048,128]{1,0:T(8,128)(2,1)S(1)} %multiply_convert_fusion.5), channel_id=1, source_target_pairs={{0,2},{1,3},{2,4},{3,5},{4,6},{5,7},{6,0},{7,1},{8,10},{9,11},{10,... | collective-permute-start | bytes 1572872 | tf_op jit(solution)/shard_map/ppermute | solution.py:407
  68.3 13.2 %collective-permute-start.9 = (f16[2048,128]{1,0:T(8,128)(2,1)S(1)}, f16[2048,128]{1,0:T(8,128)(2,1)S(1)}, u32[]{:S(2)}, u32[]{:S(2)}) collective-permute-start(f16[2048,128]{1,0:T(8,128)(2,1)S(1)} %multiply_convert_fusion.4), channel_id=1, source_target_pairs={{0,6},{1,7},{2,0},{3,1},{4,2},{5,3},{6,4},{7,5},{8,14},{9,15},{10,... | collective-permute-start | bytes 1572872 | tf_op jit(solution)/shard_map/ppermute | solution.py:407
  129.4 22.9 %collective-permute-start.17 = (f32[128,128]{1,0:T(8,128)}, f32[128,128]{1,0:T(8,128)S(1)}, u32[]{:S(2)}, u32[]{:S(2)}) collective-permute-start(f32[128,128]{1,0:T(8,128)} %get-tuple-element.83), channel_id=1, source_target_pairs={{0,64},{8,72},{16,80},{24,88},{32,96},{40,104},{48,112},{56,120},{... | collective-permute-start | bytes 196616 | tf_op jit(solution)/shard_map/ppermute | solution.py:410
  129.5 22.9 %collective-permute-start.18 = (f32[128,128]{1,0:T(8,128)}, f32[128,128]{1,0:T(8,128)S(1)}, u32[]{:S(2)}, u32[]{:S(2)}) collective-permute-start(f32[128,128]{1,0:T(8,128)} %get-tuple-element.83), channel_id=1, source_target_pairs={{0,32},{8,40},{16,48},{24,56},{32,64},{40,72},{48,80},{56,88},{64,... | collective-permute-start | bytes 196616 | tf_op jit(solution)/shard_map/ppermute | solution.py:410
  129.6 22.8 %collective-permute-start.19 = (f32[128,128]{1,0:T(8,128)}, f32[128,128]{1,0:T(8,128)S(1)}, u32[]{:S(2)}, u32[]{:S(2)}) collective-permute-start(f32[128,128]{1,0:T(8,128)} %get-tuple-element.83), channel_id=1, source_target_pairs={{0,96},{8,104},{16,112},{24,120},{32,0},{40,8},{48,16},{56,24},{64... | collective-permute-start | bytes 196616 | tf_op jit(solution)/shard_map/ppermute | solution.py:410
  152.4 34.1 %collective-permute-start.24 = (f16[4096,128]{1,0:T(8,128)(2,1)}, f16[4096,128]{1,0:T(8,128)(2,1)}, u32[]{:S(2)}, u32[]{:S(2)}) collective-permute-start(f16[4096,128]{1,0:T(8,128)(2,1)} %bitcast.19), channel_id=1, source_target_pairs={{0,96},{8,104},{16,112},{24,120},{32,0},{40,8},{48,16},{56,24},{64... | collective-permute-start | bytes 3145736 | tf_op jit(solution)/shard_map/ppermute | solution.py:410
  152.4 13.9 %collective-permute-start.20 = (f32[128,128]{1,0:T(8,128)S(1)}, f32[128,128]{1,0:T(8,128)S(1)}, u32[]{:S(2)}, u32[]{:S(2)}) collective-permute-start(f32[128,128]{1,0:T(8,128)S(1)} %add_add_fusion.1), channel_id=1, source_target_pairs={{0,16},{8,24},{16,0},{24,8},{32,48},{40,56},{48,32},{56,40},{64,80... | collective-permute-start | bytes 196616 | tf_op jit(solution)/shard_map/ppermute | solution.py:413
  159.9 6.4 %collective-permute-start.21 = (f32[128,128]{1,0:T(8,128)S(1)}, f32[128,128]{1,0:T(8,128)S(1)}, u32[]{:S(2)}, u32[]{:S(2)}) collective-permute-start(f32[128,128]{1,0:T(8,128)S(1)} %add_add_fusion.1), channel_id=1, source_target_pairs={{0,8},{8,16},{16,24},{24,0},{32,40},{40,48},{48,56},{56,32},{64,72... | collective-permute-start | bytes 196616 | tf_op jit(solution)/shard_map/ppermute | solution.py:413
  159.9 6.4 %collective-permute-start.22 = (f32[128,128]{1,0:T(8,128)S(1)}, f32[128,128]{1,0:T(8,128)S(1)}, u32[]{:S(2)}, u32[]{:S(2)}) collective-permute-start(f32[128,128]{1,0:T(8,128)S(1)} %add_add_fusion.1), channel_id=1, source_target_pairs={{0,24},{8,0},{16,8},{24,16},{32,56},{40,32},{48,40},{56,48},{64,88... | collective-permute-start | bytes 196616 | tf_op jit(solution)/shard_map/ppermute | solution.py:413
  164.4 25.3 %collective-permute-start.23 = (f16[4096,128]{1,0:T(8,128)(2,1)}, f16[4096,128]{1,0:T(8,128)(2,1)}, u32[]{:S(2)}, u32[]{:S(2)}) collective-permute-start(f16[4096,128]{1,0:T(8,128)(2,1)} %bitcast.18), channel_id=1, source_target_pairs={{0,32},{8,40},{16,48},{24,56},{32,64},{40,72},{48,80},{56,88},{64,... | collective-permute-start | bytes 3145736 | tf_op jit(solution)/shard_map/ppermute | solution.py:410
  170.6 24.0 %collective-permute-start.31 = (f16[4096,128]{1,0:T(8,128)(2,1)}, f16[4096,128]{1,0:T(8,128)(2,1)}, u32[]{:S(2)}, u32[]{:S(2)}) collective-permute-start(f16[4096,128]{1,0:T(8,128)(2,1)} %bitcast.33), channel_id=1, source_target_pairs={{0,24},{8,0},{16,8},{24,16},{32,56},{40,32},{48,40},{56,48},{64,88... | collective-permute-start | bytes 3145736 | tf_op jit(solution)/shard_map/ppermute | solution.py:413
  174.1 24.1 %collective-permute-start.30 = (f16[4096,128]{1,0:T(8,128)(2,1)}, f16[4096,128]{1,0:T(8,128)(2,1)S(1)}, u32[]{:S(2)}, u32[]{:S(2)}) collective-permute-start(f16[4096,128]{1,0:T(8,128)(2,1)} %bitcast.32), channel_id=1, source_target_pairs={{0,8},{8,16},{16,24},{24,0},{32,40},{40,48},{48,56},{56,32},{64,72... | collective-permute-start | bytes 3145736 | tf_op jit(solution)/shard_map/ppermute | solution.py:413
  191.2 12.9 %collective-permute-start.25 = (f16[2048,128]{1,0:T(8,128)(2,1)S(1)}, f16[2048,128]{1,0:T(8,128)(2,1)S(1)}, u32[]{:S(2)}, u32[]{:S(2)}) collective-permute-start(f16[2048,128]{1,0:T(8,128)(2,1)S(1)} %fusion.14), channel_id=1, source_target_pairs={{0,32},{8,40},{16,48},{24,56},{32,64},{40,72},{48,80},{56,88},{64,... | collective-permute-start | bytes 1572872 | tf_op jit(solution)/shard_map/ppermute | solution.py:410
  191.6 12.5 %collective-permute-start.26 = (f16[2048,128]{1,0:T(8,128)(2,1)S(1)}, f16[2048,128]{1,0:T(8,128)(2,1)S(1)}, u32[]{:S(2)}, u32[]{:S(2)}) collective-permute-start(f16[2048,128]{1,0:T(8,128)(2,1)S(1)} %fusion.12), channel_id=1, source_target_pairs={{0,96},{8,104},{16,112},{24,120},{32,0},{40,8},{48,16},{56,24},{64... | collective-permute-start | bytes 1572872 | tf_op jit(solution)/shard_map/ppermute | solution.py:410
  199.2 24.6 %collective-permute-start.32 = (f16[2048,128]{1,0:T(8,128)(2,1)}, f16[2048,128]{1,0:T(8,128)(2,1)}, u32[]{:S(2)}, u32[]{:S(2)}) collective-permute-start(f16[2048,128]{1,0:T(8,128)(2,1)} %fusion.10), channel_id=1, source_target_pairs={{0,8},{8,16},{16,24},{24,0},{32,40},{40,48},{48,56},{56,32},{64,72... | collective-permute-start | bytes 1572872 | tf_op jit(solution)/shard_map/ppermute | solution.py:413
  199.2 24.6 %collective-permute-start.33 = (f16[2048,128]{1,0:T(8,128)(2,1)}, f16[2048,128]{1,0:T(8,128)(2,1)}, u32[]{:S(2)}, u32[]{:S(2)}) collective-permute-start(f16[2048,128]{1,0:T(8,128)(2,1)} %fusion.8), channel_id=1, source_target_pairs={{0,24},{8,0},{16,8},{24,16},{32,56},{40,32},{48,40},{56,48},{64,88... | collective-permute-start | bytes 1572872 | tf_op jit(solution)/shard_map/ppermute | solution.py:413
  206.4 28.2 %collective-permute-start.28 = (f16[1024,128]{1,0:T(8,128)(2,1)}, f16[1024,128]{1,0:T(8,128)(2,1)}, u32[]{:S(2)}, u32[]{:S(2)}) collective-permute-start(f16[1024,128]{1,0:T(8,128)(2,1)} %get-tuple-element.130), channel_id=1, source_target_pairs={{0,24},{8,0},{16,8},{24,16},{32,56},{40,32},{48,40},{56,48},{64,88... | collective-permute-start | bytes 786440 | tf_op jit(solution)/shard_map/ppermute | solution.py:413
  207.5 27.0 %collective-permute-start.29 = (f16[1024,128]{1,0:T(8,128)(2,1)S(1)}, f16[1024,128]{1,0:T(8,128)(2,1)}, u32[]{:S(2)}, u32[]{:S(2)}) collective-permute-start(f16[1024,128]{1,0:T(8,128)(2,1)S(1)} %get-tuple-element.131), channel_id=1, source_target_pairs={{0,16},{8,24},{16,0},{24,8},{32,48},{40,56},{48,32},{56,40},{64,80... | collective-permute-start | bytes 786440 | tf_op jit(solution)/shard_map/ppermute | solution.py:413
  209.7 21.9 %collective-permute-start.27 = (f16[1024,128]{1,0:T(8,128)(2,1)}, f16[1024,128]{1,0:T(8,128)(2,1)}, u32[]{:S(2)}, u32[]{:S(2)}) collective-permute-start(f16[1024,128]{1,0:T(8,128)(2,1)} %fusion.41), channel_id=1, source_target_pairs={{0,8},{8,16},{16,24},{24,0},{32,40},{40,48},{48,56},{56,32},{64,72... | collective-permute-start | bytes 786440 | tf_op jit(solution)/shard_map/ppermute | solution.py:413
  225.8 12.8 %collective-permute-start.34 = (f16[1024,128]{1,0:T(8,128)(2,1)}, f16[1024,128]{1,0:T(8,128)(2,1)}, u32[]{:S(2)}, u32[]{:S(2)}) collective-permute-start(f16[1024,128]{1,0:T(8,128)(2,1)} %fusion.24), channel_id=1, source_target_pairs={{0,32},{8,40},{16,48},{24,56},{32,64},{40,72},{48,80},{56,88},{64,... | collective-permute-start | bytes 786440 | tf_op jit(solution)/shard_map/ppermute | solution.py:410
  228.8 10.5 %collective-permute-start.35 = (f16[1024,128]{1,0:T(8,128)(2,1)}, f16[1024,128]{1,0:T(8,128)(2,1)}, u32[]{:S(2)}, u32[]{:S(2)}) collective-permute-start(f16[1024,128]{1,0:T(8,128)(2,1)} %get-tuple-element.132), channel_id=1, source_target_pairs={{0,96},{8,104},{16,112},{24,120},{32,0},{40,8},{48,16},{56,24},{64... | collective-permute-start | bytes 786440 | tf_op jit(solution)/shard_map/ppermute | solution.py:410
  231.6 8.6 %collective-permute-start.36 = (f16[1024,128]{1,0:T(8,128)(2,1)}, f16[1024,128]{1,0:T(8,128)(2,1)}, u32[]{:S(2)}, u32[]{:S(2)}) collective-permute-start(f16[1024,128]{1,0:T(8,128)(2,1)} %get-tuple-element.133), channel_id=1, source_target_pairs={{0,64},{8,72},{16,80},{24,88},{32,96},{40,104},{48,112},{56,120},{... | collective-permute-start | bytes 786440 | tf_op jit(solution)/shard_map/ppermute | solution.py:410
  (19 other events, 137.7 us)

commit v3 on v2

--- a/solution.py
+++ b/solution.py
@@ -369,7 +369,8 @@
 
 
 def ring_exchange(parts, send, scales):
-    received = [send(pack(parts[r], scales), r) for r in (1, 3, 2)]
+    sent = [pack(parts[r], scales) for r in (1, 3, 2)]
+    received = [send(message, r) for message, r in zip(sent, (1, 3, 2))]
     up, down, across = (unpack(message, scales) for message in received)
     return parts[0] + up + down + across, received
 
@@ -502,18 +503,17 @@
         ring_second(r, values[2:4], send, z_scales, *around)
         for r, (values, send, _) in zip(received, rings)
     ]
-    lower_factor = after(lower_factor, seconds[0][2][1])
-    inverse = lax.linalg.triangular_solve(
-        lower_factor, jnp.eye(K, dtype=f32), left_side=True, lower=True
-    )
     thirds = []
     for (direct, sums, _), (values, _, send) in zip(seconds, rings):
         total = ring_total(direct, sums, [values[4:6], values[6:]], z_scales, *around)
         quarters = [total(r // 2, r % 2 * 4 * B, (r % 2 + 1) * 4 * B) for r in range(4)]
         thirds.append(ring_exchange(quarters, send, z_scales))
-    basis_factor = after(inverse, thirds[0][1][0])
+    lower_factor = after(lower_factor, thirds[0][1][0])
+    inverse = lax.linalg.triangular_solve(
+        lower_factor, jnp.eye(K, dtype=f32), left_side=True, lower=True
+    )
     q_share = jnp.dot(
-        y_share, basis_factor.T, precision=lax.Precision.HIGH, preferred_element_type=f32
+        y_share, inverse.T, precision=lax.Precision.HIGH, preferred_element_type=f32
     )
     z_raw = jnp.concatenate([z for z, _ in thirds], axis=0)
     z_share = jnp.dot(

time: 248 us -> 247 us (level)
  other arithmetic: 64.6 us -> 60.4 us
  waiting for transfers between devices: 27 us -> 31.1 us
    ppermute x13, waiting for transfers between devices: 1.36 us -> 8.37 us  [send_z(): return lax.ppermute(value, 'row', along_z(shift))]
    convert_element_type x15, other arithmetic: 28.6 us -> 25.1 us  [pack(): return by_rows((value * scales[1]).astype(f16))]
    ppermute x13, starting transfers between devices: 27.7 us -> 30.7 us  [send_z(): return lax.ppermute(value, 'row', along_z(shift))]
    ppermute x13, waiting for transfers between devices: 6.65 us -> 4.04 us  [send_x(): return lax.ppermute(value, 'row', along_x(shift))]
  transfers between devices with their start and end apart: 37 -> 37, of which waited for: 11 -> 11; matrix products, arithmetic and copies ran while one was open for 26% -> 24% of each run, Pallas kernels for 12% -> 12%
where the time goes in v3:
time: 247 us; the launch traced here: 244 us
  other arithmetic  60.4 us (24%)
  starting transfers between devices  57.6 us (23%)
  Pallas kernels  42.9 us (17%)
  blocking collectives  40 us (16%)
  waiting for transfers between devices  31.1 us (13%)
  matrix products  6.56 us (3%)
  between operations  3.98 us (2%)
    all_gather x1, blocking collectives, body(): gathered = lax.all_gather(mine, 'col', axis=0, tiled=True)  40 us
    ppermute x13, starting transfers between devices, send_z(): return lax.ppermute(value, 'row', along_z(shift))  30.7 us
    convert_element_type x15, other arithmetic, pack(): return by_rows((value * scales[1]).astype(f16))  25.1 us
    pallas_call x2, Pallas kernels, partial_rows(): pl.pallas_call(y_kernel, out_shape=sums_of(Y_PARTS) + (jax.ShapeDtypeStru...  23.8 us
    ppermute x7, waiting for transfers between devices, send_y(): return lax.ppermute(value, 'col', ring(shift))  18.6 us
    pallas_call x1, Pallas kernels, partial_cols(): pl.pallas_call(z_kernel, out_shape=sums_of(Z_PARTS * 2), in_specs=[pl.Blo...  17.2 us
    ppermute x13, starting transfers between devices, send_x(): return lax.ppermute(value, 'row', along_x(shift))  16.1 us
    another operation x3, other arithmetic, body(): lower_factor = jnp.linalg.cholesky(gram)  12.4 us
  transfers between devices with their start and end apart: 37, of which 11 were waited for; matrix products, arithmetic and copies ran while one was open for 24% of the time, Pallas kernels for 12%

profile of v3, /device:TPU:24, one launch (start us, length us, event | category | flops | bytes accessed | tf_op | source)
XLA Modules:
  0.0 244.0 jit_solution(18374071152136497364)
XLA Ops:
  3.7 10.9 %partial_rows.3 = (f32[32,256,128]{2,1,0:T(8,128)}, f32[32,256,128]{2,1,0:T(8,128)}, f32[8,128]{1,0:T(8,128)}) custom-call(s32[1]{0:T(128)} %bitcast.145.count, s32[96]{0:T(128)} %and_select_fusion.targets, s32[96]{0:T(128)} %bitcast.181, bf16[96,256,256]{2,1,0:T(8,128)(2,1)} %bitcast.151, bf16[128,256,128]{2,1,0:T(8,128)(2,1)} %bitcast.154), custom_call_target="tpu_custom_call" | custom-call | flops 805306368 | bytes 62914560 | tf_op jit(solution)/shard_map/partial_rows/pallas_call | solution.py:204
  16.8 13.0 %partial_rows.2 = (f32[32,256,128]{2,1,0:T(8,128)}, f32[32,256,128]{2,1,0:T(8,128)}, f32[8,128]{1,0:T(8,128)}) custom-call(s32[1]{0:T(128)} %bitcast.144.count, s32[96]{0:T(128)} %get-tuple-element.120.targets, s32[96]{0:T(128)} %bitcast.182, bf16[96,256,256]{2,1,0:T(8,128)(2,1)} %bitcast.152, bf16[128,256,128]{2,1,0:T(8,128)(2,1)} %bitcast.155), custom_call_target="tpu_custom_call" | custom-call | flops 805306368 | bytes 62914560 | tf_op jit(solution)/shard_map/partial_rows/pallas_call | solution.py:204
  30.6 4.5 %fusion.1 = (f16[16,256,128]{2,1,0:T(8,128)(2,1)S(1)}, f16[16,256,128]{2,1,0:T(8,128)(2,1)S(1)}) fusion(f32[32,256,128]{2,1,0:T(8,128)} %collective-permute-done.2, f32[32,256,128]{2,1,0:T(8,128)} %get-tuple-element.62, f32[]{:T(128)S(1)} %bitcast.191), kind=kLoop, calls=%fused_computation.4 | loop fusion | flops 3145728 | bytes 10485764 | tf_op jit(solution)/shard_map/convert_element_type | solution.py:331
  35.4 3.3 %collective-permute-start.4 = (f32[8,128]{1,0:T(8,128)S(1)}, f32[8,128]{1,0:T(8,128)S(1)}, u32[]{:S(2)}, u32[]{:S(2)}) collective-permute-start(f32[8,128]{1,0:T(8,128)S(1)} %get-tuple-element.64), channel_id=1, source_target_pairs={{0,2},{1,3},{2,4},{3,5},{4,6},{5,7},{6,0},{7,1},{8,10},{9,11},{10,... | collective-permute-start | bytes 12296 | tf_op jit(solution)/shard_map/ppermute | solution.py:408
  40.3 2.3 collective-permute-start.6
  43.7 2.8 %slice_add_fusion.2 = (f32[2048,128]{1,0:T(8,128)S(1)}, f32[2048,128]{1,0:T(8,128)S(1)}, f32[2048,128]{1,0:T(8,128)S(1)}, f32[2048,128]{1,0:T(8,128)S(1)}) fusion(f32[8192,128]{1,0:T(8,128)} %bitcast.7, f32[8192,128]{1,0:T(8,128)S(1)} %bitcast.156), kind=kLoop, calls=%fused_computation.35 | loop fusion | flops 1048576 | bytes 12582912 | tf_op jit(solution)/shard_map/add | solution.py:456
  46.7 3.2 %collective-permute-start.13 = (f32[8,128]{1,0:T(8,128)S(1)}, f32[8,128]{1,0:T(8,128)S(1)}, u32[]{:S(2)}, u32[]{:S(2)}) collective-permute-start(f32[8,128]{1,0:T(8,128)S(1)} %max.84), channel_id=1, source_target_pairs={{0,96},{8,104},{16,112},{24,120},{32,0},{40,8},{48,16},{56,24},{64... | collective-permute-start | bytes 12296 | tf_op jit(solution)/shard_map/ppermute | solution.py:411
  51.8 5.5 %collective-permute-start.14 = (f32[8,128]{1,0:T(8,128)S(1)}, f32[8,128]{1,0:T(8,128)S(1)}, u32[]{:S(2)}, u32[]{:S(2)}) collective-permute-start(f32[8,128]{1,0:T(8,128)S(1)} %maximum_maximum_fusion.1), channel_id=1, source_target_pairs={{0,16},{8,24},{16,0},{24,8},{32,48},{40,56},{48,32},{56,40},{64,80... | collective-permute-start | bytes 12296 | tf_op jit(solution)/shard_map/ppermute | solution.py:414
  60.5 4.1 %collective-permute-done.7 = f16[4096,128]{1,0:T(8,128)(2,1)S(1)} collective-permute-done((f16[4096,128]{1,0:T(8,128)(2,1)S(1)}, f16[4096,128]{1,0:T(8,128)(2,1)S(1)}, u32[]{:S(2)}, u32[]{:S(2)}) %collective-permute-start.7) | collective-permute-done | bytes 1048608 | tf_op jit(solution)/shard_map/ppermute | solution.py:408
  65.1 2.7 %collective-permute-start.8 = (f16[2048,128]{1,0:T(8,128)(2,1)S(1)}, f16[2048,128]{1,0:T(8,128)(2,1)S(1)}, u32[]{:S(2)}, u32[]{:S(2)}) collective-permute-start(f16[2048,128]{1,0:T(8,128)(2,1)S(1)} %multiply_convert_fusion.5), channel_id=1, source_target_pairs={{0,2},{1,3},{2,4},{3,5},{4,6},{5,7},{6,0},{7,1},{8,10},{9,11},{10,... | collective-permute-start | bytes 1572872 | tf_op jit(solution)/shard_map/ppermute | solution.py:408
  67.9 9.2 %collective-permute-done.8 = f16[2048,128]{1,0:T(8,128)(2,1)S(1)} collective-permute-done((f16[2048,128]{1,0:T(8,128)(2,1)S(1)}, f16[2048,128]{1,0:T(8,128)(2,1)S(1)}, u32[]{:S(2)}, u32[]{:S(2)}) %collective-permute-start.8) | collective-permute-done | bytes 524320 | tf_op jit(solution)/shard_map/ppermute | solution.py:408
  77.1 3.3 %collective-permute-done.9 = f16[2048,128]{1,0:T(8,128)(2,1)S(1)} collective-permute-done((f16[2048,128]{1,0:T(8,128)(2,1)S(1)}, f16[2048,128]{1,0:T(8,128)(2,1)S(1)}, u32[]{:S(2)}, u32[]{:S(2)}) %collective-permute-start.9) | collective-permute-done | bytes 524320 | tf_op jit(solution)/shard_map/ppermute | solution.py:408
  81.4 2.4 abs_reduce_fusion.1
  86.4 40.0 %all-gather.1.gathered.table = s16[35072,128]{1,0:T(8,128)(2,1)} all-gather(s16[4384,128]{1,0:T(8,128)(2,1)S(1)} %pad_add_fusion), channel_id=1, replica_groups=mesh['row'=16,'col'=8] {'col'}, dimensions={0}, use_global_device_ids=true | all-gather | bytes 10100736 | tf_op jit(solution)/shard_map/all_gather | solution.py:488
  128.5 3.2 %collective-permute-start.19 = (f32[128,128]{1,0:T(8,128)}, f32[128,128]{1,0:T(8,128)S(1)}, u32[]{:S(2)}, u32[]{:S(2)}) collective-permute-start(f32[128,128]{1,0:T(8,128)} %get-tuple-element.82), channel_id=1, source_target_pairs={{0,96},{8,104},{16,112},{24,120},{32,0},{40,8},{48,16},{56,24},{64... | collective-permute-start | bytes 196616 | tf_op jit(solution)/shard_map/ppermute | solution.py:411
  131.7 17.2 %partial_cols.1 = (f32[16,256,128]{2,1,0:T(8,128)}, f32[16,256,128]{2,1,0:T(8,128)}, f32[8,256,128]{2,1,0:T(8,128)}, f32[8,256,128]{2,1,0:T(8,128)}, f32[4,256,1...) custom-call(s32[1]{0:T(128)} %bitcast.146.count, ...), custom_call_target="tpu_custom_call" | custom-call | flops 3221225472 | bytes 44040192 | tf_op jit(solution)/shard_map/partial_cols/pallas_call | solution.py:304
  148.9 3.0 %multiply_convert_fusion.2 = f16[16,256,128]{2,1,0:T(8,128)(2,1)} fusion(f32[16,256,128]{2,1,0:T(8,128)} %get-tuple-element.87, f32[]{:T(128)S(1)} %bitcast.160), kind=kLoop, calls=%fused_computation.11 | loop fusion | flops 1048576 | bytes 3145732 | tf_op jit(solution)/shard_map/convert_element_type | solution.py:331
  152.0 9.2 %collective-permute-start.20 = (f32[128,128]{1,0:T(8,128)S(1)}, f32[128,128]{1,0:T(8,128)S(1)}, u32[]{:S(2)}, u32[]{:S(2)}) collective-permute-start(f32[128,128]{1,0:T(8,128)S(1)} %add_add_fusion.1), channel_id=1, source_target_pairs={{0,16},{8,24},{16,0},{24,8},{32,48},{40,56},{48,32},{56,40},{64,80... | collective-permute-start | bytes 196616 | tf_op jit(solution)/shard_map/ppermute | solution.py:414
  161.2 3.2 %collective-permute-start.22 = (f32[128,128]{1,0:T(8,128)S(1)}, f32[128,128]{1,0:T(8,128)S(1)}, u32[]{:S(2)}, u32[]{:S(2)}) collective-permute-start(f32[128,128]{1,0:T(8,128)S(1)} %add_add_fusion.1), channel_id=1, source_target_pairs={{0,24},{8,0},{16,8},{24,16},{32,56},{40,32},{48,40},{56,48},{64,88... | collective-permute-start | bytes 196616 | tf_op jit(solution)/shard_map/ppermute | solution.py:414
  168.1 3.0 %multiply_convert_fusion = f16[16,256,128]{2,1,0:T(8,128)(2,1)} fusion(f32[16,256,128]{2,1,0:T(8,128)} %get-tuple-element.102, f32[]{:T(128)S(6)} %add.240), kind=kLoop, calls=%fused_computation.9 | loop fusion | flops 1048576 | bytes 3145732 | tf_op jit(solution)/shard_map/convert_element_type | solution.py:331
  171.1 3.2 %collective-permute-start.31 = (f16[4096,128]{1,0:T(8,128)(2,1)}, f16[4096,128]{1,0:T(8,128)(2,1)}, u32[]{:S(2)}, u32[]{:S(2)}) collective-permute-start(f16[4096,128]{1,0:T(8,128)(2,1)} %bitcast.32), channel_id=1, source_target_pairs={{0,24},{8,0},{16,8},{24,16},{32,56},{40,32},{48,40},{56,48},{64,88... | collective-permute-start | bytes 3145736 | tf_op jit(solution)/shard_map/ppermute | solution.py:414
  175.6 11.7 %cholesky.17 = f32[128,128]{1,0:T(8,128)S(1)} custom-call(f32[128,128]{1,0:T(8,128)S(1)} %fusion.44), custom_call_target="Cholesky" | custom-call | tf_op jit(solution)/shard_map/jit(cholesky)/cholesky | solution.py:501
  191.9 3.2 %collective-permute-start.26 = (f16[2048,128]{1,0:T(8,128)(2,1)S(1)}, f16[2048,128]{1,0:T(8,128)(2,1)S(1)}, u32[]{:S(2)}, u32[]{:S(2)}) collective-permute-start(f16[2048,128]{1,0:T(8,128)(2,1)S(1)} %fusion.12), channel_id=1, source_target_pairs={{0,96},{8,104},{16,112},{24,120},{32,0},{40,8},{48,16},{56,24},{64... | collective-permute-start | bytes 1572872 | tf_op jit(solution)/shard_map/ppermute | solution.py:411
  196.7 2.3 collective-permute-done.30
  199.3 3.2 %collective-permute-start.33 = (f16[2048,128]{1,0:T(8,128)(2,1)S(1)}, f16[2048,128]{1,0:T(8,128)(2,1)S(1)}, u32[]{:S(2)}, u32[]{:S(2)}) collective-permute-start(f16[2048,128]{1,0:T(8,128)(2,1)S(1)} %fusion.8), channel_id=1, source_target_pairs={{0,24},{8,0},{16,8},{24,16},{32,56},{40,32},{48,40},{56,48},{64,88... | collective-permute-start | bytes 1572872 | tf_op jit(solution)/shard_map/ppermute | solution.py:414
  204.2 2.4 fusion.34
  206.5 2.1 collective-permute-start.28
  210.7 5.1 %collective-permute-done.32 = f16[2048,128]{1,0:T(8,128)(2,1)S(1)} collective-permute-done((f16[2048,128]{1,0:T(8,128)(2,1)S(1)}, f16[2048,128]{1,0:T(8,128)(2,1)S(1)}, u32[]{:S(2)}, u32[]{:S(2)}) %collective-permute-start.32) | collective-permute-done | bytes 524320 | tf_op jit(solution)/shard_map/ppermute | solution.py:414
  217.8 2.5 %collective-permute-start.34 = (f16[1024,128]{1,0:T(8,128)(2,1)}, f16[1024,128]{1,0:T(8,128)(2,1)}, u32[]{:S(2)}, u32[]{:S(2)}) collective-permute-start(f16[1024,128]{1,0:T(8,128)(2,1)} %fusion.24), channel_id=1, source_target_pairs={{0,32},{8,40},{16,48},{24,56},{32,64},{40,72},{48,80},{56,88},{64,... | collective-permute-start | bytes 786440 | tf_op jit(solution)/shard_map/ppermute | solution.py:411
  222.2 2.8 %collective-permute-start.36 = (f16[1024,128]{1,0:T(8,128)(2,1)}, f16[1024,128]{1,0:T(8,128)(2,1)S(1)}, u32[]{:S(2)}, u32[]{:S(2)}) collective-permute-start(f16[1024,128]{1,0:T(8,128)(2,1)} %get-tuple-element.131), channel_id=1, source_target_pairs={{0,64},{8,72},{16,80},{24,88},{32,96},{40,104},{48,112},{56,120},{... | collective-permute-start | bytes 786440 | tf_op jit(solution)/shard_map/ppermute | solution.py:411
  226.9 9.8 %custom-call.6 = f32[1,128,128]{1,2,0:T(8,128)S(1)} custom-call(f32[1,128,128]{2,1,0:T(8,128)S(1)} %select_bitcast_fusion), custom_call_target="InvertDiagBlocksLowerTriangular" | custom-call | tf_op jit(solution)/shard_map/triangular_solve | solution.py:512
  238.7 2.3 convolution_multiply_fusion
  (148 shorter events, 43.4 us)
Async XLA Ops:
  14.6 16.0 %collective-permute-start.2 = (f32[32,256,128]{2,1,0:T(8,128)}, f32[32,256,128]{2,1,0:T(8,128)}, u32[]{:S(2)}, u32[]{:S(2)}) collective-permute-start(f32[32,256,128]{2,1,0:T(8,128)} %get-tuple-element.63), channel_id=1, source_target_pairs={{0,1},{1,0},{2,3},{3,2},{4,5},{5,4},{6,7},{7,6},{8,9},{9,8},{10,11... | collective-permute-start | bytes 12582920 | tf_op jit(solution)/shard_map/ppermute | solution.py:405
  16.3 27.4 %collective-permute-start = (f32[32,256,128]{2,1,0:T(8,128)}, f32[32,256,128]{2,1,0:T(8,128)}, u32[]{:S(2)}, u32[]{:S(2)}) collective-permute-start(f32[32,256,128]{2,1,0:T(8,128)} %get-tuple-element.59), channel_id=1, source_target_pairs={{0,1},{1,0},{2,3},{3,2},{4,5},{5,4},{6,7},{7,6},{8,9},{9,8},{10,11... | collective-permute-start | bytes 12582920 | tf_op jit(solution)/shard_map/ppermute | solution.py:405
  16.4 13.4 %collective-permute-start.1 = (f32[8,128]{1,0:T(8,128)}, f32[8,128]{1,0:T(8,128)S(1)}, u32[]{:S(2)}, u32[]{:S(2)}) collective-permute-start(f32[8,128]{1,0:T(8,128)} %get-tuple-element.61), channel_id=1, source_target_pairs={{0,1},{1,0},{2,3},{3,2},{4,5},{5,4},{6,7},{7,6},{8,9},{9,8},{10,11... | collective-permute-start | bytes 12296 | tf_op jit(solution)/shard_map/ppermute | solution.py:405
  35.1 5.2 %collective-permute-start.3 = (f32[8,128]{1,0:T(8,128)S(1)}, f32[8,128]{1,0:T(8,128)S(1)}, u32[]{:S(2)}, u32[]{:S(2)}) collective-permute-start(f32[8,128]{1,0:T(8,128)S(1)} %get-tuple-element.64), channel_id=1, source_target_pairs={{0,4},{1,5},{2,6},{3,7},{4,0},{5,1},{6,2},{7,3},{8,12},{9,13},{10,... | collective-permute-start | bytes 12296 | tf_op jit(solution)/shard_map/ppermute | solution.py:408
  35.4 7.1 %collective-permute-start.4 = (f32[8,128]{1,0:T(8,128)S(1)}, f32[8,128]{1,0:T(8,128)S(1)}, u32[]{:S(2)}, u32[]{:S(2)}) collective-permute-start(f32[8,128]{1,0:T(8,128)S(1)} %get-tuple-element.64), channel_id=1, source_target_pairs={{0,2},{1,3},{2,4},{3,5},{4,6},{5,7},{6,0},{7,1},{8,10},{9,11},{10,... | collective-permute-start | bytes 12296 | tf_op jit(solution)/shard_map/ppermute | solution.py:408
  39.3 25.3 %collective-permute-start.7 = (f16[4096,128]{1,0:T(8,128)(2,1)S(1)}, f16[4096,128]{1,0:T(8,128)(2,1)S(1)}, u32[]{:S(2)}, u32[]{:S(2)}) collective-permute-start(f16[4096,128]{1,0:T(8,128)(2,1)S(1)} %bitcast.158), channel_id=1, source_target_pairs={{0,6},{1,7},{2,0},{3,1},{4,2},{5,3},{6,4},{7,5},{8,14},{9,15},{10,... | collective-permute-start | bytes 3145736 | tf_op jit(solution)/shard_map/ppermute | solution.py:408
  40.3 24.5 %collective-permute-start.6 = (f16[4096,128]{1,0:T(8,128)(2,1)S(1)}, f16[4096,128]{1,0:T(8,128)(2,1)S(1)}, u32[]{:S(2)}, u32[]{:S(2)}) collective-permute-start(f16[4096,128]{1,0:T(8,128)(2,1)S(1)} %bitcast.157), channel_id=1, source_target_pairs={{0,2},{1,3},{2,4},{3,5},{4,6},{5,7},{6,0},{7,1},{8,10},{9,11},{10,... | collective-permute-start | bytes 3145736 | tf_op jit(solution)/shard_map/ppermute | solution.py:408
  51.8 16.1 %collective-permute-start.14 = (f32[8,128]{1,0:T(8,128)S(1)}, f32[8,128]{1,0:T(8,128)S(1)}, u32[]{:S(2)}, u32[]{:S(2)}) collective-permute-start(f32[8,128]{1,0:T(8,128)S(1)} %maximum_maximum_fusion.1), channel_id=1, source_target_pairs={{0,16},{8,24},{16,0},{24,8},{32,48},{40,56},{48,32},{56,40},{64,80... | collective-permute-start | bytes 12296 | tf_op jit(solution)/shard_map/ppermute | solution.py:414
  57.2 10.6 %collective-permute-start.15 = (f32[8,128]{1,0:T(8,128)S(1)}, f32[8,128]{1,0:T(8,128)S(1)}, u32[]{:S(2)}, u32[]{:S(2)}) collective-permute-start(f32[8,128]{1,0:T(8,128)S(1)} %maximum_maximum_fusion.1), channel_id=1, source_target_pairs={{0,8},{8,16},{16,24},{24,0},{32,40},{40,48},{48,56},{56,32},{64,72... | collective-permute-start | bytes 12296 | tf_op jit(solution)/shard_map/ppermute | solution.py:414
  58.7 9.2 %collective-permute-start.16 = (f32[8,128]{1,0:T(8,128)S(1)}, f32[8,128]{1,0:T(8,128)S(1)}, u32[]{:S(2)}, u32[]{:S(2)}) collective-permute-start(f32[8,128]{1,0:T(8,128)S(1)} %maximum_maximum_fusion.1), channel_id=1, source_target_pairs={{0,24},{8,0},{16,8},{24,16},{32,56},{40,32},{48,40},{56,48},{64,88... | collective-permute-start | bytes 12296 | tf_op jit(solution)/shard_map/ppermute | solution.py:414
  65.1 12.0 %collective-permute-start.8 = (f16[2048,128]{1,0:T(8,128)(2,1)S(1)}, f16[2048,128]{1,0:T(8,128)(2,1)S(1)}, u32[]{:S(2)}, u32[]{:S(2)}) collective-permute-start(f16[2048,128]{1,0:T(8,128)(2,1)S(1)} %multiply_convert_fusion.5), channel_id=1, source_target_pairs={{0,2},{1,3},{2,4},{3,5},{4,6},{5,7},{6,0},{7,1},{8,10},{9,11},{10,... | collective-permute-start | bytes 1572872 | tf_op jit(solution)/shard_map/ppermute | solution.py:408
  67.8 12.5 %collective-permute-start.9 = (f16[2048,128]{1,0:T(8,128)(2,1)S(1)}, f16[2048,128]{1,0:T(8,128)(2,1)S(1)}, u32[]{:S(2)}, u32[]{:S(2)}) collective-permute-start(f16[2048,128]{1,0:T(8,128)(2,1)S(1)} %multiply_convert_fusion.4), channel_id=1, source_target_pairs={{0,6},{1,7},{2,0},{3,1},{4,2},{5,3},{6,4},{7,5},{8,14},{9,15},{10,... | collective-permute-start | bytes 1572872 | tf_op jit(solution)/shard_map/ppermute | solution.py:408
  128.3 23.6 %collective-permute-start.17 = (f32[128,128]{1,0:T(8,128)}, f32[128,128]{1,0:T(8,128)S(1)}, u32[]{:S(2)}, u32[]{:S(2)}) collective-permute-start(f32[128,128]{1,0:T(8,128)} %get-tuple-element.82), channel_id=1, source_target_pairs={{0,64},{8,72},{16,80},{24,88},{32,96},{40,104},{48,112},{56,120},{... | collective-permute-start | bytes 196616 | tf_op jit(solution)/shard_map/ppermute | solution.py:411
  128.4 23.5 %collective-permute-start.18 = (f32[128,128]{1,0:T(8,128)}, f32[128,128]{1,0:T(8,128)S(1)}, u32[]{:S(2)}, u32[]{:S(2)}) collective-permute-start(f32[128,128]{1,0:T(8,128)} %get-tuple-element.82), channel_id=1, source_target_pairs={{0,32},{8,40},{16,48},{24,56},{32,64},{40,72},{48,80},{56,88},{64,... | collective-permute-start | bytes 196616 | tf_op jit(solution)/shard_map/ppermute | solution.py:411
  128.5 23.5 %collective-permute-start.19 = (f32[128,128]{1,0:T(8,128)}, f32[128,128]{1,0:T(8,128)S(1)}, u32[]{:S(2)}, u32[]{:S(2)}) collective-permute-start(f32[128,128]{1,0:T(8,128)} %get-tuple-element.82), channel_id=1, source_target_pairs={{0,96},{8,104},{16,112},{24,120},{32,0},{40,8},{48,16},{56,24},{64... | collective-permute-start | bytes 196616 | tf_op jit(solution)/shard_map/ppermute | solution.py:411
  151.9 36.1 %collective-permute-start.24 = (f16[4096,128]{1,0:T(8,128)(2,1)}, f16[4096,128]{1,0:T(8,128)(2,1)}, u32[]{:S(2)}, u32[]{:S(2)}) collective-permute-start(f16[4096,128]{1,0:T(8,128)(2,1)} %bitcast.20), channel_id=1, source_target_pairs={{0,96},{8,104},{16,112},{24,120},{32,0},{40,8},{48,16},{56,24},{64... | collective-permute-start | bytes 3145736 | tf_op jit(solution)/shard_map/ppermute | solution.py:411
  152.0 13.7 %collective-permute-start.20 = (f32[128,128]{1,0:T(8,128)S(1)}, f32[128,128]{1,0:T(8,128)S(1)}, u32[]{:S(2)}, u32[]{:S(2)}) collective-permute-start(f32[128,128]{1,0:T(8,128)S(1)} %add_add_fusion.1), channel_id=1, source_target_pairs={{0,16},{8,24},{16,0},{24,8},{32,48},{40,56},{48,32},{56,40},{64,80... | collective-permute-start | bytes 196616 | tf_op jit(solution)/shard_map/ppermute | solution.py:414
  161.2 5.5 %collective-permute-start.21 = (f32[128,128]{1,0:T(8,128)S(1)}, f32[128,128]{1,0:T(8,128)S(1)}, u32[]{:S(2)}, u32[]{:S(2)}) collective-permute-start(f32[128,128]{1,0:T(8,128)S(1)} %add_add_fusion.1), channel_id=1, source_target_pairs={{0,8},{8,16},{16,24},{24,0},{32,40},{40,48},{48,56},{56,32},{64,72... | collective-permute-start | bytes 196616 | tf_op jit(solution)/shard_map/ppermute | solution.py:414
  161.2 5.5 %collective-permute-start.22 = (f32[128,128]{1,0:T(8,128)S(1)}, f32[128,128]{1,0:T(8,128)S(1)}, u32[]{:S(2)}, u32[]{:S(2)}) collective-permute-start(f32[128,128]{1,0:T(8,128)S(1)} %add_add_fusion.1), channel_id=1, source_target_pairs={{0,24},{8,0},{16,8},{24,16},{32,56},{40,32},{48,40},{56,48},{64,88... | collective-permute-start | bytes 196616 | tf_op jit(solution)/shard_map/ppermute | solution.py:414
  165.7 24.7 %collective-permute-start.23 = (f16[4096,128]{1,0:T(8,128)(2,1)}, f16[4096,128]{1,0:T(8,128)(2,1)}, u32[]{:S(2)}, u32[]{:S(2)}) collective-permute-start(f16[4096,128]{1,0:T(8,128)(2,1)} %bitcast.19), channel_id=1, source_target_pairs={{0,32},{8,40},{16,48},{24,56},{32,64},{40,72},{48,80},{56,88},{64,... | collective-permute-start | bytes 3145736 | tf_op jit(solution)/shard_map/ppermute | solution.py:411
  171.1 24.1 %collective-permute-start.31 = (f16[4096,128]{1,0:T(8,128)(2,1)}, f16[4096,128]{1,0:T(8,128)(2,1)}, u32[]{:S(2)}, u32[]{:S(2)}) collective-permute-start(f16[4096,128]{1,0:T(8,128)(2,1)} %bitcast.32), channel_id=1, source_target_pairs={{0,24},{8,0},{16,8},{24,16},{32,56},{40,32},{48,40},{56,48},{64,88... | collective-permute-start | bytes 3145736 | tf_op jit(solution)/shard_map/ppermute | solution.py:414
  175.6 23.4 %collective-permute-start.30 = (f16[4096,128]{1,0:T(8,128)(2,1)}, f16[4096,128]{1,0:T(8,128)(2,1)S(1)}, u32[]{:S(2)}, u32[]{:S(2)}) collective-permute-start(f16[4096,128]{1,0:T(8,128)(2,1)} %bitcast.31), channel_id=1, source_target_pairs={{0,8},{8,16},{16,24},{24,0},{32,40},{40,48},{48,56},{56,32},{64,72... | collective-permute-start | bytes 3145736 | tf_op jit(solution)/shard_map/ppermute | solution.py:414
  191.9 12.3 %collective-permute-start.25 = (f16[2048,128]{1,0:T(8,128)(2,1)S(1)}, f16[2048,128]{1,0:T(8,128)(2,1)S(1)}, u32[]{:S(2)}, u32[]{:S(2)}) collective-permute-start(f16[2048,128]{1,0:T(8,128)(2,1)S(1)} %fusion.14), channel_id=1, source_target_pairs={{0,32},{8,40},{16,48},{24,56},{32,64},{40,72},{48,80},{56,88},{64,... | collective-permute-start | bytes 1572872 | tf_op jit(solution)/shard_map/ppermute | solution.py:411
  191.9 12.2 %collective-permute-start.26 = (f16[2048,128]{1,0:T(8,128)(2,1)S(1)}, f16[2048,128]{1,0:T(8,128)(2,1)S(1)}, u32[]{:S(2)}, u32[]{:S(2)}) collective-permute-start(f16[2048,128]{1,0:T(8,128)(2,1)S(1)} %fusion.12), channel_id=1, source_target_pairs={{0,96},{8,104},{16,112},{24,120},{32,0},{40,8},{48,16},{56,24},{64... | collective-permute-start | bytes 1572872 | tf_op jit(solution)/shard_map/ppermute | solution.py:411
  199.3 16.6 %collective-permute-start.32 = (f16[2048,128]{1,0:T(8,128)(2,1)S(1)}, f16[2048,128]{1,0:T(8,128)(2,1)S(1)}, u32[]{:S(2)}, u32[]{:S(2)}) collective-permute-start(f16[2048,128]{1,0:T(8,128)(2,1)S(1)} %fusion.10), channel_id=1, source_target_pairs={{0,8},{8,16},{16,24},{24,0},{32,40},{40,48},{48,56},{56,32},{64,72... | collective-permute-start | bytes 1572872 | tf_op jit(solution)/shard_map/ppermute | solution.py:414
  199.3 16.5 %collective-permute-start.33 = (f16[2048,128]{1,0:T(8,128)(2,1)S(1)}, f16[2048,128]{1,0:T(8,128)(2,1)S(1)}, u32[]{:S(2)}, u32[]{:S(2)}) collective-permute-start(f16[2048,128]{1,0:T(8,128)(2,1)S(1)} %fusion.8), channel_id=1, source_target_pairs={{0,24},{8,0},{16,8},{24,16},{32,56},{40,32},{48,40},{56,48},{64,88... | collective-permute-start | bytes 1572872 | tf_op jit(solution)/shard_map/ppermute | solution.py:414
  206.5 30.4 %collective-permute-start.28 = (f16[1024,128]{1,0:T(8,128)(2,1)}, f16[1024,128]{1,0:T(8,128)(2,1)}, u32[]{:S(2)}, u32[]{:S(2)}) collective-permute-start(f16[1024,128]{1,0:T(8,128)(2,1)} %get-tuple-element.128), channel_id=1, source_target_pairs={{0,24},{8,0},{16,8},{24,16},{32,56},{40,32},{48,40},{56,48},{64,88... | collective-permute-start | bytes 786440 | tf_op jit(solution)/shard_map/ppermute | solution.py:414
  208.6 28.3 %collective-permute-start.29 = (f16[1024,128]{1,0:T(8,128)(2,1)S(1)}, f16[1024,128]{1,0:T(8,128)(2,1)}, u32[]{:S(2)}, u32[]{:S(2)}) collective-permute-start(f16[1024,128]{1,0:T(8,128)(2,1)S(1)} %get-tuple-element.129), channel_id=1, source_target_pairs={{0,16},{8,24},{16,0},{24,8},{32,48},{40,56},{48,32},{56,40},{64,80... | collective-permute-start | bytes 786440 | tf_op jit(solution)/shard_map/ppermute | solution.py:414
  209.8 12.4 %collective-permute-start.27 = (f16[1024,128]{1,0:T(8,128)(2,1)S(1)}, f16[1024,128]{1,0:T(8,128)(2,1)S(1)}, u32[]{:S(2)}, u32[]{:S(2)}) collective-permute-start(f16[1024,128]{1,0:T(8,128)(2,1)S(1)} %fusion.41), channel_id=1, source_target_pairs={{0,8},{8,16},{16,24},{24,0},{32,40},{40,48},{48,56},{56,32},{64,72... | collective-permute-start | bytes 786440 | tf_op jit(solution)/shard_map/ppermute | solution.py:414
  217.8 23.2 %collective-permute-start.34 = (f16[1024,128]{1,0:T(8,128)(2,1)}, f16[1024,128]{1,0:T(8,128)(2,1)}, u32[]{:S(2)}, u32[]{:S(2)}) collective-permute-start(f16[1024,128]{1,0:T(8,128)(2,1)} %fusion.24), channel_id=1, source_target_pairs={{0,32},{8,40},{16,48},{24,56},{32,64},{40,72},{48,80},{56,88},{64,... | collective-permute-start | bytes 786440 | tf_op jit(solution)/shard_map/ppermute | solution.py:411
  221.5 19.5 %collective-permute-start.35 = (f16[1024,128]{1,0:T(8,128)(2,1)}, f16[1024,128]{1,0:T(8,128)(2,1)S(1)}, u32[]{:S(2)}, u32[]{:S(2)}) collective-permute-start(f16[1024,128]{1,0:T(8,128)(2,1)} %get-tuple-element.130), channel_id=1, source_target_pairs={{0,96},{8,104},{16,112},{24,120},{32,0},{40,8},{48,16},{56,24},{64... | collective-permute-start | bytes 786440 | tf_op jit(solution)/shard_map/ppermute | solution.py:411
  222.2 18.8 %collective-permute-start.36 = (f16[1024,128]{1,0:T(8,128)(2,1)}, f16[1024,128]{1,0:T(8,128)(2,1)S(1)}, u32[]{:S(2)}, u32[]{:S(2)}) collective-permute-start(f16[1024,128]{1,0:T(8,128)(2,1)} %get-tuple-element.131), channel_id=1, source_target_pairs={{0,64},{8,72},{16,80},{24,88},{32,96},{40,104},{48,112},{56,120},{... | collective-permute-start | bytes 786440 | tf_op jit(solution)/shard_map/ppermute | solution.py:411
  (25 other events, 204.4 us)

commit v4 on v2

--- a/solution.py
+++ b/solution.py
@@ -181,7 +181,7 @@
 
 
 Y_PARTS = (32, 32)
-Z_PARTS = (16, 16, 8, 8, 4, 4, 4, 4)
+Z_PARTS = (16, 16, 16, 4, 4, 4, 4)
 
 
 def sums_of(parts):
@@ -256,7 +256,7 @@
 
 
 def z_kernel(count, targets, rows, blocks, table, tile_scales, *rest):
-    outs, scratch = rest[:16], rest[16:]
+    outs, scratch = rest[:14], rest[14:]
     total_sum, order, bounds, block_buf, y_buf, sems, out_sems = scratch
 
     def copies(j):
@@ -307,7 +307,7 @@
         in_specs=[pl.BlockSpec(memory_space=pltpu.SMEM)] * 3
         + [pl.BlockSpec(memory_space=pl.ANY)] * 2
         + [pl.BlockSpec(memory_space=pltpu.VMEM)],
-        out_specs=(pl.BlockSpec(memory_space=pl.ANY),) * 16,
+        out_specs=(pl.BlockSpec(memory_space=pl.ANY),) * 14,
         scratch_shapes=scratch_for(2, Z_PARTS, jnp.int16),
         compiler_params=pltpu.CompilerParams(vmem_limit_bytes=VMEM_BYTES),
         cost_estimate=pl.CostEstimate(
@@ -336,6 +336,7 @@
 
 
 PLACES = (6, 7, 4, 1, 0, 2, 3, 5)
+Z_PLACES = (6, 7, 0, 1, 4, 5, 2, 3)
 
 
 HALF = CHUNK * B
@@ -414,19 +415,19 @@
 
     live = jnp.arange(NBLK, dtype=jnp.int32) < count
 
-    def chunk_of(rel, half):
+    def chunk_of(rel, half, places):
         key = (rel & 3) * 2 + half
-        chunk = PLACES[7]
+        chunk = places[7]
         for k in range(7):
-            chunk = jnp.where(key == k, PLACES[k], chunk)
+            chunk = jnp.where(key == k, places[k], chunk)
         return chunk * CHUNK
 
-    y_target = chunk_of((rows >> 5) - here_y, (rows >> 3) & 1) + (rows & 7)
+    y_target = chunk_of((rows >> 5) - here_y, (rows >> 3) & 1, PLACES) + (rows & 7)
     row_core = (rows >> 4) & 1
     rel_x, rel_z = ((cols >> 5) - here_x) & 3, ((cols >> 3) - here_z) & 3
     is_a = ((cols >> 2) & 1) == 0
     one, two = jnp.where(is_a, rel_x, rel_z), jnp.where(is_a, rel_z, rel_x)
-    z_target = chunk_of(one, two >> 1) + (two & 1) * 4 + (cols & 3) + jnp.where(is_a, 0, 8 * CHUNK)
+    z_target = chunk_of(one, two >> 1, Z_PLACES) + (two & 1) * 4 + (cols & 3) + jnp.where(is_a, 0, 8 * CHUNK)
     other_target = jnp.where(live & (row_core != core), y_target, -1)
     own_target = jnp.where(live & (row_core == core), y_target, -1)
     z_target = jnp.where(live, z_target, -1)
@@ -490,26 +491,22 @@
     partial = flat(partial_cols(count, z_target, rows, blocks, gathered, tile_scales))
     gram = by_rows(ring_fold(gram, send_z, jnp.add)[0])
 
-    rings = [(partial[:8], send_x, send_z), (partial[8:], send_z, send_x)]
-    around = z_scales, z_scales
+    rings = [(partial[:7], send_x, send_z), (partial[7:], send_z, send_x)]
     scales_each = [z_scales, (z_scales[0], after(z_scales[1], gram))]
-    messages = [
-        [pack(v, scales) for v in values[:2]] for (values, _, _), scales in zip(rings, scales_each)
+    received = [
+        [send(pack(v, scales), to) for v, to in zip(values[:3], (1, 3, 2))]
+        for (values, send, _), scales in zip(rings, scales_each)
     ]
-    received = [[send(m[0], 1), send(m[1], -1)] for m, (_, send, _) in zip(messages, rings)]
     lower_factor = jnp.linalg.cholesky(gram)
-    seconds = [
-        ring_second(r, values[2:4], send, z_scales, *around)
-        for r, (values, send, _) in zip(received, rings)
-    ]
-    lower_factor = after(lower_factor, seconds[0][2][1])
     inverse = lax.linalg.triangular_solve(
         lower_factor, jnp.eye(K, dtype=f32), left_side=True, lower=True
     )
     thirds = []
-    for (direct, sums, _), (values, _, send) in zip(seconds, rings):
-        total = ring_total(direct, sums, [values[4:6], values[6:]], z_scales, *around)
-        quarters = [total(r // 2, r % 2 * 4 * B, (r % 2 + 1) * 4 * B) for r in range(4)]
+    for came, (values, _, send) in zip(received, rings):
+        quarters = []
+        for r in range(4):
+            at = slice(r * 4 * B, (r + 1) * 4 * B)
+            quarters.append(sum((unpack(message[at], z_scales) for message in came), values[3 + r]))
         thirds.append(ring_exchange(quarters, send, z_scales))
     basis_factor = after(inverse, thirds[0][1][0])
     q_share = jnp.dot(

time: 248 us -> 262 us (1.056)
  waiting for transfers between devices: 27 us -> 46.9 us
  starting transfers between devices: 55.8 us -> 64.5 us
  other arithmetic: 64.6 us -> 58.2 us
  Pallas kernels: 41.4 us -> 36.1 us
    ppermute x13 -> x12, waiting for transfers between devices: 6.65 us -> 22.7 us  [send_x(): return lax.ppermute(value, 'row', along_x(shift))]
    ppermute x13 -> x12, starting transfers between devices: 27.7 us -> 35.6 us  [send_z(): return lax.ppermute(value, 'row', along_z(shift))]
    convert_element_type x15 -> x11, other arithmetic: 28.6 us -> 22.4 us  [pack(): return by_rows((value * scales[1]).astype(f16))]
    ppermute x13 -> x12, waiting for transfers between devices: 1.36 us -> 5.03 us  [send_z(): return lax.ppermute(value, 'row', along_z(shift))]
    ppermute x13 -> x12, starting transfers between devices: 16.4 us -> 19.7 us  [send_x(): return lax.ppermute(value, 'row', along_x(shift))]
    pallas_call x1, Pallas kernels: 16.5 us -> 13.2 us  [partial_cols(): pl.pallas_call(z_kernel, out_shape=sums_of(Z_PARTS * 2), in_specs=[pl.Blo...]
  transfers between devices with their start and end apart: 37 -> 35, of which waited for: 11 -> 10; matrix products, arithmetic and copies ran while one was open for 26% -> 21% of each run, Pallas kernels for 12% -> 9%
where the time goes in v4:
time: 262 us; the launch traced here: 259 us
  starting transfers between devices  64.5 us (25%)
  other arithmetic  58.2 us (22%)
  waiting for transfers between devices  46.9 us (18%)
  blocking collectives  40.8 us (16%)
  Pallas kernels  36.1 us (14%)
  matrix products  6.54 us (2%)
  between operations  3.76 us (1%)
    all_gather x1, blocking collectives, body(): gathered = lax.all_gather(mine, 'col', axis=0, tiled=True)  40.8 us
    ppermute x12, starting transfers between devices, send_z(): return lax.ppermute(value, 'row', along_z(shift))  35.6 us
    ppermute x12, waiting for transfers between devices, send_x(): return lax.ppermute(value, 'row', along_x(shift))  22.7 us
    convert_element_type x11, other arithmetic, pack(): return by_rows((value * scales[1]).astype(f16))  22.4 us
    pallas_call x2, Pallas kernels, partial_rows(): pl.pallas_call(y_kernel, out_shape=sums_of(Y_PARTS) + (jax.ShapeDtypeStru...  21 us
    ppermute x12, starting transfers between devices, send_x(): return lax.ppermute(value, 'row', along_x(shift))  19.7 us
    ppermute x7, waiting for transfers between devices, send_y(): return lax.ppermute(value, 'col', ring(shift))  19.2 us
    pallas_call x1, Pallas kernels, partial_cols(): pl.pallas_call(z_kernel, out_shape=sums_of(Z_PARTS * 2), in_specs=[pl.Blo...  13.2 us
  transfers between devices with their start and end apart: 35, of which 10 were waited for; matrix products, arithmetic and copies ran while one was open for 21% of the time, Pallas kernels for 9%

profile of v4, /device:TPU:24, one launch (start us, length us, event | category | flops | bytes accessed | tf_op | source)
XLA Modules:
  0.0 258.8 jit_solution(7730927582197389149)
XLA Ops:
  3.7 10.4 %partial_rows.3 = (f32[32,256,128]{2,1,0:T(8,128)}, f32[32,256,128]{2,1,0:T(8,128)}, f32[8,128]{1,0:T(8,128)}) custom-call(s32[1]{0:T(128)} %bitcast.138.count, s32[96]{0:T(128)} %and_select_fusion.targets, s32[96]{0:T(128)} %bitcast.163, bf16[96,256,256]{2,1,0:T(8,128)(2,1)} %bitcast.144, bf16[128,256,128]{2,1,0:T(8,128)(2,1)} %bitcast.147), custom_call_target="tpu_custom_call" | custom-call | flops 805306368 | bytes 62914560 | tf_op jit(solution)/shard_map/partial_rows/pallas_call | solution.py:204
  14.8 10.6 %partial_rows.2 = (f32[32,256,128]{2,1,0:T(8,128)}, f32[32,256,128]{2,1,0:T(8,128)}, f32[8,128]{1,0:T(8,128)}) custom-call(s32[1]{0:T(128)} %bitcast.137.count, s32[96]{0:T(128)} %get-tuple-element.92.targets, s32[96]{0:T(128)} %bitcast.164, bf16[96,256,256]{2,1,0:T(8,128)(2,1)} %bitcast.145, bf16[128,256,128]{2,1,0:T(8,128)(2,1)} %bitcast.148), custom_call_target="tpu_custom_call" | custom-call | flops 805306368 | bytes 62914560 | tf_op jit(solution)/shard_map/partial_rows/pallas_call | solution.py:204
  26.3 4.5 %fusion.1 = (f16[16,256,128]{2,1,0:T(8,128)(2,1)S(1)}, f16[16,256,128]{2,1,0:T(8,128)(2,1)S(1)}) fusion(f32[32,256,128]{2,1,0:T(8,128)} %collective-permute-done.2, f32[32,256,128]{2,1,0:T(8,128)} %get-tuple-element.48, f32[]{:T(128)S(1)} %bitcast.173), kind=kLoop, calls=%fused_computation.4 | loop fusion | flops 3145728 | bytes 10485764 | tf_op jit(solution)/shard_map/convert_element_type | solution.py:331
  38.6 2.8 %slice_add_fusion.2 = (f32[2048,128]{1,0:T(8,128)S(1)}, f32[2048,128]{1,0:T(8,128)S(1)}, f32[2048,128]{1,0:T(8,128)S(1)}, f32[2048,128]{1,0:T(8,128)S(1)}) fusion(f32[8192,128]{1,0:T(8,128)} %bitcast.7, f32[8192,128]{1,0:T(8,128)S(1)} %bitcast.149), kind=kLoop, calls=%fused_computation.25 | loop fusion | flops 1048576 | bytes 12582912 | tf_op jit(solution)/shard_map/add | solution.py:456
  41.6 6.3 %collective-permute-start.12 = (f32[8,128]{1,0:T(8,128)S(1)}, f32[8,128]{1,0:T(8,128)S(1)}, u32[]{:S(2)}, u32[]{:S(2)}) collective-permute-start(f32[8,128]{1,0:T(8,128)S(1)} %max.84), channel_id=1, source_target_pairs={{0,32},{8,40},{16,48},{24,56},{32,64},{40,72},{48,80},{56,88},{64,... | collective-permute-start | bytes 12296 | tf_op jit(solution)/shard_map/ppermute | solution.py:411
  47.9 2.6 %collective-permute-start.13 = (f32[8,128]{1,0:T(8,128)S(1)}, f32[8,128]{1,0:T(8,128)S(1)}, u32[]{:S(2)}, u32[]{:S(2)}) collective-permute-start(f32[8,128]{1,0:T(8,128)S(1)} %max.84), channel_id=1, source_target_pairs={{0,96},{8,104},{16,112},{24,120},{32,0},{40,8},{48,16},{56,24},{64... | collective-permute-start | bytes 12296 | tf_op jit(solution)/shard_map/ppermute | solution.py:411
  52.1 3.2 %collective-permute-start.14 = (f32[8,128]{1,0:T(8,128)S(1)}, f32[8,128]{1,0:T(8,128)S(1)}, u32[]{:S(2)}, u32[]{:S(2)}) collective-permute-start(f32[8,128]{1,0:T(8,128)S(1)} %maximum_maximum_fusion.1), channel_id=1, source_target_pairs={{0,16},{8,24},{16,0},{24,8},{32,48},{40,56},{48,32},{56,40},{64,80... | collective-permute-start | bytes 12296 | tf_op jit(solution)/shard_map/ppermute | solution.py:414
  55.6 2.9 %collective-permute-start.16 = (f32[8,128]{1,0:T(8,128)S(1)}, f32[8,128]{1,0:T(8,128)S(1)}, u32[]{:S(2)}, u32[]{:S(2)}) collective-permute-start(f32[8,128]{1,0:T(8,128)S(1)} %maximum_maximum_fusion.1), channel_id=1, source_target_pairs={{0,24},{8,0},{16,8},{24,16},{32,56},{40,32},{48,40},{56,48},{64,88... | collective-permute-start | bytes 12296 | tf_op jit(solution)/shard_map/ppermute | solution.py:414
  58.5 3.2 %collective-permute-done.7 = f16[4096,128]{1,0:T(8,128)(2,1)S(1)} collective-permute-done((f16[4096,128]{1,0:T(8,128)(2,1)S(1)}, f16[4096,128]{1,0:T(8,128)(2,1)S(1)}, u32[]{:S(2)}, u32[]{:S(2)}) %collective-permute-start.7) | collective-permute-done | bytes 1048608 | tf_op jit(solution)/shard_map/ppermute | solution.py:408
  62.2 2.8 %collective-permute-start.8 = (f16[2048,128]{1,0:T(8,128)(2,1)S(1)}, f16[2048,128]{1,0:T(8,128)(2,1)S(1)}, u32[]{:S(2)}, u32[]{:S(2)}) collective-permute-start(f16[2048,128]{1,0:T(8,128)(2,1)S(1)} %multiply_convert_fusion.7), channel_id=1, source_target_pairs={{0,2},{1,3},{2,4},{3,5},{4,6},{5,7},{6,0},{7,1},{8,10},{9,11},{10,... | collective-permute-start | bytes 1572872 | tf_op jit(solution)/shard_map/ppermute | solution.py:408
  65.1 11.1 %collective-permute-done.8 = f16[2048,128]{1,0:T(8,128)(2,1)S(1)} collective-permute-done((f16[2048,128]{1,0:T(8,128)(2,1)S(1)}, f16[2048,128]{1,0:T(8,128)(2,1)S(1)}, u32[]{:S(2)}, u32[]{:S(2)}) %collective-permute-start.8) | collective-permute-done | bytes 524320 | tf_op jit(solution)/shard_map/ppermute | solution.py:408
  76.2 3.4 %collective-permute-done.9 = f16[2048,128]{1,0:T(8,128)(2,1)S(1)} collective-permute-done((f16[2048,128]{1,0:T(8,128)(2,1)S(1)}, f16[2048,128]{1,0:T(8,128)(2,1)S(1)}, u32[]{:S(2)}, u32[]{:S(2)}) %collective-permute-start.9) | collective-permute-done | bytes 524320 | tf_op jit(solution)/shard_map/ppermute | solution.py:408
  80.7 2.4 abs_reduce_fusion.1
  85.6 40.8 %all-gather.1.gathered.table = s16[35072,128]{1,0:T(8,128)(2,1)} all-gather(s16[4384,128]{1,0:T(8,128)(2,1)S(1)} %pad_add_fusion), channel_id=1, replica_groups=mesh['row'=16,'col'=8] {'col'}, dimensions={0}, use_global_device_ids=true | all-gather | bytes 10100736 | tf_op jit(solution)/shard_map/all_gather | solution.py:488
  129.4 2.6 %collective-permute-start.19 = (f32[128,128]{1,0:T(8,128)}, f32[128,128]{1,0:T(8,128)S(1)}, u32[]{:S(2)}, u32[]{:S(2)}) collective-permute-start(f32[128,128]{1,0:T(8,128)} %get-tuple-element.68), channel_id=1, source_target_pairs={{0,96},{8,104},{16,112},{24,120},{32,0},{40,8},{48,16},{56,24},{64... | collective-permute-start | bytes 196616 | tf_op jit(solution)/shard_map/ppermute | solution.py:411
  132.0 13.2 %partial_cols.1 = (f32[16,256,128]{2,1,0:T(8,128)}, f32[16,256,128]{2,1,0:T(8,128)}, f32[16,256,128]{2,1,0:T(8,128)}, f32[4,256,128]{2,1,0:T(8,128)}, f32[4,256,...) custom-call(s32[1]{0:T(128)} %bitcast.139.count, ...), custom_call_target="tpu_custom_call" | custom-call | flops 3221225472 | bytes 44040192 | tf_op jit(solution)/shard_map/partial_cols/pallas_call | solution.py:304
  145.3 3.0 %multiply_convert_fusion.5 = f16[16,256,128]{2,1,0:T(8,128)(2,1)} fusion(f32[16,256,128]{2,1,0:T(8,128)} %get-tuple-element.71, f32[]{:T(128)S(1)} %bitcast.153), kind=kLoop, calls=%fused_computation.14 | loop fusion | flops 1048576 | bytes 3145732 | tf_op jit(solution)/shard_map/convert_element_type | solution.py:331
  148.3 3.7 %collective-permute-start.23 = (f16[4096,128]{1,0:T(8,128)(2,1)}, f16[4096,128]{1,0:T(8,128)(2,1)S(1)}, u32[]{:S(2)}, u32[]{:S(2)}) collective-permute-start(f16[4096,128]{1,0:T(8,128)(2,1)} %bitcast.21), channel_id=1, source_target_pairs={{0,32},{8,40},{16,48},{24,56},{32,64},{40,72},{48,80},{56,88},{64,... | collective-permute-start | bytes 3145736 | tf_op jit(solution)/shard_map/ppermute | solution.py:411
  153.4 9.7 %collective-permute-start.20 = (f32[128,128]{1,0:T(8,128)S(1)}, f32[128,128]{1,0:T(8,128)S(1)}, u32[]{:S(2)}, u32[]{:S(2)}) collective-permute-start(f32[128,128]{1,0:T(8,128)S(1)} %add_add_fusion.1), channel_id=1, source_target_pairs={{0,16},{8,24},{16,0},{24,8},{32,48},{40,56},{48,32},{56,40},{64,80... | collective-permute-start | bytes 196616 | tf_op jit(solution)/shard_map/ppermute | solution.py:414
  163.1 3.2 %collective-permute-start.22 = (f32[128,128]{1,0:T(8,128)S(1)}, f32[128,128]{1,0:T(8,128)S(1)}, u32[]{:S(2)}, u32[]{:S(2)}) collective-permute-start(f32[128,128]{1,0:T(8,128)S(1)} %add_add_fusion.1), channel_id=1, source_target_pairs={{0,24},{8,0},{16,8},{24,16},{32,56},{40,32},{48,40},{56,48},{64,88... | collective-permute-start | bytes 196616 | tf_op jit(solution)/shard_map/ppermute | solution.py:414
  169.9 3.0 %multiply_convert_fusion.2 = f16[16,256,128]{2,1,0:T(8,128)(2,1)} fusion(f32[16,256,128]{2,1,0:T(8,128)} %get-tuple-element.80, f32[]{:T(128)S(6)} %add.254), kind=kLoop, calls=%fused_computation.11 | loop fusion | flops 1048576 | bytes 3145732 | tf_op jit(solution)/shard_map/convert_element_type | solution.py:331
  174.2 3.2 %collective-permute-start.30 = (f16[4096,128]{1,0:T(8,128)(2,1)}, f16[4096,128]{1,0:T(8,128)(2,1)}, u32[]{:S(2)}, u32[]{:S(2)}) collective-permute-start(f16[4096,128]{1,0:T(8,128)(2,1)} %bitcast.31), channel_id=1, source_target_pairs={{0,24},{8,0},{16,8},{24,16},{32,56},{40,32},{48,40},{56,48},{64,88... | collective-permute-start | bytes 3145736 | tf_op jit(solution)/shard_map/ppermute | solution.py:414
  178.7 18.8 %collective-permute-done.23 = f16[4096,128]{1,0:T(8,128)(2,1)S(1)} collective-permute-done((f16[4096,128]{1,0:T(8,128)(2,1)}, f16[4096,128]{1,0:T(8,128)(2,1)S(1)}, u32[]{:S(2)}, u32[]{:S(2)}) %collective-permute-start.23) | collective-permute-done | bytes 1048608 | tf_op jit(solution)/shard_map/ppermute | solution.py:411
  197.5 9.7 %collective-permute-start.31 = (f16[4096,128]{1,0:T(8,128)(2,1)}, f16[4096,128]{1,0:T(8,128)(2,1)}, u32[]{:S(2)}, u32[]{:S(2)}) collective-permute-start(f16[4096,128]{1,0:T(8,128)(2,1)} %bitcast.32), channel_id=1, source_target_pairs={{0,16},{8,24},{16,0},{24,8},{32,48},{40,56},{48,32},{56,40},{64,80... | collective-permute-start | bytes 3145736 | tf_op jit(solution)/shard_map/ppermute | solution.py:414
  207.2 11.7 %cholesky.17 = f32[128,128]{1,0:T(8,128)S(1)} custom-call(f32[128,128]{1,0:T(8,128)S(1)} %fusion.45), custom_call_target="Cholesky" | custom-call | tf_op jit(solution)/shard_map/jit(cholesky)/cholesky | solution.py:500
  220.3 9.8 %custom-call.6 = f32[1,128,128]{1,2,0:T(8,128)S(1)} custom-call(f32[1,128,128]{2,1,0:T(8,128)S(1)} %fusion.42), custom_call_target="InvertDiagBlocksLowerTriangular" | custom-call | tf_op jit(solution)/shard_map/triangular_solve | solution.py:501
  230.5 3.3 %fusion.32 = (f16[1024,128]{1,0:T(8,128)(2,1)}, f16[1024,128]{1,0:T(8,128)(2,1)S(1)}, f16[1024,128]{1,0:T(8,128)(2,1)S(1)}) fusion(f32[4,256,128]{2,1,0:T(8,128)} %get-tuple-element.77, f16[4096,128]{1,0:T(8,128)(2,1)} %collective-permute-done.25, f16[4096,128]{1,0:T(8,128)(2,1)} %collective-permute-done.24, ...), kind=kLoop, calls=%fused_computation.60 | loop fusion | flops 4325376 | bytes 4718600 | tf_op jit(solution)/shard_map/convert_element_type | solution.py:331
  233.7 3.2 %collective-permute-start.27 = (f16[1024,128]{1,0:T(8,128)(2,1)}, f16[1024,128]{1,0:T(8,128)(2,1)}, u32[]{:S(2)}, u32[]{:S(2)}) collective-permute-start(f16[1024,128]{1,0:T(8,128)(2,1)} %get-tuple-element.100), channel_id=1, source_target_pairs={{0,24},{8,0},{16,8},{24,16},{32,56},{40,32},{48,40},{56,48},{64,88... | collective-permute-start | bytes 786440 | tf_op jit(solution)/shard_map/ppermute | solution.py:414
  237.0 3.1 %fusion.19 = (f16[1024,128]{1,0:T(8,128)(2,1)}, f16[1024,128]{1,0:T(8,128)(2,1)}, f16[1024,128]{1,0:T(8,128)(2,1)}) fusion(f32[4,256,128]{2,1,0:T(8,128)S(1)} %copy-done.5, f16[4096,128]{1,0:T(8,128)(2,1)} %collective-permute-done.31, f16[4096,128]{1,0:T(8,128)(2,1)} %collective-permute-done.30, f16[4096,128]{1,0:T(8,128)(2,1)} %collective-permute-done.29, ...), kind=kLoop, calls=%fused_computation.44 | loop fusion | flops 4325376 | bytes 4718600 | tf_op jit(solution)/shard_map/convert_element_type | solution.py:331
  240.1 3.2 %collective-permute-start.33 = (f16[1024,128]{1,0:T(8,128)(2,1)}, f16[1024,128]{1,0:T(8,128)(2,1)}, u32[]{:S(2)}, u32[]{:S(2)}) collective-permute-start(f16[1024,128]{1,0:T(8,128)(2,1)} %get-tuple-element.105), channel_id=1, source_target_pairs={{0,96},{8,104},{16,112},{24,120},{32,0},{40,8},{48,16},{56,24},{64... | collective-permute-start | bytes 786440 | tf_op jit(solution)/shard_map/ppermute | solution.py:411
  243.3 4.0 %collective-permute-done.26 = f16[1024,128]{1,0:T(8,128)(2,1)S(1)} collective-permute-done((f16[1024,128]{1,0:T(8,128)(2,1)S(1)}, f16[1024,128]{1,0:T(8,128)(2,1)S(1)}, u32[]{:S(2)}, u32[]{:S(2)}) %collective-permute-start.26) | collective-permute-done | bytes 262176 | tf_op jit(solution)/shard_map/ppermute | solution.py:414
  250.9 2.3 convolution_multiply_fusion
  (126 shorter events, 37.3 us)
Async XLA Ops:
  14.1 12.1 %collective-permute-start.2 = (f32[32,256,128]{2,1,0:T(8,128)}, f32[32,256,128]{2,1,0:T(8,128)}, u32[]{:S(2)}, u32[]{:S(2)}) collective-permute-start(f32[32,256,128]{2,1,0:T(8,128)} %get-tuple-element.49), channel_id=1, source_target_pairs={{0,1},{1,0},{2,3},{3,2},{4,5},{5,4},{6,7},{7,6},{8,9},{9,8},{10,11... | collective-permute-start | bytes 12582920 | tf_op jit(solution)/shard_map/ppermute | solution.py:405
  14.2 24.4 %collective-permute-start = (f32[32,256,128]{2,1,0:T(8,128)}, f32[32,256,128]{2,1,0:T(8,128)}, u32[]{:S(2)}, u32[]{:S(2)}) collective-permute-start(f32[32,256,128]{2,1,0:T(8,128)} %get-tuple-element.45), channel_id=1, source_target_pairs={{0,1},{1,0},{2,3},{3,2},{4,5},{5,4},{6,7},{7,6},{8,9},{9,8},{10,11... | collective-permute-start | bytes 12582920 | tf_op jit(solution)/shard_map/ppermute | solution.py:405
  14.7 10.7 %collective-permute-start.1 = (f32[8,128]{1,0:T(8,128)}, f32[8,128]{1,0:T(8,128)S(1)}, u32[]{:S(2)}, u32[]{:S(2)}) collective-permute-start(f32[8,128]{1,0:T(8,128)} %get-tuple-element.47), channel_id=1, source_target_pairs={{0,1},{1,0},{2,3},{3,2},{4,5},{5,4},{6,7},{7,6},{8,9},{9,8},{10,11... | collective-permute-start | bytes 12296 | tf_op jit(solution)/shard_map/ppermute | solution.py:405
  30.7 5.2 %collective-permute-start.3 = (f32[8,128]{1,0:T(8,128)S(1)}, f32[8,128]{1,0:T(8,128)S(1)}, u32[]{:S(2)}, u32[]{:S(2)}) collective-permute-start(f32[8,128]{1,0:T(8,128)S(1)} %get-tuple-element.50), channel_id=1, source_target_pairs={{0,4},{1,5},{2,6},{3,7},{4,0},{5,1},{6,2},{7,3},{8,12},{9,13},{10,... | collective-permute-start | bytes 12296 | tf_op jit(solution)/shard_map/ppermute | solution.py:408
  32.0 5.9 %collective-permute-start.4 = (f32[8,128]{1,0:T(8,128)S(1)}, f32[8,128]{1,0:T(8,128)S(1)}, u32[]{:S(2)}, u32[]{:S(2)}) collective-permute-start(f32[8,128]{1,0:T(8,128)S(1)} %get-tuple-element.50), channel_id=1, source_target_pairs={{0,2},{1,3},{2,4},{3,5},{4,6},{5,7},{6,0},{7,1},{8,10},{9,11},{10,... | collective-permute-start | bytes 12296 | tf_op jit(solution)/shard_map/ppermute | solution.py:408
  34.6 27.1 %collective-permute-start.7 = (f16[4096,128]{1,0:T(8,128)(2,1)S(1)}, f16[4096,128]{1,0:T(8,128)(2,1)S(1)}, u32[]{:S(2)}, u32[]{:S(2)}) collective-permute-start(f16[4096,128]{1,0:T(8,128)(2,1)S(1)} %bitcast.151), channel_id=1, source_target_pairs={{0,6},{1,7},{2,0},{3,1},{4,2},{5,3},{6,4},{7,5},{8,14},{9,15},{10,... | collective-permute-start | bytes 3145736 | tf_op jit(solution)/shard_map/ppermute | solution.py:408
  35.9 26.1 %collective-permute-start.6 = (f16[4096,128]{1,0:T(8,128)(2,1)S(1)}, f16[4096,128]{1,0:T(8,128)(2,1)S(1)}, u32[]{:S(2)}, u32[]{:S(2)}) collective-permute-start(f16[4096,128]{1,0:T(8,128)(2,1)S(1)} %bitcast.150), channel_id=1, source_target_pairs={{0,2},{1,3},{2,4},{3,5},{4,6},{5,7},{6,0},{7,1},{8,10},{9,11},{10,... | collective-permute-start | bytes 3145736 | tf_op jit(solution)/shard_map/ppermute | solution.py:408
  41.5 9.0 %collective-permute-start.11 = (f32[8,128]{1,0:T(8,128)S(1)}, f32[8,128]{1,0:T(8,128)S(1)}, u32[]{:S(2)}, u32[]{:S(2)}) collective-permute-start(f32[8,128]{1,0:T(8,128)S(1)} %max.84), channel_id=1, source_target_pairs={{0,64},{8,72},{16,80},{24,88},{32,96},{40,104},{48,112},{56,120},{... | collective-permute-start | bytes 12296 | tf_op jit(solution)/shard_map/ppermute | solution.py:411
  41.6 10.5 %collective-permute-start.12 = (f32[8,128]{1,0:T(8,128)S(1)}, f32[8,128]{1,0:T(8,128)S(1)}, u32[]{:S(2)}, u32[]{:S(2)}) collective-permute-start(f32[8,128]{1,0:T(8,128)S(1)} %max.84), channel_id=1, source_target_pairs={{0,32},{8,40},{16,48},{24,56},{32,64},{40,72},{48,80},{56,88},{64,... | collective-permute-start | bytes 12296 | tf_op jit(solution)/shard_map/ppermute | solution.py:411
  52.1 12.9 %collective-permute-start.14 = (f32[8,128]{1,0:T(8,128)S(1)}, f32[8,128]{1,0:T(8,128)S(1)}, u32[]{:S(2)}, u32[]{:S(2)}) collective-permute-start(f32[8,128]{1,0:T(8,128)S(1)} %maximum_maximum_fusion.1), channel_id=1, source_target_pairs={{0,16},{8,24},{16,0},{24,8},{32,48},{40,56},{48,32},{56,40},{64,80... | collective-permute-start | bytes 12296 | tf_op jit(solution)/shard_map/ppermute | solution.py:414
  55.3 9.7 %collective-permute-start.15 = (f32[8,128]{1,0:T(8,128)S(1)}, f32[8,128]{1,0:T(8,128)S(1)}, u32[]{:S(2)}, u32[]{:S(2)}) collective-permute-start(f32[8,128]{1,0:T(8,128)S(1)} %maximum_maximum_fusion.1), channel_id=1, source_target_pairs={{0,8},{8,16},{16,24},{24,0},{32,40},{40,48},{48,56},{56,32},{64,72... | collective-permute-start | bytes 12296 | tf_op jit(solution)/shard_map/ppermute | solution.py:414
  55.6 9.4 %collective-permute-start.16 = (f32[8,128]{1,0:T(8,128)S(1)}, f32[8,128]{1,0:T(8,128)S(1)}, u32[]{:S(2)}, u32[]{:S(2)}) collective-permute-start(f32[8,128]{1,0:T(8,128)S(1)} %maximum_maximum_fusion.1), channel_id=1, source_target_pairs={{0,24},{8,0},{16,8},{24,16},{32,56},{40,32},{48,40},{56,48},{64,88... | collective-permute-start | bytes 12296 | tf_op jit(solution)/shard_map/ppermute | solution.py:414
  62.2 13.9 %collective-permute-start.8 = (f16[2048,128]{1,0:T(8,128)(2,1)S(1)}, f16[2048,128]{1,0:T(8,128)(2,1)S(1)}, u32[]{:S(2)}, u32[]{:S(2)}) collective-permute-start(f16[2048,128]{1,0:T(8,128)(2,1)S(1)} %multiply_convert_fusion.7), channel_id=1, source_target_pairs={{0,2},{1,3},{2,4},{3,5},{4,6},{5,7},{6,0},{7,1},{8,10},{9,11},{10,... | collective-permute-start | bytes 1572872 | tf_op jit(solution)/shard_map/ppermute | solution.py:408
  65.0 14.6 %collective-permute-start.9 = (f16[2048,128]{1,0:T(8,128)(2,1)S(1)}, f16[2048,128]{1,0:T(8,128)(2,1)S(1)}, u32[]{:S(2)}, u32[]{:S(2)}) collective-permute-start(f16[2048,128]{1,0:T(8,128)(2,1)S(1)} %multiply_convert_fusion.6), channel_id=1, source_target_pairs={{0,6},{1,7},{2,0},{3,1},{4,2},{5,3},{6,4},{7,5},{8,14},{9,15},{10,... | collective-permute-start | bytes 1572872 | tf_op jit(solution)/shard_map/ppermute | solution.py:408
  128.3 25.0 %collective-permute-start.17 = (f32[128,128]{1,0:T(8,128)}, f32[128,128]{1,0:T(8,128)S(1)}, u32[]{:S(2)}, u32[]{:S(2)}) collective-permute-start(f32[128,128]{1,0:T(8,128)} %get-tuple-element.68), channel_id=1, source_target_pairs={{0,64},{8,72},{16,80},{24,88},{32,96},{40,104},{48,112},{56,120},{... | collective-permute-start | bytes 196616 | tf_op jit(solution)/shard_map/ppermute | solution.py:411
  128.4 24.9 %collective-permute-start.18 = (f32[128,128]{1,0:T(8,128)}, f32[128,128]{1,0:T(8,128)S(1)}, u32[]{:S(2)}, u32[]{:S(2)}) collective-permute-start(f32[128,128]{1,0:T(8,128)} %get-tuple-element.68), channel_id=1, source_target_pairs={{0,32},{8,40},{16,48},{24,56},{32,64},{40,72},{48,80},{56,88},{64,... | collective-permute-start | bytes 196616 | tf_op jit(solution)/shard_map/ppermute | solution.py:411
  129.4 23.9 %collective-permute-start.19 = (f32[128,128]{1,0:T(8,128)}, f32[128,128]{1,0:T(8,128)S(1)}, u32[]{:S(2)}, u32[]{:S(2)}) collective-permute-start(f32[128,128]{1,0:T(8,128)} %get-tuple-element.68), channel_id=1, source_target_pairs={{0,96},{8,104},{16,112},{24,120},{32,0},{40,8},{48,16},{56,24},{64... | collective-permute-start | bytes 196616 | tf_op jit(solution)/shard_map/ppermute | solution.py:411
  148.3 49.1 %collective-permute-start.23 = (f16[4096,128]{1,0:T(8,128)(2,1)}, f16[4096,128]{1,0:T(8,128)(2,1)S(1)}, u32[]{:S(2)}, u32[]{:S(2)}) collective-permute-start(f16[4096,128]{1,0:T(8,128)(2,1)} %bitcast.21), channel_id=1, source_target_pairs={{0,32},{8,40},{16,48},{24,56},{32,64},{40,72},{48,80},{56,88},{64,... | collective-permute-start | bytes 3145736 | tf_op jit(solution)/shard_map/ppermute | solution.py:411
  153.3 77.1 %collective-permute-start.24 = (f16[4096,128]{1,0:T(8,128)(2,1)}, f16[4096,128]{1,0:T(8,128)(2,1)}, u32[]{:S(2)}, u32[]{:S(2)}) collective-permute-start(f16[4096,128]{1,0:T(8,128)(2,1)} %bitcast.22), channel_id=1, source_target_pairs={{0,96},{8,104},{16,112},{24,120},{32,0},{40,8},{48,16},{56,24},{64... | collective-permute-start | bytes 3145736 | tf_op jit(solution)/shard_map/ppermute | solution.py:411
  153.4 14.2 %collective-permute-start.20 = (f32[128,128]{1,0:T(8,128)S(1)}, f32[128,128]{1,0:T(8,128)S(1)}, u32[]{:S(2)}, u32[]{:S(2)}) collective-permute-start(f32[128,128]{1,0:T(8,128)S(1)} %add_add_fusion.1), channel_id=1, source_target_pairs={{0,16},{8,24},{16,0},{24,8},{32,48},{40,56},{48,32},{56,40},{64,80... | collective-permute-start | bytes 196616 | tf_op jit(solution)/shard_map/ppermute | solution.py:414
  163.1 5.5 %collective-permute-start.21 = (f32[128,128]{1,0:T(8,128)S(1)}, f32[128,128]{1,0:T(8,128)S(1)}, u32[]{:S(2)}, u32[]{:S(2)}) collective-permute-start(f32[128,128]{1,0:T(8,128)S(1)} %add_add_fusion.1), channel_id=1, source_target_pairs={{0,8},{8,16},{16,24},{24,0},{32,40},{40,48},{48,56},{56,32},{64,72... | collective-permute-start | bytes 196616 | tf_op jit(solution)/shard_map/ppermute | solution.py:414
  163.1 5.5 %collective-permute-start.22 = (f32[128,128]{1,0:T(8,128)S(1)}, f32[128,128]{1,0:T(8,128)S(1)}, u32[]{:S(2)}, u32[]{:S(2)}) collective-permute-start(f32[128,128]{1,0:T(8,128)S(1)} %add_add_fusion.1), channel_id=1, source_target_pairs={{0,24},{8,0},{16,8},{24,16},{32,56},{40,32},{48,40},{56,48},{64,88... | collective-permute-start | bytes 196616 | tf_op jit(solution)/shard_map/ppermute | solution.py:414
  167.6 62.8 %collective-permute-start.25 = (f16[4096,128]{1,0:T(8,128)(2,1)}, f16[4096,128]{1,0:T(8,128)(2,1)}, u32[]{:S(2)}, u32[]{:S(2)}) collective-permute-start(f16[4096,128]{1,0:T(8,128)(2,1)} %bitcast.23), channel_id=1, source_target_pairs={{0,64},{8,72},{16,80},{24,88},{32,96},{40,104},{48,112},{56,120},{... | collective-permute-start | bytes 3145736 | tf_op jit(solution)/shard_map/ppermute | solution.py:411
  172.9 64.1 %collective-permute-start.29 = (f16[4096,128]{1,0:T(8,128)(2,1)}, f16[4096,128]{1,0:T(8,128)(2,1)}, u32[]{:S(2)}, u32[]{:S(2)}) collective-permute-start(f16[4096,128]{1,0:T(8,128)(2,1)} %bitcast.30), channel_id=1, source_target_pairs={{0,8},{8,16},{16,24},{24,0},{32,40},{40,48},{48,56},{56,32},{64,72... | collective-permute-start | bytes 3145736 | tf_op jit(solution)/shard_map/ppermute | solution.py:414
  174.2 62.8 %collective-permute-start.30 = (f16[4096,128]{1,0:T(8,128)(2,1)}, f16[4096,128]{1,0:T(8,128)(2,1)}, u32[]{:S(2)}, u32[]{:S(2)}) collective-permute-start(f16[4096,128]{1,0:T(8,128)(2,1)} %bitcast.31), channel_id=1, source_target_pairs={{0,24},{8,0},{16,8},{24,16},{32,56},{40,32},{48,40},{56,48},{64,88... | collective-permute-start | bytes 3145736 | tf_op jit(solution)/shard_map/ppermute | solution.py:414
  197.5 39.5 %collective-permute-start.31 = (f16[4096,128]{1,0:T(8,128)(2,1)}, f16[4096,128]{1,0:T(8,128)(2,1)}, u32[]{:S(2)}, u32[]{:S(2)}) collective-permute-start(f16[4096,128]{1,0:T(8,128)(2,1)} %bitcast.32), channel_id=1, source_target_pairs={{0,16},{8,24},{16,0},{24,8},{32,48},{40,56},{48,32},{56,40},{64,80... | collective-permute-start | bytes 3145736 | tf_op jit(solution)/shard_map/ppermute | solution.py:414
  233.7 13.6 %collective-permute-start.26 = (f16[1024,128]{1,0:T(8,128)(2,1)S(1)}, f16[1024,128]{1,0:T(8,128)(2,1)S(1)}, u32[]{:S(2)}, u32[]{:S(2)}) collective-permute-start(f16[1024,128]{1,0:T(8,128)(2,1)S(1)} %get-tuple-element.102), channel_id=1, source_target_pairs={{0,8},{8,16},{16,24},{24,0},{32,40},{40,48},{48,56},{56,32},{64,72... | collective-permute-start | bytes 786440 | tf_op jit(solution)/shard_map/ppermute | solution.py:414
  233.7 15.4 %collective-permute-start.27 = (f16[1024,128]{1,0:T(8,128)(2,1)}, f16[1024,128]{1,0:T(8,128)(2,1)}, u32[]{:S(2)}, u32[]{:S(2)}) collective-permute-start(f16[1024,128]{1,0:T(8,128)(2,1)} %get-tuple-element.100), channel_id=1, source_target_pairs={{0,24},{8,0},{16,8},{24,16},{32,56},{40,32},{48,40},{56,48},{64,88... | collective-permute-start | bytes 786440 | tf_op jit(solution)/shard_map/ppermute | solution.py:414
  237.0 12.2 %collective-permute-start.28 = (f16[1024,128]{1,0:T(8,128)(2,1)S(1)}, f16[1024,128]{1,0:T(8,128)(2,1)}, u32[]{:S(2)}, u32[]{:S(2)}) collective-permute-start(f16[1024,128]{1,0:T(8,128)(2,1)S(1)} %get-tuple-element.101), channel_id=1, source_target_pairs={{0,16},{8,24},{16,0},{24,8},{32,48},{40,56},{48,32},{56,40},{64,80... | collective-permute-start | bytes 786440 | tf_op jit(solution)/shard_map/ppermute | solution.py:414
  240.1 13.2 %collective-permute-start.32 = (f16[1024,128]{1,0:T(8,128)(2,1)}, f16[1024,128]{1,0:T(8,128)(2,1)}, u32[]{:S(2)}, u32[]{:S(2)}) collective-permute-start(f16[1024,128]{1,0:T(8,128)(2,1)} %get-tuple-element.103), channel_id=1, source_target_pairs={{0,32},{8,40},{16,48},{24,56},{32,64},{40,72},{48,80},{56,88},{64,... | collective-permute-start | bytes 786440 | tf_op jit(solution)/shard_map/ppermute | solution.py:411
  240.1 13.2 %collective-permute-start.33 = (f16[1024,128]{1,0:T(8,128)(2,1)}, f16[1024,128]{1,0:T(8,128)(2,1)}, u32[]{:S(2)}, u32[]{:S(2)}) collective-permute-start(f16[1024,128]{1,0:T(8,128)(2,1)} %get-tuple-element.105), channel_id=1, source_target_pairs={{0,96},{8,104},{16,112},{24,120},{32,0},{40,8},{48,16},{56,24},{64... | collective-permute-start | bytes 786440 | tf_op jit(solution)/shard_map/ppermute | solution.py:411
  247.4 8.2 %collective-permute-start.34 = (f16[1024,128]{1,0:T(8,128)(2,1)}, f16[1024,128]{1,0:T(8,128)(2,1)}, u32[]{:S(2)}, u32[]{:S(2)}) collective-permute-start(f16[1024,128]{1,0:T(8,128)(2,1)} %get-tuple-element.104), channel_id=1, source_target_pairs={{0,64},{8,72},{16,80},{24,88},{32,96},{40,104},{48,112},{56,120},{... | collective-permute-start | bytes 786440 | tf_op jit(solution)/shard_map/ppermute | solution.py:411
  (16 other events, 105.1 us)

commit v5 on v1

--- a/solution.py
+++ b/solution.py
@@ -40,36 +40,10 @@
 PAIR = [(c, c ^ 1) for c in range(8)]
 
 
-def run_slots(parts, count, targets, order, bounds, begin, group, carry, total_sum, outs, out_sems):
+def run_slots(parts, ends, begin, group, carry, total_sum, outs, out_sems):
     chunks = total_sum.shape[0] // CHUNK
 
-    def chunk_of(s):
-        return jnp.where(targets[s] < 0, chunks, targets[s] // CHUNK)
-
-    for c in range(chunks + 1):
-        bounds[c] = 0
-
-    def tally(s, _):
-        c = chunk_of(s)
-        bounds[c] = bounds[c] + 1
-        return 0
-
-    lax.fori_loop(0, count, tally, 0)
-    total = 0
-    for c in range(chunks):
-        here = bounds[c]
-        bounds[c] = total
-        total = total + here
-    bounds[chunks] = total
-
-    def place(s, _):
-        c = chunk_of(s)
-        at = bounds[c]
-        order[at] = s
-        bounds[c] = at + 1
-        return 0
-
-    lax.fori_loop(0, count, place, 0)
+    total = ends[chunks - 1]
 
     def begin_later(j):
         @pl.when(j < total)
@@ -113,7 +87,7 @@
             return c + 1
 
         return lax.while_loop(
-            lambda c: (c < chunks) & (bounds[jnp.minimum(c, chunks - 1)] <= done), step, chunk
+            lambda c: (c < chunks) & (ends[jnp.minimum(c, chunks - 1)] <= done), step, chunk
         )
 
     def by_group(size, first):
@@ -135,9 +109,40 @@
     return state[1]
 
 
+def sort_slots(count, targets, chunks, order, bounds):
+    def chunk_of(s):
+        return jnp.where(targets[s] < 0, chunks, targets[s] // CHUNK)
+
+    for c in range(chunks + 1):
+        bounds[c] = 0
+
+    def tally(s, _):
+        c = chunk_of(s)
+        bounds[c] = bounds[c] + 1
+        return 0
+
+    lax.fori_loop(0, count, tally, 0)
+    total = 0
+    for c in range(chunks):
+        here = bounds[c]
+        bounds[c] = total
+        total = total + here
+    bounds[chunks] = total
+
+    def place(s, _):
+        c = chunk_of(s)
+        at = bounds[c]
+        order[at] = s
+        bounds[c] = at + 1
+        return 0
+
+    lax.fori_loop(0, count, place, 0)
+
+
 def y_kernel(count, targets, cols, blocks, sketch, *rest):
     outs, stat, scratch = rest[:3], rest[3], rest[4:]
-    total_sum, order, bounds, block_buf, sketch_buf, sems, out_sems = scratch
+    total_sum, block_buf, sketch_buf, sems, out_sems, order, ends = scratch
+    sort_slots(count[0], targets, 8, order, ends)
 
     def copies(j):
         s, at = order[j], lax.rem(j, BUFFERS)
@@ -174,7 +179,7 @@
 
     carry = jnp.zeros((8, K), f32), jnp.zeros((16, B), jnp.bfloat16)
     largest, largest_block = run_slots(
-        Y_PARTS, count[0], targets, order, bounds, begin, group, carry, total_sum, outs, out_sems
+        Y_PARTS, ends, begin, group, carry, total_sum, outs, out_sems
     )
     stat[:4] = jnp.full((4, K), jnp.max(largest))
     stat[4:] = jnp.full((4, K), jnp.max(largest_block.astype(f32)))
@@ -191,8 +196,6 @@
 def scratch_for(halves, parts, y_type):
     return [
         pltpu.VMEM((halves * 8 * CHUNK, B, K), f32),
-        pltpu.SMEM((NBLK + 1,), jnp.int32),
-        pltpu.SMEM((halves * 8 + 1,), jnp.int32),
         pltpu.VMEM((BUFFERS, B, B), jnp.bfloat16),
         pltpu.VMEM((BUFFERS, B, K), y_type),
         pltpu.SemaphoreType.DMA((2, BUFFERS)),
@@ -208,7 +211,8 @@
         + [pl.BlockSpec(memory_space=pl.ANY)] * 2,
         out_specs=(pl.BlockSpec(memory_space=pl.ANY),) * 3
         + (pl.BlockSpec(memory_space=pltpu.VMEM),),
-        scratch_shapes=scratch_for(1, Y_PARTS, jnp.bfloat16),
+        scratch_shapes=scratch_for(1, Y_PARTS, jnp.bfloat16)
+        + [pltpu.SMEM((NBLK + 1,), jnp.int32), pltpu.SMEM((9,), jnp.int32)],
         compiler_params=pltpu.CompilerParams(vmem_limit_bytes=VMEM_BYTES),
         cost_estimate=pl.CostEstimate(
             flops=NBLK * B * B * K, bytes_accessed=60 * 1024 * 1024, transcendentals=0
@@ -255,9 +259,9 @@
     )(gathered)
 
 
-def z_kernel(count, targets, rows, blocks, table, tile_scales, *rest):
+def z_kernel(order, ends, targets, rows, blocks, table, tile_scales, *rest):
     outs, scratch = rest[:16], rest[16:]
-    total_sum, order, bounds, block_buf, y_buf, sems, out_sems = scratch
+    total_sum, block_buf, y_buf, sems, out_sems = scratch
 
     def copies(j):
         s, at = order[j], lax.rem(j, BUFFERS)
@@ -296,15 +300,15 @@
         return carry
 
     run_slots(
-        Z_PARTS, count[0], targets, order, bounds, begin, group, 0, total_sum, outs, out_sems
-    )
-
-
-def partial_cols(count, targets, rows, blocks, table, tile_scales):
+        Z_PARTS, ends, begin, group, 0, total_sum, outs, out_sems
+    )
+
+
+def partial_cols(plan, rows, blocks, table, tile_scales):
     return pl.pallas_call(
         z_kernel,
         out_shape=sums_of(Z_PARTS * 2),
-        in_specs=[pl.BlockSpec(memory_space=pltpu.SMEM)] * 3
+        in_specs=[pl.BlockSpec(memory_space=pltpu.SMEM)] * 4
         + [pl.BlockSpec(memory_space=pl.ANY)] * 2
         + [pl.BlockSpec(memory_space=pltpu.VMEM)],
         out_specs=(pl.BlockSpec(memory_space=pl.ANY),) * 16,
@@ -314,7 +318,7 @@
             flops=NBLK * B * B * K * 4, bytes_accessed=42 * 1024 * 1024, transcendentals=0
         ),
         name="partial_cols",
-    )(count, targets, rows, blocks, table, tile_scales)
+    )(*plan, rows, blocks, table, tile_scales)
 
 
 def scales_for(bound):
@@ -430,6 +434,7 @@
     other_target = jnp.where(live & (row_core != core), y_target, -1)
     own_target = jnp.where(live & (row_core == core), y_target, -1)
     z_target = jnp.where(live, z_target, -1)
+
     count = count[None]
 
     def flat(values):
@@ -458,6 +463,16 @@
     around = scales_for(below[:1]), scales_for(above[:1])
     sum_scales = scales_for(bounds[:1] * 4.0)
     received, sums, messages = ring_second(received, passing, send_y, sum_scales, *around)
+    z_target = after(z_target, staying[0])
+    chunk = jnp.where(z_target < 0, 16, z_target // CHUNK)
+    slot = jnp.arange(NBLK, dtype=jnp.int32)
+    key = chunk * NBLK + slot
+    rank = jnp.sum((key[None, :] < key[:, None]).astype(jnp.int32), axis=1)
+    order = jnp.sum(jnp.where(rank[None, :] == slot[:, None], slot[None, :], 0), axis=1)
+    ends = jnp.arange(16, dtype=jnp.int32)
+    ends = jnp.sum((chunk[None, :] <= ends[:, None]).astype(jnp.int32), axis=1)
+    z_plan = order, ends, z_target
+
     y_part = ring_total(received, sums, [[v] for v in staying], sum_scales, *around)
     y_share = jnp.concatenate([y_part(0), y_part(1)], axis=0)
 
@@ -486,7 +501,7 @@
     gathered = lax.all_gather(mine, "col", axis=0, tiled=True)
     gram, tile_scales = read_shares(gathered)
     gram = ring_fold(by_rows(gram), send_x, jnp.add)[0]
-    partial = flat(partial_cols(count, z_target, rows, blocks, gathered, tile_scales))
+    partial = flat(partial_cols(z_plan, rows, blocks, gathered, tile_scales))
     gram = by_rows(ring_fold(gram, send_z, jnp.add)[0])
 
     rings = [(partial[:8], send_x, send_z), (partial[8:], send_z, send_x)]

time: 244 us -> 244 us (level)
  waiting for transfers between devices: 31.7 us -> 24.5 us
  starting transfers between devices: 50.8 us -> 57.3 us
  Pallas kernels: 44.5 us -> 39.2 us
  other arithmetic: 59.6 us -> 63.8 us
    ppermute x13, starting transfers between devices: 20.1 us -> 28.5 us  [send_z(): return lax.ppermute(value, 'row', along_z(shift))]
    ppermute x7, waiting for transfers between devices: 18.5 us -> 11.6 us  [send_y(): return lax.ppermute(value, 'col', ring(shift))]
    ppermute x13, starting transfers between devices: 20.3 us -> 15.7 us  [send_x(): return lax.ppermute(value, 'row', along_x(shift))]
    pallas_call x1, Pallas kernels: 17.7 us -> 13.8 us  [partial_cols(): pl.pallas_call(z_kernel, out_shape=sums_of(Z_PARTS * 2), in_specs=[pl.Blo...]
    ppermute x7, starting transfers between devices: 9.25 us -> 11.9 us  [send_y(): return lax.ppermute(value, 'col', ring(shift))]
  transfers between devices with their start and end apart: 38 -> 38, of which waited for: 10 -> 8; matrix products, arithmetic and copies ran while one was open for 24% -> 25% of each run, Pallas kernels for 13% -> 10%
where the time goes in v5:
time: 244 us; the launch traced here: 242 us
  other arithmetic  63.8 us (26%)
  starting transfers between devices  57.3 us (23%)
  blocking collectives  42.7 us (18%)
  Pallas kernels  39.2 us (16%)
  waiting for transfers between devices  24.5 us (10%)
  matrix products  6.54 us (3%)
  between operations  4.57 us (2%)
  local copies, waits for them, and re-layouts  3.29 us (1%)
    all_gather x1, blocking collectives, body(): gathered = lax.all_gather(mine, 'col', axis=0, tiled=True)  42.7 us
    ppermute x13, starting transfers between devices, send_z(): return lax.ppermute(value, 'row', along_z(shift))  28.5 us
    convert_element_type x15, other arithmetic, pack(): return by_rows((value * scales[1]).astype(f16))  25.9 us
    pallas_call x2, Pallas kernels, partial_rows(): pl.pallas_call(y_kernel, out_shape=sums_of(Y_PARTS) + (jax.ShapeDtypeStru...  23.5 us
    ppermute x13, starting transfers between devices, send_x(): return lax.ppermute(value, 'row', along_x(shift))  15.7 us
    pallas_call x1, Pallas kernels, partial_cols(): pl.pallas_call(z_kernel, out_shape=sums_of(Z_PARTS * 2), in_specs=[pl.Blo...  13.8 us
    another operation x3, other arithmetic, body(): lower_factor = jnp.linalg.cholesky(gram)  12.4 us
    ppermute x7, starting transfers between devices, send_y(): return lax.ppermute(value, 'col', ring(shift))  11.9 us
  transfers between devices with their start and end apart: 38, of which 8 were waited for; matrix products, arithmetic and copies ran while one was open for 25% of the time, Pallas kernels for 10%

profile of v5, /device:TPU:24, one launch (start us, length us, event | category | flops | bytes accessed | tf_op | source)
XLA Modules:
  0.0 241.8 jit_solution(4797846508978936413)
XLA Ops:
  3.8 12.4 %partial_rows.3 = (f32[32,256,128]{2,1,0:T(8,128)}, f32[16,256,128]{2,1,0:T(8,128)}, f32[16,256,128]{2,1,0:T(8,128)}, f32[8,128]{1,0:T(8,128)}) custom-call(s32[1]{0:T(128)} %bitcast.148.count, s32[96]{0:T(128)} %and_select_fusion.1.targets, s32[96]{0:T(128)} %bitcast.185, bf16[96,256,256]{2,1,0:T(8,128)(2,1)} %bitcast.153, bf16[128,256,128]{2,1,0:T(8,128)(2,1)} %bitcast.156), custom_call_target="tpu_custom_call" | custom-call | flops 805306368 | bytes 62914560 | tf_op jit(solution)/shard_map/partial_rows/pallas_call | solution.py:207
  17.3 11.1 %partial_rows.2 = (f32[32,256,128]{2,1,0:T(8,128)}, f32[16,256,128]{2,1,0:T(8,128)}, f32[16,256,128]{2,1,0:T(8,128)}, f32[8,128]{1,0:T(8,128)}) custom-call(s32[1]{0:T(128)} %bitcast.147.count, s32[96]{0:T(128)} %get-tuple-element.131.targets, s32[96]{0:T(128)} %bitcast.186, bf16[96,256,256]{2,1,0:T(8,128)(2,1)} %bitcast.154, bf16[128,256,128]{2,1,0:T(8,128)(2,1)} %bitcast.157), custom_call_target="tpu_custom_call" | custom-call | flops 805306368 | bytes 62914560 | tf_op jit(solution)/shard_map/partial_rows/pallas_call | solution.py:207
  29.2 5.3 %fusion.1 = (f16[16,256,128]{2,1,0:T(8,128)(2,1)}, f16[16,256,128]{2,1,0:T(8,128)(2,1)S(1)}) fusion(f32[32,256,128]{2,1,0:T(8,128)} %collective-permute-done.3, f32[32,256,128]{2,1,0:T(8,128)} %get-tuple-element.68, f32[]{:T(128)S(1)} %bitcast.196), kind=kLoop, calls=%fused_computation.4 | loop fusion | flops 3145728 | bytes 10485764 | tf_op jit(solution)/shard_map/convert_element_type | solution.py:335
  34.5 2.4 collective-permute-start.4
  36.9 2.1 collective-permute-start.5
  41.4 2.4 collective-permute-start.7
  45.2 3.8 %slice_add_fusion.2 = (f32[2048,128]{1,0:T(8,128)S(1)}, f32[2048,128]{1,0:T(8,128)S(1)}, f32[2048,128]{1,0:T(8,128)S(1)}, f32[2048,128]{1,0:T(8,128)S(1)}) fusion(f32[4096,128]{1,0:T(8,128)} %bitcast.9, f32[4096,128]{1,0:T(8,128)} %bitcast.160, f32[4096,128]{1,0:T(8,128)} %bitcast.158, f32[4096,128]{1,0:T(8,128)} %bitcast.159), kind=kLoop, calls=%fused_computation.35 | loop fusion | flops 1048576 | bytes 12582912 | tf_op jit(solution)/shard_map/add | solution.py:460
  51.7 3.3 %collective-permute-start.13 = (f32[8,128]{1,0:T(8,128)S(1)}, f32[8,128]{1,0:T(8,128)S(1)}, u32[]{:S(2)}, u32[]{:S(2)}) collective-permute-start(f32[8,128]{1,0:T(8,128)S(1)} %max.84), channel_id=1, source_target_pairs={{0,32},{8,40},{16,48},{24,56},{32,64},{40,72},{48,80},{56,88},{64,... | collective-permute-start | bytes 12296 | tf_op jit(solution)/shard_map/ppermute | solution.py:414
  58.7 4.5 %collective-permute-start.15 = (f32[8,128]{1,0:T(8,128)S(1)}, f32[8,128]{1,0:T(8,128)S(1)}, u32[]{:S(2)}, u32[]{:S(2)}) collective-permute-start(f32[8,128]{1,0:T(8,128)S(1)} %maximum_maximum_fusion.1), channel_id=1, source_target_pairs={{0,16},{8,24},{16,0},{24,8},{32,48},{40,56},{48,32},{56,40},{64,80... | collective-permute-start | bytes 12296 | tf_op jit(solution)/shard_map/ppermute | solution.py:417
  63.3 3.1 %collective-permute-start.17 = (f32[8,128]{1,0:T(8,128)S(1)}, f32[8,128]{1,0:T(8,128)S(1)}, u32[]{:S(2)}, u32[]{:S(2)}) collective-permute-start(f32[8,128]{1,0:T(8,128)S(1)} %maximum_maximum_fusion.1), channel_id=1, source_target_pairs={{0,24},{8,0},{16,8},{24,16},{32,56},{40,32},{48,40},{56,48},{64,88... | collective-permute-start | bytes 12296 | tf_op jit(solution)/shard_map/ppermute | solution.py:417
  67.0 3.2 %collective-permute-start.9 = (f16[2048,128]{1,0:T(8,128)(2,1)S(1)}, f16[2048,128]{1,0:T(8,128)(2,1)S(1)}, u32[]{:S(2)}, u32[]{:S(2)}) collective-permute-start(f16[2048,128]{1,0:T(8,128)(2,1)S(1)} %multiply_convert_fusion.5), channel_id=1, source_target_pairs={{0,2},{1,3},{2,4},{3,5},{4,6},{5,7},{6,0},{7,1},{8,10},{9,11},{10,... | collective-permute-start | bytes 1572872 | tf_op jit(solution)/shard_map/ppermute | solution.py:411
  70.3 10.9 %collective-permute-done.10 = f16[2048,128]{1,0:T(8,128)(2,1)S(1)} collective-permute-done((f16[2048,128]{1,0:T(8,128)(2,1)S(1)}, f16[2048,128]{1,0:T(8,128)(2,1)S(1)}, u32[]{:S(2)}, u32[]{:S(2)}) %collective-permute-start.10) | collective-permute-done | bytes 524320 | tf_op jit(solution)/shard_map/ppermute | solution.py:411
  82.4 2.4 abs_reduce_fusion.1
  87.3 42.7 %all-gather.1.gathered.table = s16[35072,128]{1,0:T(8,128)(2,1)} all-gather(s16[4384,128]{1,0:T(8,128)(2,1)S(1)} %pad_add_fusion), channel_id=1, replica_groups=mesh['row'=16,'col'=8] {'col'}, dimensions={0}, use_global_device_ids=true | all-gather | bytes 10100736 | tf_op jit(solution)/shard_map/all_gather | solution.py:501
  132.1 3.1 %collective-permute-start.19 = (f32[128,128]{1,0:T(8,128)}, f32[128,128]{1,0:T(8,128)S(1)}, u32[]{:S(2)}, u32[]{:S(2)}) collective-permute-start(f32[128,128]{1,0:T(8,128)} %get-tuple-element.90), channel_id=1, source_target_pairs={{0,32},{8,40},{16,48},{24,56},{32,64},{40,72},{48,80},{56,88},{64,... | collective-permute-start | bytes 196616 | tf_op jit(solution)/shard_map/ppermute | solution.py:414
  135.3 13.8 %partial_cols.1 = (f32[16,256,128]{2,1,0:T(8,128)}, f32[16,256,128]{2,1,0:T(8,128)}, f32[8,256,128]{2,1,0:T(8,128)}, f32[8,256,128]{2,1,0:T(8,128)}, f32[4,256,1...) custom-call(s32[96]{0:T(128)} %select_reduce_fusion.1.order, ...), custom_call_target="tpu_custom_call" | custom-call | flops 3221225472 | bytes 44040192 | tf_op jit(solution)/shard_map/partial_cols/pallas_call | solution.py:308
  149.1 3.0 %multiply_convert_fusion.2 = f16[16,256,128]{2,1,0:T(8,128)(2,1)} fusion(f32[16,256,128]{2,1,0:T(8,128)} %get-tuple-element.95, f32[]{:T(128)S(1)} %bitcast.164), kind=kLoop, calls=%fused_computation.11 | loop fusion | flops 1048576 | bytes 3145732 | tf_op jit(solution)/shard_map/convert_element_type | solution.py:335
  153.5 7.1 %collective-permute-start.21 = (f32[128,128]{1,0:T(8,128)S(1)}, f32[128,128]{1,0:T(8,128)S(1)}, u32[]{:S(2)}, u32[]{:S(2)}) collective-permute-start(f32[128,128]{1,0:T(8,128)S(1)} %add_add_fusion.1), channel_id=1, source_target_pairs={{0,16},{8,24},{16,0},{24,8},{32,48},{40,56},{48,32},{56,40},{64,80... | collective-permute-start | bytes 196616 | tf_op jit(solution)/shard_map/ppermute | solution.py:417
  160.6 3.2 %collective-permute-start.23 = (f32[128,128]{1,0:T(8,128)S(1)}, f32[128,128]{1,0:T(8,128)S(1)}, u32[]{:S(2)}, u32[]{:S(2)}) collective-permute-start(f32[128,128]{1,0:T(8,128)S(1)} %add_add_fusion.1), channel_id=1, source_target_pairs={{0,24},{8,0},{16,8},{24,16},{32,56},{40,32},{48,40},{56,48},{64,88... | collective-permute-start | bytes 196616 | tf_op jit(solution)/shard_map/ppermute | solution.py:417
  167.4 3.0 %multiply_convert_fusion = f16[16,256,128]{2,1,0:T(8,128)(2,1)} fusion(f32[16,256,128]{2,1,0:T(8,128)} %get-tuple-element.110, f32[]{:T(128)S(6)} %add.316), kind=kLoop, calls=%fused_computation.9 | loop fusion | flops 1048576 | bytes 3145732 | tf_op jit(solution)/shard_map/convert_element_type | solution.py:335
  170.4 3.2 %collective-permute-start.32 = (f16[4096,128]{1,0:T(8,128)(2,1)}, f16[4096,128]{1,0:T(8,128)(2,1)}, u32[]{:S(2)}, u32[]{:S(2)}) collective-permute-start(f16[4096,128]{1,0:T(8,128)(2,1)} %bitcast.35), channel_id=1, source_target_pairs={{0,24},{8,0},{16,8},{24,16},{32,56},{40,32},{48,40},{56,48},{64,88... | collective-permute-start | bytes 3145736 | tf_op jit(solution)/shard_map/ppermute | solution.py:417
  174.9 11.7 %cholesky.17 = f32[128,128]{1,0:T(8,128)S(1)} custom-call(f32[128,128]{1,0:T(8,128)S(1)} %fusion.45), custom_call_target="Cholesky" | custom-call | tf_op jit(solution)/shard_map/jit(cholesky)/cholesky | solution.py:514
  187.9 9.8 %custom-call.6 = f32[1,128,128]{1,2,0:T(8,128)S(1)} custom-call(f32[1,128,128]{2,1,0:T(8,128)S(1)} %fusion.42), custom_call_target="InvertDiagBlocksLowerTriangular" | custom-call | tf_op jit(solution)/shard_map/triangular_solve | solution.py:519
  201.3 3.2 %collective-permute-start.27 = (f16[2048,128]{1,0:T(8,128)(2,1)S(1)}, f16[2048,128]{1,0:T(8,128)(2,1)S(1)}, u32[]{:S(2)}, u32[]{:S(2)}) collective-permute-start(f16[2048,128]{1,0:T(8,128)(2,1)S(1)} %fusion.12), channel_id=1, source_target_pairs={{0,96},{8,104},{16,112},{24,120},{32,0},{40,8},{48,16},{56,24},{64... | collective-permute-start | bytes 1572872 | tf_op jit(solution)/shard_map/ppermute | solution.py:414
  206.4 3.3 %collective-permute-start.34 = (f16[2048,128]{1,0:T(8,128)(2,1)S(1)}, f16[2048,128]{1,0:T(8,128)(2,1)S(1)}, u32[]{:S(2)}, u32[]{:S(2)}) collective-permute-start(f16[2048,128]{1,0:T(8,128)(2,1)S(1)} %fusion.8), channel_id=1, source_target_pairs={{0,24},{8,0},{16,8},{24,16},{32,56},{40,32},{48,40},{56,48},{64,88... | collective-permute-start | bytes 1572872 | tf_op jit(solution)/shard_map/ppermute | solution.py:417
  209.7 4.2 %collective-permute-done.26 = f16[2048,128]{1,0:T(8,128)(2,1)S(1)} collective-permute-done((f16[2048,128]{1,0:T(8,128)(2,1)S(1)}, f16[2048,128]{1,0:T(8,128)(2,1)S(1)}, u32[]{:S(2)}, u32[]{:S(2)}) %collective-permute-start.26) | collective-permute-done | bytes 524320 | tf_op jit(solution)/shard_map/ppermute | solution.py:414
  213.9 2.4 fusion.34
  216.2 3.0 %collective-permute-start.29 = (f16[1024,128]{1,0:T(8,128)(2,1)}, f16[1024,128]{1,0:T(8,128)(2,1)}, u32[]{:S(2)}, u32[]{:S(2)}) collective-permute-start(f16[1024,128]{1,0:T(8,128)(2,1)} %get-tuple-element.139), channel_id=1, source_target_pairs={{0,24},{8,0},{16,8},{24,16},{32,56},{40,32},{48,40},{56,48},{64,88... | collective-permute-start | bytes 786440 | tf_op jit(solution)/shard_map/ppermute | solution.py:417
  221.3 2.0 fusion.24
  224.5 3.2 %collective-permute-start.36 = (f16[1024,128]{1,0:T(8,128)(2,1)}, f16[1024,128]{1,0:T(8,128)(2,1)S(1)}, u32[]{:S(2)}, u32[]{:S(2)}) collective-permute-start(f16[1024,128]{1,0:T(8,128)(2,1)} %get-tuple-element.141), channel_id=1, source_target_pairs={{0,96},{8,104},{16,112},{24,120},{32,0},{40,8},{48,16},{56,24},{64... | collective-permute-start | bytes 786440 | tf_op jit(solution)/shard_map/ppermute | solution.py:414
  227.7 3.0 %collective-permute-done.28 = f16[1024,128]{1,0:T(8,128)(2,1)S(1)} collective-permute-done((f16[1024,128]{1,0:T(8,128)(2,1)S(1)}, f16[1024,128]{1,0:T(8,128)(2,1)S(1)}, u32[]{:S(2)}, u32[]{:S(2)}) %collective-permute-start.28) | collective-permute-done | bytes 262176 | tf_op jit(solution)/shard_map/ppermute | solution.py:417
  234.8 2.3 convolution_multiply_fusion
  (155 shorter events, 43.1 us)
Async XLA Ops:
  16.2 13.0 %collective-permute-start.3 = (f32[32,256,128]{2,1,0:T(8,128)}, f32[32,256,128]{2,1,0:T(8,128)}, u32[]{:S(2)}, u32[]{:S(2)}) collective-permute-start(f32[32,256,128]{2,1,0:T(8,128)} %get-tuple-element.69), channel_id=1, source_target_pairs={{0,1},{1,0},{2,3},{3,2},{4,5},{5,4},{6,7},{7,6},{8,9},{9,8},{10,11... | collective-permute-start | bytes 12582920 | tf_op jit(solution)/shard_map/ppermute | solution.py:408
  16.3 27.6 %collective-permute-start = (f32[16,256,128]{2,1,0:T(8,128)}, f32[16,256,128]{2,1,0:T(8,128)S(1)}, u32[]{:S(2)}, u32[]{:S(2)}) collective-permute-start(f32[16,256,128]{2,1,0:T(8,128)} %get-tuple-element.64), channel_id=1, source_target_pairs={{0,1},{1,0},{2,3},{3,2},{4,5},{5,4},{6,7},{7,6},{8,9},{9,8},{10,11... | collective-permute-start | bytes 6291464 | tf_op jit(solution)/shard_map/ppermute | solution.py:408
  16.8 27.1 %collective-permute-start.1 = (f32[16,256,128]{2,1,0:T(8,128)}, f32[16,256,128]{2,1,0:T(8,128)}, u32[]{:S(2)}, u32[]{:S(2)}) collective-permute-start(f32[16,256,128]{2,1,0:T(8,128)} %get-tuple-element.65), channel_id=1, source_target_pairs={{0,1},{1,0},{2,3},{3,2},{4,5},{5,4},{6,7},{7,6},{8,9},{9,8},{10,11... | collective-permute-start | bytes 6291464 | tf_op jit(solution)/shard_map/ppermute | solution.py:408
  16.9 11.5 %collective-permute-start.2 = (f32[8,128]{1,0:T(8,128)}, f32[8,128]{1,0:T(8,128)S(1)}, u32[]{:S(2)}, u32[]{:S(2)}) collective-permute-start(f32[8,128]{1,0:T(8,128)} %get-tuple-element.67), channel_id=1, source_target_pairs={{0,1},{1,0},{2,3},{3,2},{4,5},{5,4},{6,7},{7,6},{8,9},{9,8},{10,11... | collective-permute-start | bytes 12296 | tf_op jit(solution)/shard_map/ppermute | solution.py:408
  39.6 26.7 %collective-permute-start.8 = (f16[4096,128]{1,0:T(8,128)(2,1)}, f16[4096,128]{1,0:T(8,128)(2,1)S(1)}, u32[]{:S(2)}, u32[]{:S(2)}) collective-permute-start(f16[4096,128]{1,0:T(8,128)(2,1)} %bitcast.162), channel_id=1, source_target_pairs={{0,6},{1,7},{2,0},{3,1},{4,2},{5,3},{6,4},{7,5},{8,14},{9,15},{10,... | collective-permute-start | bytes 3145736 | tf_op jit(solution)/shard_map/ppermute | solution.py:411
  41.4 25.2 %collective-permute-start.7 = (f16[4096,128]{1,0:T(8,128)(2,1)S(1)}, f16[4096,128]{1,0:T(8,128)(2,1)S(1)}, u32[]{:S(2)}, u32[]{:S(2)}) collective-permute-start(f16[4096,128]{1,0:T(8,128)(2,1)S(1)} %bitcast.161), channel_id=1, source_target_pairs={{0,2},{1,3},{2,4},{3,5},{4,6},{5,7},{6,0},{7,1},{8,10},{9,11},{10,... | collective-permute-start | bytes 3145736 | tf_op jit(solution)/shard_map/ppermute | solution.py:411
  43.8 7.9 %collective-permute-start.11 = (f32[8,128]{1,0:T(8,128)S(1)}, f32[8,128]{1,0:T(8,128)S(1)}, u32[]{:S(2)}, u32[]{:S(2)}) collective-permute-start(f32[8,128]{1,0:T(8,128)S(1)} %maximum_maximum_fusion.2), channel_id=1, source_target_pairs={{0,1},{1,0},{2,3},{3,2},{4,5},{5,4},{6,7},{7,6},{8,9},{9,8},{10,11... | collective-permute-start | bytes 12296 | tf_op jit(solution)/shard_map/ppermute | solution.py:408
  58.7 11.6 %collective-permute-start.15 = (f32[8,128]{1,0:T(8,128)S(1)}, f32[8,128]{1,0:T(8,128)S(1)}, u32[]{:S(2)}, u32[]{:S(2)}) collective-permute-start(f32[8,128]{1,0:T(8,128)S(1)} %maximum_maximum_fusion.1), channel_id=1, source_target_pairs={{0,16},{8,24},{16,0},{24,8},{32,48},{40,56},{48,32},{56,40},{64,80... | collective-permute-start | bytes 12296 | tf_op jit(solution)/shard_map/ppermute | solution.py:417
  63.1 7.1 %collective-permute-start.16 = (f32[8,128]{1,0:T(8,128)S(1)}, f32[8,128]{1,0:T(8,128)S(1)}, u32[]{:S(2)}, u32[]{:S(2)}) collective-permute-start(f32[8,128]{1,0:T(8,128)S(1)} %maximum_maximum_fusion.1), channel_id=1, source_target_pairs={{0,8},{8,16},{16,24},{24,0},{32,40},{40,48},{48,56},{56,32},{64,72... | collective-permute-start | bytes 12296 | tf_op jit(solution)/shard_map/ppermute | solution.py:417
  63.3 6.9 %collective-permute-start.17 = (f32[8,128]{1,0:T(8,128)S(1)}, f32[8,128]{1,0:T(8,128)S(1)}, u32[]{:S(2)}, u32[]{:S(2)}) collective-permute-start(f32[8,128]{1,0:T(8,128)S(1)} %maximum_maximum_fusion.1), channel_id=1, source_target_pairs={{0,24},{8,0},{16,8},{24,16},{32,56},{40,32},{48,40},{56,48},{64,88... | collective-permute-start | bytes 12296 | tf_op jit(solution)/shard_map/ppermute | solution.py:417
  66.9 14.3 %collective-permute-start.10 = (f16[2048,128]{1,0:T(8,128)(2,1)S(1)}, f16[2048,128]{1,0:T(8,128)(2,1)S(1)}, u32[]{:S(2)}, u32[]{:S(2)}) collective-permute-start(f16[2048,128]{1,0:T(8,128)(2,1)S(1)} %multiply_convert_fusion.4), channel_id=1, source_target_pairs={{0,6},{1,7},{2,0},{3,1},{4,2},{5,3},{6,4},{7,5},{8,14},{9,15},{10,... | collective-permute-start | bytes 1572872 | tf_op jit(solution)/shard_map/ppermute | solution.py:411
  67.0 14.2 %collective-permute-start.9 = (f16[2048,128]{1,0:T(8,128)(2,1)S(1)}, f16[2048,128]{1,0:T(8,128)(2,1)S(1)}, u32[]{:S(2)}, u32[]{:S(2)}) collective-permute-start(f16[2048,128]{1,0:T(8,128)(2,1)S(1)} %multiply_convert_fusion.5), channel_id=1, source_target_pairs={{0,2},{1,3},{2,4},{3,5},{4,6},{5,7},{6,0},{7,1},{8,10},{9,11},{10,... | collective-permute-start | bytes 1572872 | tf_op jit(solution)/shard_map/ppermute | solution.py:411
  131.9 21.6 %collective-permute-start.18 = (f32[128,128]{1,0:T(8,128)}, f32[128,128]{1,0:T(8,128)S(1)}, u32[]{:S(2)}, u32[]{:S(2)}) collective-permute-start(f32[128,128]{1,0:T(8,128)} %get-tuple-element.90), channel_id=1, source_target_pairs={{0,64},{8,72},{16,80},{24,88},{32,96},{40,104},{48,112},{56,120},{... | collective-permute-start | bytes 196616 | tf_op jit(solution)/shard_map/ppermute | solution.py:414
  132.1 21.4 %collective-permute-start.19 = (f32[128,128]{1,0:T(8,128)}, f32[128,128]{1,0:T(8,128)S(1)}, u32[]{:S(2)}, u32[]{:S(2)}) collective-permute-start(f32[128,128]{1,0:T(8,128)} %get-tuple-element.90), channel_id=1, source_target_pairs={{0,32},{8,40},{16,48},{24,56},{32,64},{40,72},{48,80},{56,88},{64,... | collective-permute-start | bytes 196616 | tf_op jit(solution)/shard_map/ppermute | solution.py:414
  135.2 18.3 %collective-permute-start.20 = (f32[128,128]{1,0:T(8,128)}, f32[128,128]{1,0:T(8,128)S(1)}, u32[]{:S(2)}, u32[]{:S(2)}) collective-permute-start(f32[128,128]{1,0:T(8,128)} %get-tuple-element.90), channel_id=1, source_target_pairs={{0,96},{8,104},{16,112},{24,120},{32,0},{40,8},{48,16},{56,24},{64... | collective-permute-start | bytes 196616 | tf_op jit(solution)/shard_map/ppermute | solution.py:414
  152.1 45.8 %collective-permute-start.25 = (f16[4096,128]{1,0:T(8,128)(2,1)}, f16[4096,128]{1,0:T(8,128)(2,1)}, u32[]{:S(2)}, u32[]{:S(2)}) collective-permute-start(f16[4096,128]{1,0:T(8,128)(2,1)} %bitcast.25), channel_id=1, source_target_pairs={{0,96},{8,104},{16,112},{24,120},{32,0},{40,8},{48,16},{56,24},{64... | collective-permute-start | bytes 3145736 | tf_op jit(solution)/shard_map/ppermute | solution.py:414
  153.5 11.6 %collective-permute-start.21 = (f32[128,128]{1,0:T(8,128)S(1)}, f32[128,128]{1,0:T(8,128)S(1)}, u32[]{:S(2)}, u32[]{:S(2)}) collective-permute-start(f32[128,128]{1,0:T(8,128)S(1)} %add_add_fusion.1), channel_id=1, source_target_pairs={{0,16},{8,24},{16,0},{24,8},{32,48},{40,56},{48,32},{56,40},{64,80... | collective-permute-start | bytes 196616 | tf_op jit(solution)/shard_map/ppermute | solution.py:417
  160.6 5.5 %collective-permute-start.22 = (f32[128,128]{1,0:T(8,128)S(1)}, f32[128,128]{1,0:T(8,128)S(1)}, u32[]{:S(2)}, u32[]{:S(2)}) collective-permute-start(f32[128,128]{1,0:T(8,128)S(1)} %add_add_fusion.1), channel_id=1, source_target_pairs={{0,8},{8,16},{16,24},{24,0},{32,40},{40,48},{48,56},{56,32},{64,72... | collective-permute-start | bytes 196616 | tf_op jit(solution)/shard_map/ppermute | solution.py:417
  160.6 5.5 %collective-permute-start.23 = (f32[128,128]{1,0:T(8,128)S(1)}, f32[128,128]{1,0:T(8,128)S(1)}, u32[]{:S(2)}, u32[]{:S(2)}) collective-permute-start(f32[128,128]{1,0:T(8,128)S(1)} %add_add_fusion.1), channel_id=1, source_target_pairs={{0,24},{8,0},{16,8},{24,16},{32,56},{40,32},{48,40},{56,48},{64,88... | collective-permute-start | bytes 196616 | tf_op jit(solution)/shard_map/ppermute | solution.py:417
  165.1 34.6 %collective-permute-start.24 = (f16[4096,128]{1,0:T(8,128)(2,1)}, f16[4096,128]{1,0:T(8,128)(2,1)}, u32[]{:S(2)}, u32[]{:S(2)}) collective-permute-start(f16[4096,128]{1,0:T(8,128)(2,1)} %bitcast.24), channel_id=1, source_target_pairs={{0,32},{8,40},{16,48},{24,56},{32,64},{40,72},{48,80},{56,88},{64,... | collective-permute-start | bytes 3145736 | tf_op jit(solution)/shard_map/ppermute | solution.py:414
  170.4 34.1 %collective-permute-start.32 = (f16[4096,128]{1,0:T(8,128)(2,1)}, f16[4096,128]{1,0:T(8,128)(2,1)}, u32[]{:S(2)}, u32[]{:S(2)}) collective-permute-start(f16[4096,128]{1,0:T(8,128)(2,1)} %bitcast.35), channel_id=1, source_target_pairs={{0,24},{8,0},{16,8},{24,16},{32,56},{40,32},{48,40},{56,48},{64,88... | collective-permute-start | bytes 3145736 | tf_op jit(solution)/shard_map/ppermute | solution.py:417
  174.9 31.1 %collective-permute-start.31 = (f16[4096,128]{1,0:T(8,128)(2,1)}, f16[4096,128]{1,0:T(8,128)(2,1)S(1)}, u32[]{:S(2)}, u32[]{:S(2)}) collective-permute-start(f16[4096,128]{1,0:T(8,128)(2,1)} %bitcast.34), channel_id=1, source_target_pairs={{0,8},{8,16},{16,24},{24,0},{32,40},{40,48},{48,56},{56,32},{64,72... | collective-permute-start | bytes 3145736 | tf_op jit(solution)/shard_map/ppermute | solution.py:417
  201.2 12.7 %collective-permute-start.26 = (f16[2048,128]{1,0:T(8,128)(2,1)S(1)}, f16[2048,128]{1,0:T(8,128)(2,1)S(1)}, u32[]{:S(2)}, u32[]{:S(2)}) collective-permute-start(f16[2048,128]{1,0:T(8,128)(2,1)S(1)} %fusion.14), channel_id=1, source_target_pairs={{0,32},{8,40},{16,48},{24,56},{32,64},{40,72},{48,80},{56,88},{64,... | collective-permute-start | bytes 1572872 | tf_op jit(solution)/shard_map/ppermute | solution.py:414
  201.3 12.6 %collective-permute-start.27 = (f16[2048,128]{1,0:T(8,128)(2,1)S(1)}, f16[2048,128]{1,0:T(8,128)(2,1)S(1)}, u32[]{:S(2)}, u32[]{:S(2)}) collective-permute-start(f16[2048,128]{1,0:T(8,128)(2,1)S(1)} %fusion.12), channel_id=1, source_target_pairs={{0,96},{8,104},{16,112},{24,120},{32,0},{40,8},{48,16},{56,24},{64... | collective-permute-start | bytes 1572872 | tf_op jit(solution)/shard_map/ppermute | solution.py:414
  206.3 15.1 %collective-permute-start.33 = (f16[2048,128]{1,0:T(8,128)(2,1)S(1)}, f16[2048,128]{1,0:T(8,128)(2,1)S(1)}, u32[]{:S(2)}, u32[]{:S(2)}) collective-permute-start(f16[2048,128]{1,0:T(8,128)(2,1)S(1)} %fusion.10), channel_id=1, source_target_pairs={{0,8},{8,16},{16,24},{24,0},{32,40},{40,48},{48,56},{56,32},{64,72... | collective-permute-start | bytes 1572872 | tf_op jit(solution)/shard_map/ppermute | solution.py:417
  206.4 15.0 %collective-permute-start.34 = (f16[2048,128]{1,0:T(8,128)(2,1)S(1)}, f16[2048,128]{1,0:T(8,128)(2,1)S(1)}, u32[]{:S(2)}, u32[]{:S(2)}) collective-permute-start(f16[2048,128]{1,0:T(8,128)(2,1)S(1)} %fusion.8), channel_id=1, source_target_pairs={{0,24},{8,0},{16,8},{24,16},{32,56},{40,32},{48,40},{56,48},{64,88... | collective-permute-start | bytes 1572872 | tf_op jit(solution)/shard_map/ppermute | solution.py:417
  216.2 16.8 %collective-permute-start.29 = (f16[1024,128]{1,0:T(8,128)(2,1)}, f16[1024,128]{1,0:T(8,128)(2,1)}, u32[]{:S(2)}, u32[]{:S(2)}) collective-permute-start(f16[1024,128]{1,0:T(8,128)(2,1)} %get-tuple-element.139), channel_id=1, source_target_pairs={{0,24},{8,0},{16,8},{24,16},{32,56},{40,32},{48,40},{56,48},{64,88... | collective-permute-start | bytes 786440 | tf_op jit(solution)/shard_map/ppermute | solution.py:417
  219.2 13.9 %collective-permute-start.30 = (f16[1024,128]{1,0:T(8,128)(2,1)S(1)}, f16[1024,128]{1,0:T(8,128)(2,1)}, u32[]{:S(2)}, u32[]{:S(2)}) collective-permute-start(f16[1024,128]{1,0:T(8,128)(2,1)S(1)} %get-tuple-element.140), channel_id=1, source_target_pairs={{0,16},{8,24},{16,0},{24,8},{32,48},{40,56},{48,32},{56,40},{64,80... | collective-permute-start | bytes 786440 | tf_op jit(solution)/shard_map/ppermute | solution.py:417
  220.4 10.4 %collective-permute-start.28 = (f16[1024,128]{1,0:T(8,128)(2,1)S(1)}, f16[1024,128]{1,0:T(8,128)(2,1)S(1)}, u32[]{:S(2)}, u32[]{:S(2)}) collective-permute-start(f16[1024,128]{1,0:T(8,128)(2,1)S(1)} %fusion.41), channel_id=1, source_target_pairs={{0,8},{8,16},{16,24},{24,0},{32,40},{40,48},{48,56},{56,32},{64,72... | collective-permute-start | bytes 786440 | tf_op jit(solution)/shard_map/ppermute | solution.py:417
  223.3 13.8 %collective-permute-start.35 = (f16[1024,128]{1,0:T(8,128)(2,1)}, f16[1024,128]{1,0:T(8,128)(2,1)}, u32[]{:S(2)}, u32[]{:S(2)}) collective-permute-start(f16[1024,128]{1,0:T(8,128)(2,1)} %fusion.24), channel_id=1, source_target_pairs={{0,32},{8,40},{16,48},{24,56},{32,64},{40,72},{48,80},{56,88},{64,... | collective-permute-start | bytes 786440 | tf_op jit(solution)/shard_map/ppermute | solution.py:414
  224.5 12.7 %collective-permute-start.36 = (f16[1024,128]{1,0:T(8,128)(2,1)}, f16[1024,128]{1,0:T(8,128)(2,1)S(1)}, u32[]{:S(2)}, u32[]{:S(2)}) collective-permute-start(f16[1024,128]{1,0:T(8,128)(2,1)} %get-tuple-element.141), channel_id=1, source_target_pairs={{0,96},{8,104},{16,112},{24,120},{32,0},{40,8},{48,16},{56,24},{64... | collective-permute-start | bytes 786440 | tf_op jit(solution)/shard_map/ppermute | solution.py:414
  230.8 8.1 %collective-permute-start.37 = (f16[1024,128]{1,0:T(8,128)(2,1)}, f16[1024,128]{1,0:T(8,128)(2,1)S(1)}, u32[]{:S(2)}, u32[]{:S(2)}) collective-permute-start(f16[1024,128]{1,0:T(8,128)(2,1)} %get-tuple-element.142), channel_id=1, source_target_pairs={{0,64},{8,72},{16,80},{24,88},{32,96},{40,104},{48,112},{56,120},{... | collective-permute-start | bytes 786440 | tf_op jit(solution)/shard_map/ppermute | solution.py:414
  (26 other events, 173.6 us)

commit v6 on v5

--- a/solution.py
+++ b/solution.py
@@ -140,7 +140,7 @@
 
 
 def y_kernel(count, targets, cols, blocks, sketch, *rest):
-    outs, stat, scratch = rest[:3], rest[3], rest[4:]
+    outs, stat, scratch = rest[:2], rest[2], rest[3:]
     total_sum, block_buf, sketch_buf, sems, out_sems, order, ends = scratch
     sort_slots(count[0], targets, 8, order, ends)
 
@@ -185,7 +185,7 @@
     stat[4:] = jnp.full((4, K), jnp.max(largest_block.astype(f32)))
 
 
-Y_PARTS = (32, 16, 16)
+Y_PARTS = (32, 32)
 Z_PARTS = (16, 16, 8, 8, 4, 4, 4, 4)
 
 
@@ -209,7 +209,7 @@
         out_shape=sums_of(Y_PARTS) + (jax.ShapeDtypeStruct((8, K), f32),),
         in_specs=[pl.BlockSpec(memory_space=pltpu.SMEM)] * 3
         + [pl.BlockSpec(memory_space=pl.ANY)] * 2,
-        out_specs=(pl.BlockSpec(memory_space=pl.ANY),) * 3
+        out_specs=(pl.BlockSpec(memory_space=pl.ANY),) * 2
         + (pl.BlockSpec(memory_space=pltpu.VMEM),),
         scratch_shapes=scratch_for(1, Y_PARTS, jnp.bfloat16)
         + [pltpu.SMEM((NBLK + 1,), jnp.int32), pltpu.SMEM((9,), jnp.int32)],
@@ -455,9 +455,10 @@
     entries = jnp.maximum(own_stat, other_stat) * count[0].astype(f32)
     bounds, _ = lax.optimization_barrier((jnp.where(in_first, first_bound, entries), first))
     bounds, below, above = ring_fold(bounds, send_y, jnp.maximum)
-    later, _ = lax.optimization_barrier(((own[1:], from_pair[1:]), bounds))
+    later, _ = lax.optimization_barrier(((own[1], from_pair[1]), bounds))
     parts = [
-        [mine[at : at + HALF] + pair[at : at + HALF] for at in (0, HALF)] for mine, pair in zip(*later)
+        [later[0][at : at + HALF] + later[1][at : at + HALF] for at in (start, start + HALF)]
+        for start in (0, 2 * HALF)
     ]
     passing, staying = lax.optimization_barrier(parts)
     around = scales_for(below[:1]), scales_for(above[:1])

time: 244 us -> 241 us (0.988)
  starting transfers between devices: 57.3 us -> 49.9 us
  waiting for transfers between devices: 24.5 us -> 29 us
  blocking collectives: 42.7 us -> 40 us
    ppermute x7, waiting for transfers between devices: 11.6 us -> 19.2 us  [send_y(): return lax.ppermute(value, 'col', ring(shift))]
    ppermute x7, starting transfers between devices: 11.9 us -> 6.3 us  [send_y(): return lax.ppermute(value, 'col', ring(shift))]
    ppermute x13, starting transfers between devices: 28.5 us -> 25.4 us  [send_z(): return lax.ppermute(value, 'row', along_z(shift))]
    all_gather x1, blocking collectives: 42.7 us -> 40 us  [body(): gathered = lax.all_gather(mine, 'col', axis=0, tiled=True)]
  transfers between devices with their start and end apart: 38 -> 37, of which waited for: 8 -> 10; matrix products, arithmetic and copies ran while one was open for 25% -> 26% of each run, Pallas kernels for 10% -> 12%
where the time goes in v6:
time: 241 us; the launch traced here: 237 us
  other arithmetic  63.4 us (26%)
  starting transfers between devices  49.9 us (21%)
  Pallas kernels  41.5 us (17%)
  blocking collectives  40 us (17%)
  waiting for transfers between devices  29 us (12%)
  matrix products  6.56 us (3%)
  between operations  4.67 us (2%)
    all_gather x1, blocking collectives, body(): gathered = lax.all_gather(mine, 'col', axis=0, tiled=True)  40 us
    convert_element_type x15, other arithmetic, pack(): return by_rows((value * scales[1]).astype(f16))  25.7 us
    ppermute x13, starting transfers between devices, send_z(): return lax.ppermute(value, 'row', along_z(shift))  25.4 us
    pallas_call x2, Pallas kernels, partial_rows(): pl.pallas_call(y_kernel, out_shape=sums_of(Y_PARTS) + (jax.ShapeDtypeStru...  24.8 us
    ppermute x7, waiting for transfers between devices, send_y(): return lax.ppermute(value, 'col', ring(shift))  19.2 us
    ppermute x13, starting transfers between devices, send_x(): return lax.ppermute(value, 'row', along_x(shift))  16.4 us
    pallas_call x1, Pallas kernels, partial_cols(): pl.pallas_call(z_kernel, out_shape=sums_of(Z_PARTS * 2), in_specs=[pl.Blo...  14.8 us
    another operation x3, other arithmetic, body(): lower_factor = jnp.linalg.cholesky(gram)  12.4 us
  transfers between devices with their start and end apart: 37, of which 10 were waited for; matrix products, arithmetic and copies ran while one was open for 26% of the time, Pallas kernels for 12%

profile of v6, /device:TPU:24, one launch (start us, length us, event | category | flops | bytes accessed | tf_op | source)
XLA Modules:
  0.0 237.2 jit_solution(10635315459002065456)
XLA Ops:
  3.7 11.5 %partial_rows.3 = (f32[32,256,128]{2,1,0:T(8,128)}, f32[32,256,128]{2,1,0:T(8,128)}, f32[8,128]{1,0:T(8,128)}) custom-call(s32[1]{0:T(128)} %bitcast.146.count, s32[96]{0:T(128)} %and_select_fusion.1.targets, s32[96]{0:T(128)} %bitcast.180, bf16[96,256,256]{2,1,0:T(8,128)(2,1)} %bitcast.151, bf16[128,256,128]{2,1,0:T(8,128)(2,1)} %bitcast.154), custom_call_target="tpu_custom_call" | custom-call | flops 805306368 | bytes 62914560 | tf_op jit(solution)/shard_map/partial_rows/pallas_call | solution.py:207
  17.1 13.3 %partial_rows.2 = (f32[32,256,128]{2,1,0:T(8,128)}, f32[32,256,128]{2,1,0:T(8,128)}, f32[8,128]{1,0:T(8,128)}) custom-call(s32[1]{0:T(128)} %bitcast.145.count, s32[96]{0:T(128)} %get-tuple-element.123.targets, s32[96]{0:T(128)} %bitcast.181, bf16[96,256,256]{2,1,0:T(8,128)(2,1)} %bitcast.152, bf16[128,256,128]{2,1,0:T(8,128)(2,1)} %bitcast.155), custom_call_target="tpu_custom_call" | custom-call | flops 805306368 | bytes 62914560 | tf_op jit(solution)/shard_map/partial_rows/pallas_call | solution.py:207
  31.2 5.3 %fusion.1 = (f16[16,256,128]{2,1,0:T(8,128)(2,1)}, f16[16,256,128]{2,1,0:T(8,128)(2,1)S(1)}) fusion(f32[32,256,128]{2,1,0:T(8,128)} %collective-permute-done.2, f32[32,256,128]{2,1,0:T(8,128)} %get-tuple-element.62, f32[]{:T(128)S(1)} %bitcast.190), kind=kLoop, calls=%fused_computation.4 | loop fusion | flops 3145728 | bytes 10485764 | tf_op jit(solution)/shard_map/convert_element_type | solution.py:335
  42.8 3.8 %slice_add_fusion.2 = (f32[2048,128]{1,0:T(8,128)S(1)}, f32[2048,128]{1,0:T(8,128)S(1)}, f32[2048,128]{1,0:T(8,128)S(1)}, f32[2048,128]{1,0:T(8,128)S(1)}) fusion(f32[8192,128]{1,0:T(8,128)} %bitcast.7, f32[8192,128]{1,0:T(8,128)} %bitcast.156), kind=kLoop, calls=%fused_computation.35 | loop fusion | flops 1048576 | bytes 12582912 | tf_op jit(solution)/shard_map/add | solution.py:460
  49.4 3.2 %collective-permute-start.13 = (f32[8,128]{1,0:T(8,128)S(1)}, f32[8,128]{1,0:T(8,128)S(1)}, u32[]{:S(2)}, u32[]{:S(2)}) collective-permute-start(f32[8,128]{1,0:T(8,128)S(1)} %max.84), channel_id=1, source_target_pairs={{0,96},{8,104},{16,112},{24,120},{32,0},{40,8},{48,16},{56,24},{64... | collective-permute-start | bytes 12296 | tf_op jit(solution)/shard_map/ppermute | solution.py:414
  54.4 4.3 %collective-permute-start.14 = (f32[8,128]{1,0:T(8,128)S(1)}, f32[8,128]{1,0:T(8,128)S(1)}, u32[]{:S(2)}, u32[]{:S(2)}) collective-permute-start(f32[8,128]{1,0:T(8,128)S(1)} %maximum_maximum_fusion.1), channel_id=1, source_target_pairs={{0,16},{8,24},{16,0},{24,8},{32,48},{40,56},{48,32},{56,40},{64,80... | collective-permute-start | bytes 12296 | tf_op jit(solution)/shard_map/ppermute | solution.py:417
  59.3 2.6 %collective-permute-start.16 = (f32[8,128]{1,0:T(8,128)S(1)}, f32[8,128]{1,0:T(8,128)S(1)}, u32[]{:S(2)}, u32[]{:S(2)}) collective-permute-start(f32[8,128]{1,0:T(8,128)S(1)} %maximum_maximum_fusion.1), channel_id=1, source_target_pairs={{0,24},{8,0},{16,8},{24,16},{32,56},{40,32},{48,40},{56,48},{64,88... | collective-permute-start | bytes 12296 | tf_op jit(solution)/shard_map/ppermute | solution.py:417
  61.9 3.2 %collective-permute-done.7 = f16[4096,128]{1,0:T(8,128)(2,1)S(1)} collective-permute-done((f16[4096,128]{1,0:T(8,128)(2,1)}, f16[4096,128]{1,0:T(8,128)(2,1)S(1)}, u32[]{:S(2)}, u32[]{:S(2)}) %collective-permute-start.7) | collective-permute-done | bytes 1048608 | tf_op jit(solution)/shard_map/ppermute | solution.py:411
  65.7 2.5 %collective-permute-start.8 = (f16[2048,128]{1,0:T(8,128)(2,1)S(1)}, f16[2048,128]{1,0:T(8,128)(2,1)S(1)}, u32[]{:S(2)}, u32[]{:S(2)}) collective-permute-start(f16[2048,128]{1,0:T(8,128)(2,1)S(1)} %multiply_convert_fusion.5), channel_id=1, source_target_pairs={{0,2},{1,3},{2,4},{3,5},{4,6},{5,7},{6,0},{7,1},{8,10},{9,11},{10,... | collective-permute-start | bytes 1572872 | tf_op jit(solution)/shard_map/ppermute | solution.py:411
  68.3 10.4 %collective-permute-done.8 = f16[2048,128]{1,0:T(8,128)(2,1)S(1)} collective-permute-done((f16[2048,128]{1,0:T(8,128)(2,1)S(1)}, f16[2048,128]{1,0:T(8,128)(2,1)S(1)}, u32[]{:S(2)}, u32[]{:S(2)}) %collective-permute-start.8) | collective-permute-done | bytes 524320 | tf_op jit(solution)/shard_map/ppermute | solution.py:411
  78.7 3.0 %collective-permute-done.9 = f16[2048,128]{1,0:T(8,128)(2,1)S(1)} collective-permute-done((f16[2048,128]{1,0:T(8,128)(2,1)S(1)}, f16[2048,128]{1,0:T(8,128)(2,1)S(1)}, u32[]{:S(2)}, u32[]{:S(2)}) %collective-permute-start.9) | collective-permute-done | bytes 524320 | tf_op jit(solution)/shard_map/ppermute | solution.py:411
  82.8 2.4 %abs_reduce_fusion.1 = (f32[]{:T(128)}, f32[128,128]{1,0:T(8,128)S(1)}) fusion(f32[2048,128]{1,0:T(8,128)S(1)} %get-tuple-element.141, f32[2048,128]{1,0:T(8,128)S(1)} %get-tuple-element.142), kind=kOutput, calls=%fused_computation.87 | convolution fusion | flops 403210240 | bytes 2162692 | tf_op jit(solution)/shard_map/dot_general | solution.py:486
  87.8 40.0 %all-gather.1.gathered.table = s16[35072,128]{1,0:T(8,128)(2,1)} all-gather(s16[4384,128]{1,0:T(8,128)(2,1)S(1)} %pad_add_fusion), channel_id=1, replica_groups=mesh['row'=16,'col'=8] {'col'}, dimensions={0}, use_global_device_ids=true | all-gather | bytes 10100736 | tf_op jit(solution)/shard_map/all_gather | solution.py:502
  129.8 3.2 %collective-permute-start.19 = (f32[128,128]{1,0:T(8,128)}, f32[128,128]{1,0:T(8,128)S(1)}, u32[]{:S(2)}, u32[]{:S(2)}) collective-permute-start(f32[128,128]{1,0:T(8,128)} %get-tuple-element.82), channel_id=1, source_target_pairs={{0,96},{8,104},{16,112},{24,120},{32,0},{40,8},{48,16},{56,24},{64... | collective-permute-start | bytes 196616 | tf_op jit(solution)/shard_map/ppermute | solution.py:414
  133.1 14.8 %partial_cols.1 = (f32[16,256,128]{2,1,0:T(8,128)}, f32[16,256,128]{2,1,0:T(8,128)}, f32[8,256,128]{2,1,0:T(8,128)}, f32[8,256,128]{2,1,0:T(8,128)}, f32[4,256,1...) custom-call(s32[96]{0:T(128)} %select_reduce_fusion.1.order, ...), custom_call_target="tpu_custom_call" | custom-call | flops 3221225472 | bytes 44040192 | tf_op jit(solution)/shard_map/partial_cols/pallas_call | solution.py:308
  147.9 3.0 %multiply_convert_fusion.2 = f16[16,256,128]{2,1,0:T(8,128)(2,1)} fusion(f32[16,256,128]{2,1,0:T(8,128)} %get-tuple-element.87, f32[]{:T(128)S(1)} %bitcast.159), kind=kLoop, calls=%fused_computation.11 | loop fusion | flops 1048576 | bytes 3145732 | tf_op jit(solution)/shard_map/convert_element_type | solution.py:335
  151.0 4.2 %collective-permute-start.20 = (f32[128,128]{1,0:T(8,128)S(1)}, f32[128,128]{1,0:T(8,128)S(1)}, u32[]{:S(2)}, u32[]{:S(2)}) collective-permute-start(f32[128,128]{1,0:T(8,128)S(1)} %add_add_fusion.1), channel_id=1, source_target_pairs={{0,16},{8,24},{16,0},{24,8},{32,48},{40,56},{48,32},{56,40},{64,80... | collective-permute-start | bytes 196616 | tf_op jit(solution)/shard_map/ppermute | solution.py:417
  156.9 2.6 %collective-permute-start.22 = (f32[128,128]{1,0:T(8,128)S(1)}, f32[128,128]{1,0:T(8,128)S(1)}, u32[]{:S(2)}, u32[]{:S(2)}) collective-permute-start(f32[128,128]{1,0:T(8,128)S(1)} %add_add_fusion.1), channel_id=1, source_target_pairs={{0,24},{8,0},{16,8},{24,16},{32,56},{40,32},{48,40},{56,48},{64,88... | collective-permute-start | bytes 196616 | tf_op jit(solution)/shard_map/ppermute | solution.py:417
  160.8 2.0 collective-permute-start.23
  164.3 3.0 %multiply_convert_fusion = f16[16,256,128]{2,1,0:T(8,128)(2,1)} fusion(f32[16,256,128]{2,1,0:T(8,128)} %get-tuple-element.102, f32[]{:T(128)S(6)} %add.316), kind=kLoop, calls=%fused_computation.9 | loop fusion | flops 1048576 | bytes 3145732 | tf_op jit(solution)/shard_map/convert_element_type | solution.py:335
  167.3 2.2 collective-permute-start.31
  170.7 11.7 %cholesky.17 = f32[128,128]{1,0:T(8,128)S(1)} custom-call(f32[128,128]{1,0:T(8,128)S(1)} %fusion.45), custom_call_target="Cholesky" | custom-call | tf_op jit(solution)/shard_map/jit(cholesky)/cholesky | solution.py:515
  183.6 9.8 %custom-call.6 = f32[1,128,128]{1,2,0:T(8,128)S(1)} custom-call(f32[1,128,128]{2,1,0:T(8,128)S(1)} %fusion.42), custom_call_target="InvertDiagBlocksLowerTriangular" | custom-call | tf_op jit(solution)/shard_map/triangular_solve | solution.py:520
  196.9 2.1 collective-permute-start.25
  202.4 3.0 %collective-permute-start.33 = (f16[2048,128]{1,0:T(8,128)(2,1)S(1)}, f16[2048,128]{1,0:T(8,128)(2,1)S(1)}, u32[]{:S(2)}, u32[]{:S(2)}) collective-permute-start(f16[2048,128]{1,0:T(8,128)(2,1)S(1)} %fusion.8), channel_id=1, source_target_pairs={{0,24},{8,0},{16,8},{24,16},{32,56},{40,32},{48,40},{56,48},{64,88... | collective-permute-start | bytes 1572872 | tf_op jit(solution)/shard_map/ppermute | solution.py:417
  205.4 3.8 %collective-permute-done.25 = f16[2048,128]{1,0:T(8,128)(2,1)S(1)} collective-permute-done((f16[2048,128]{1,0:T(8,128)(2,1)S(1)}, f16[2048,128]{1,0:T(8,128)(2,1)S(1)}, u32[]{:S(2)}, u32[]{:S(2)}) %collective-permute-start.25) | collective-permute-done | bytes 524320 | tf_op jit(solution)/shard_map/ppermute | solution.py:414
  209.6 2.2 fusion.34
  211.8 3.0 %collective-permute-start.28 = (f16[1024,128]{1,0:T(8,128)(2,1)}, f16[1024,128]{1,0:T(8,128)(2,1)}, u32[]{:S(2)}, u32[]{:S(2)}) collective-permute-start(f16[1024,128]{1,0:T(8,128)(2,1)} %get-tuple-element.131), channel_id=1, source_target_pairs={{0,24},{8,0},{16,8},{24,16},{32,56},{40,32},{48,40},{56,48},{64,88... | collective-permute-start | bytes 786440 | tf_op jit(solution)/shard_map/ppermute | solution.py:417
  216.9 2.0 fusion.24
  220.5 2.8 %collective-permute-start.35 = (f16[1024,128]{1,0:T(8,128)(2,1)}, f16[1024,128]{1,0:T(8,128)(2,1)S(1)}, u32[]{:S(2)}, u32[]{:S(2)}) collective-permute-start(f16[1024,128]{1,0:T(8,128)(2,1)} %get-tuple-element.133), channel_id=1, source_target_pairs={{0,96},{8,104},{16,112},{24,120},{32,0},{40,8},{48,16},{56,24},{64... | collective-permute-start | bytes 786440 | tf_op jit(solution)/shard_map/ppermute | solution.py:414
  223.3 2.8 %collective-permute-done.27 = f16[1024,128]{1,0:T(8,128)(2,1)S(1)} collective-permute-done((f16[1024,128]{1,0:T(8,128)(2,1)S(1)}, f16[1024,128]{1,0:T(8,128)(2,1)S(1)}, u32[]{:S(2)}, u32[]{:S(2)}) %collective-permute-start.27) | collective-permute-done | bytes 262176 | tf_op jit(solution)/shard_map/ppermute | solution.py:417
  230.3 2.3 convolution_multiply_fusion
  (150 shorter events, 46.4 us)
Async XLA Ops:
  15.3 16.0 %collective-permute-start.2 = (f32[32,256,128]{2,1,0:T(8,128)}, f32[32,256,128]{2,1,0:T(8,128)}, u32[]{:S(2)}, u32[]{:S(2)}) collective-permute-start(f32[32,256,128]{2,1,0:T(8,128)} %get-tuple-element.63), channel_id=1, source_target_pairs={{0,1},{1,0},{2,3},{3,2},{4,5},{5,4},{6,7},{7,6},{8,9},{9,8},{10,11... | collective-permute-start | bytes 12582920 | tf_op jit(solution)/shard_map/ppermute | solution.py:408
  16.6 26.2 %collective-permute-start = (f32[32,256,128]{2,1,0:T(8,128)}, f32[32,256,128]{2,1,0:T(8,128)}, u32[]{:S(2)}, u32[]{:S(2)}) collective-permute-start(f32[32,256,128]{2,1,0:T(8,128)} %get-tuple-element.59), channel_id=1, source_target_pairs={{0,1},{1,0},{2,3},{3,2},{4,5},{5,4},{6,7},{7,6},{8,9},{9,8},{10,11... | collective-permute-start | bytes 12582920 | tf_op jit(solution)/shard_map/ppermute | solution.py:408
  16.7 13.7 %collective-permute-start.1 = (f32[8,128]{1,0:T(8,128)}, f32[8,128]{1,0:T(8,128)S(1)}, u32[]{:S(2)}, u32[]{:S(2)}) collective-permute-start(f32[8,128]{1,0:T(8,128)} %get-tuple-element.61), channel_id=1, source_target_pairs={{0,1},{1,0},{2,3},{3,2},{4,5},{5,4},{6,7},{7,6},{8,9},{9,8},{10,11... | collective-permute-start | bytes 12296 | tf_op jit(solution)/shard_map/ppermute | solution.py:408
  36.6 5.3 %collective-permute-start.4 = (f32[8,128]{1,0:T(8,128)S(1)}, f32[8,128]{1,0:T(8,128)S(1)}, u32[]{:S(2)}, u32[]{:S(2)}) collective-permute-start(f32[8,128]{1,0:T(8,128)S(1)} %get-tuple-element.64), channel_id=1, source_target_pairs={{0,2},{1,3},{2,4},{3,5},{4,6},{5,7},{6,0},{7,1},{8,10},{9,11},{10,... | collective-permute-start | bytes 12296 | tf_op jit(solution)/shard_map/ppermute | solution.py:411
  38.7 26.5 %collective-permute-start.7 = (f16[4096,128]{1,0:T(8,128)(2,1)}, f16[4096,128]{1,0:T(8,128)(2,1)S(1)}, u32[]{:S(2)}, u32[]{:S(2)}) collective-permute-start(f16[4096,128]{1,0:T(8,128)(2,1)} %bitcast.10), channel_id=1, source_target_pairs={{0,6},{1,7},{2,0},{3,1},{4,2},{5,3},{6,4},{7,5},{8,14},{9,15},{10,... | collective-permute-start | bytes 3145736 | tf_op jit(solution)/shard_map/ppermute | solution.py:411
  41.6 23.8 %collective-permute-start.6 = (f16[4096,128]{1,0:T(8,128)(2,1)S(1)}, f16[4096,128]{1,0:T(8,128)(2,1)S(1)}, u32[]{:S(2)}, u32[]{:S(2)}) collective-permute-start(f16[4096,128]{1,0:T(8,128)(2,1)S(1)} %bitcast.157), channel_id=1, source_target_pairs={{0,2},{1,3},{2,4},{3,5},{4,6},{5,7},{6,0},{7,1},{8,10},{9,11},{10,... | collective-permute-start | bytes 3145736 | tf_op jit(solution)/shard_map/ppermute | solution.py:411
  42.8 6.5 %collective-permute-start.10 = (f32[8,128]{1,0:T(8,128)S(1)}, f32[8,128]{1,0:T(8,128)S(1)}, u32[]{:S(2)}, u32[]{:S(2)}) collective-permute-start(f32[8,128]{1,0:T(8,128)S(1)} %maximum_maximum_fusion.2), channel_id=1, source_target_pairs={{0,1},{1,0},{2,3},{3,2},{4,5},{5,4},{6,7},{7,6},{8,9},{9,8},{10,11... | collective-permute-start | bytes 12296 | tf_op jit(solution)/shard_map/ppermute | solution.py:408
  54.4 13.8 %collective-permute-start.14 = (f32[8,128]{1,0:T(8,128)S(1)}, f32[8,128]{1,0:T(8,128)S(1)}, u32[]{:S(2)}, u32[]{:S(2)}) collective-permute-start(f32[8,128]{1,0:T(8,128)S(1)} %maximum_maximum_fusion.1), channel_id=1, source_target_pairs={{0,16},{8,24},{16,0},{24,8},{32,48},{40,56},{48,32},{56,40},{64,80... | collective-permute-start | bytes 12296 | tf_op jit(solution)/shard_map/ppermute | solution.py:417
  58.7 9.5 %collective-permute-start.15 = (f32[8,128]{1,0:T(8,128)S(1)}, f32[8,128]{1,0:T(8,128)S(1)}, u32[]{:S(2)}, u32[]{:S(2)}) collective-permute-start(f32[8,128]{1,0:T(8,128)S(1)} %maximum_maximum_fusion.1), channel_id=1, source_target_pairs={{0,8},{8,16},{16,24},{24,0},{32,40},{40,48},{48,56},{56,32},{64,72... | collective-permute-start | bytes 12296 | tf_op jit(solution)/shard_map/ppermute | solution.py:417
  59.3 8.9 %collective-permute-start.16 = (f32[8,128]{1,0:T(8,128)S(1)}, f32[8,128]{1,0:T(8,128)S(1)}, u32[]{:S(2)}, u32[]{:S(2)}) collective-permute-start(f32[8,128]{1,0:T(8,128)S(1)} %maximum_maximum_fusion.1), channel_id=1, source_target_pairs={{0,24},{8,0},{16,8},{24,16},{32,56},{40,32},{48,40},{56,48},{64,88... | collective-permute-start | bytes 12296 | tf_op jit(solution)/shard_map/ppermute | solution.py:417
  65.7 13.0 %collective-permute-start.8 = (f16[2048,128]{1,0:T(8,128)(2,1)S(1)}, f16[2048,128]{1,0:T(8,128)(2,1)S(1)}, u32[]{:S(2)}, u32[]{:S(2)}) collective-permute-start(f16[2048,128]{1,0:T(8,128)(2,1)S(1)} %multiply_convert_fusion.5), channel_id=1, source_target_pairs={{0,2},{1,3},{2,4},{3,5},{4,6},{5,7},{6,0},{7,1},{8,10},{9,11},{10,... | collective-permute-start | bytes 1572872 | tf_op jit(solution)/shard_map/ppermute | solution.py:411
  68.2 13.5 %collective-permute-start.9 = (f16[2048,128]{1,0:T(8,128)(2,1)S(1)}, f16[2048,128]{1,0:T(8,128)(2,1)S(1)}, u32[]{:S(2)}, u32[]{:S(2)}) collective-permute-start(f16[2048,128]{1,0:T(8,128)(2,1)S(1)} %multiply_convert_fusion.4), channel_id=1, source_target_pairs={{0,6},{1,7},{2,0},{3,1},{4,2},{5,3},{6,4},{7,5},{8,14},{9,15},{10,... | collective-permute-start | bytes 1572872 | tf_op jit(solution)/shard_map/ppermute | solution.py:411
  129.7 21.3 %collective-permute-start.17 = (f32[128,128]{1,0:T(8,128)}, f32[128,128]{1,0:T(8,128)S(1)}, u32[]{:S(2)}, u32[]{:S(2)}) collective-permute-start(f32[128,128]{1,0:T(8,128)} %get-tuple-element.82), channel_id=1, source_target_pairs={{0,64},{8,72},{16,80},{24,88},{32,96},{40,104},{48,112},{56,120},{... | collective-permute-start | bytes 196616 | tf_op jit(solution)/shard_map/ppermute | solution.py:414
  129.8 21.2 %collective-permute-start.18 = (f32[128,128]{1,0:T(8,128)}, f32[128,128]{1,0:T(8,128)S(1)}, u32[]{:S(2)}, u32[]{:S(2)}) collective-permute-start(f32[128,128]{1,0:T(8,128)} %get-tuple-element.82), channel_id=1, source_target_pairs={{0,32},{8,40},{16,48},{24,56},{32,64},{40,72},{48,80},{56,88},{64,... | collective-permute-start | bytes 196616 | tf_op jit(solution)/shard_map/ppermute | solution.py:414
  129.8 21.1 %collective-permute-start.19 = (f32[128,128]{1,0:T(8,128)}, f32[128,128]{1,0:T(8,128)S(1)}, u32[]{:S(2)}, u32[]{:S(2)}) collective-permute-start(f32[128,128]{1,0:T(8,128)} %get-tuple-element.82), channel_id=1, source_target_pairs={{0,96},{8,104},{16,112},{24,120},{32,0},{40,8},{48,16},{56,24},{64... | collective-permute-start | bytes 196616 | tf_op jit(solution)/shard_map/ppermute | solution.py:414
  150.9 42.8 %collective-permute-start.24 = (f16[4096,128]{1,0:T(8,128)(2,1)}, f16[4096,128]{1,0:T(8,128)(2,1)}, u32[]{:S(2)}, u32[]{:S(2)}) collective-permute-start(f16[4096,128]{1,0:T(8,128)(2,1)} %bitcast.23), channel_id=1, source_target_pairs={{0,96},{8,104},{16,112},{24,120},{32,0},{40,8},{48,16},{56,24},{64... | collective-permute-start | bytes 3145736 | tf_op jit(solution)/shard_map/ppermute | solution.py:414
  151.0 11.8 %collective-permute-start.20 = (f32[128,128]{1,0:T(8,128)S(1)}, f32[128,128]{1,0:T(8,128)S(1)}, u32[]{:S(2)}, u32[]{:S(2)}) collective-permute-start(f32[128,128]{1,0:T(8,128)S(1)} %add_add_fusion.1), channel_id=1, source_target_pairs={{0,16},{8,24},{16,0},{24,8},{32,48},{40,56},{48,32},{56,40},{64,80... | collective-permute-start | bytes 196616 | tf_op jit(solution)/shard_map/ppermute | solution.py:417
  155.1 7.6 %collective-permute-start.21 = (f32[128,128]{1,0:T(8,128)S(1)}, f32[128,128]{1,0:T(8,128)S(1)}, u32[]{:S(2)}, u32[]{:S(2)}) collective-permute-start(f32[128,128]{1,0:T(8,128)S(1)} %add_add_fusion.1), channel_id=1, source_target_pairs={{0,8},{8,16},{16,24},{24,0},{32,40},{40,48},{48,56},{56,32},{64,72... | collective-permute-start | bytes 196616 | tf_op jit(solution)/shard_map/ppermute | solution.py:417
  156.9 5.9 %collective-permute-start.22 = (f32[128,128]{1,0:T(8,128)S(1)}, f32[128,128]{1,0:T(8,128)S(1)}, u32[]{:S(2)}, u32[]{:S(2)}) collective-permute-start(f32[128,128]{1,0:T(8,128)S(1)} %add_add_fusion.1), channel_id=1, source_target_pairs={{0,24},{8,0},{16,8},{24,16},{32,56},{40,32},{48,40},{56,48},{64,88... | collective-permute-start | bytes 196616 | tf_op jit(solution)/shard_map/ppermute | solution.py:417
  160.8 34.7 %collective-permute-start.23 = (f16[4096,128]{1,0:T(8,128)(2,1)}, f16[4096,128]{1,0:T(8,128)(2,1)}, u32[]{:S(2)}, u32[]{:S(2)}) collective-permute-start(f16[4096,128]{1,0:T(8,128)(2,1)} %bitcast.22), channel_id=1, source_target_pairs={{0,32},{8,40},{16,48},{24,56},{32,64},{40,72},{48,80},{56,88},{64,... | collective-permute-start | bytes 3145736 | tf_op jit(solution)/shard_map/ppermute | solution.py:414
  167.3 33.0 %collective-permute-start.31 = (f16[4096,128]{1,0:T(8,128)(2,1)}, f16[4096,128]{1,0:T(8,128)(2,1)}, u32[]{:S(2)}, u32[]{:S(2)}) collective-permute-start(f16[4096,128]{1,0:T(8,128)(2,1)} %bitcast.33), channel_id=1, source_target_pairs={{0,24},{8,0},{16,8},{24,16},{32,56},{40,32},{48,40},{56,48},{64,88... | collective-permute-start | bytes 3145736 | tf_op jit(solution)/shard_map/ppermute | solution.py:417
  170.7 31.1 %collective-permute-start.30 = (f16[4096,128]{1,0:T(8,128)(2,1)}, f16[4096,128]{1,0:T(8,128)(2,1)S(1)}, u32[]{:S(2)}, u32[]{:S(2)}) collective-permute-start(f16[4096,128]{1,0:T(8,128)(2,1)} %bitcast.32), channel_id=1, source_target_pairs={{0,8},{8,16},{16,24},{24,0},{32,40},{40,48},{48,56},{56,32},{64,72... | collective-permute-start | bytes 3145736 | tf_op jit(solution)/shard_map/ppermute | solution.py:417
  196.9 12.3 %collective-permute-start.25 = (f16[2048,128]{1,0:T(8,128)(2,1)S(1)}, f16[2048,128]{1,0:T(8,128)(2,1)S(1)}, u32[]{:S(2)}, u32[]{:S(2)}) collective-permute-start(f16[2048,128]{1,0:T(8,128)(2,1)S(1)} %fusion.14), channel_id=1, source_target_pairs={{0,32},{8,40},{16,48},{24,56},{32,64},{40,72},{48,80},{56,88},{64,... | collective-permute-start | bytes 1572872 | tf_op jit(solution)/shard_map/ppermute | solution.py:414
  199.0 10.6 %collective-permute-start.26 = (f16[2048,128]{1,0:T(8,128)(2,1)S(1)}, f16[2048,128]{1,0:T(8,128)(2,1)S(1)}, u32[]{:S(2)}, u32[]{:S(2)}) collective-permute-start(f16[2048,128]{1,0:T(8,128)(2,1)S(1)} %fusion.12), channel_id=1, source_target_pairs={{0,96},{8,104},{16,112},{24,120},{32,0},{40,8},{48,16},{56,24},{64... | collective-permute-start | bytes 1572872 | tf_op jit(solution)/shard_map/ppermute | solution.py:414
  202.0 14.8 %collective-permute-start.32 = (f16[2048,128]{1,0:T(8,128)(2,1)S(1)}, f16[2048,128]{1,0:T(8,128)(2,1)S(1)}, u32[]{:S(2)}, u32[]{:S(2)}) collective-permute-start(f16[2048,128]{1,0:T(8,128)(2,1)S(1)} %fusion.10), channel_id=1, source_target_pairs={{0,8},{8,16},{16,24},{24,0},{32,40},{40,48},{48,56},{56,32},{64,72... | collective-permute-start | bytes 1572872 | tf_op jit(solution)/shard_map/ppermute | solution.py:417
  202.4 14.4 %collective-permute-start.33 = (f16[2048,128]{1,0:T(8,128)(2,1)S(1)}, f16[2048,128]{1,0:T(8,128)(2,1)S(1)}, u32[]{:S(2)}, u32[]{:S(2)}) collective-permute-start(f16[2048,128]{1,0:T(8,128)(2,1)S(1)} %fusion.8), channel_id=1, source_target_pairs={{0,24},{8,0},{16,8},{24,16},{32,56},{40,32},{48,40},{56,48},{64,88... | collective-permute-start | bytes 1572872 | tf_op jit(solution)/shard_map/ppermute | solution.py:417
  211.8 16.7 %collective-permute-start.28 = (f16[1024,128]{1,0:T(8,128)(2,1)}, f16[1024,128]{1,0:T(8,128)(2,1)}, u32[]{:S(2)}, u32[]{:S(2)}) collective-permute-start(f16[1024,128]{1,0:T(8,128)(2,1)} %get-tuple-element.131), channel_id=1, source_target_pairs={{0,24},{8,0},{16,8},{24,16},{32,56},{40,32},{48,40},{56,48},{64,88... | collective-permute-start | bytes 786440 | tf_op jit(solution)/shard_map/ppermute | solution.py:417
  214.7 13.8 %collective-permute-start.29 = (f16[1024,128]{1,0:T(8,128)(2,1)S(1)}, f16[1024,128]{1,0:T(8,128)(2,1)}, u32[]{:S(2)}, u32[]{:S(2)}) collective-permute-start(f16[1024,128]{1,0:T(8,128)(2,1)S(1)} %get-tuple-element.132), channel_id=1, source_target_pairs={{0,16},{8,24},{16,0},{24,8},{32,48},{40,56},{48,32},{56,40},{64,80... | collective-permute-start | bytes 786440 | tf_op jit(solution)/shard_map/ppermute | solution.py:417
  215.9 10.2 %collective-permute-start.27 = (f16[1024,128]{1,0:T(8,128)(2,1)S(1)}, f16[1024,128]{1,0:T(8,128)(2,1)S(1)}, u32[]{:S(2)}, u32[]{:S(2)}) collective-permute-start(f16[1024,128]{1,0:T(8,128)(2,1)S(1)} %fusion.41), channel_id=1, source_target_pairs={{0,8},{8,16},{16,24},{24,0},{32,40},{40,48},{48,56},{56,32},{64,72... | collective-permute-start | bytes 786440 | tf_op jit(solution)/shard_map/ppermute | solution.py:417
  218.9 13.7 %collective-permute-start.34 = (f16[1024,128]{1,0:T(8,128)(2,1)}, f16[1024,128]{1,0:T(8,128)(2,1)}, u32[]{:S(2)}, u32[]{:S(2)}) collective-permute-start(f16[1024,128]{1,0:T(8,128)(2,1)} %fusion.24), channel_id=1, source_target_pairs={{0,32},{8,40},{16,48},{24,56},{32,64},{40,72},{48,80},{56,88},{64,... | collective-permute-start | bytes 786440 | tf_op jit(solution)/shard_map/ppermute | solution.py:414
  220.5 12.1 %collective-permute-start.35 = (f16[1024,128]{1,0:T(8,128)(2,1)}, f16[1024,128]{1,0:T(8,128)(2,1)S(1)}, u32[]{:S(2)}, u32[]{:S(2)}) collective-permute-start(f16[1024,128]{1,0:T(8,128)(2,1)} %get-tuple-element.133), channel_id=1, source_target_pairs={{0,96},{8,104},{16,112},{24,120},{32,0},{40,8},{48,16},{56,24},{64... | collective-permute-start | bytes 786440 | tf_op jit(solution)/shard_map/ppermute | solution.py:414
  226.1 8.1 %collective-permute-start.36 = (f16[1024,128]{1,0:T(8,128)(2,1)}, f16[1024,128]{1,0:T(8,128)(2,1)S(1)}, u32[]{:S(2)}, u32[]{:S(2)}) collective-permute-start(f16[1024,128]{1,0:T(8,128)(2,1)} %get-tuple-element.134), channel_id=1, source_target_pairs={{0,64},{8,72},{16,80},{24,88},{32,96},{40,104},{48,112},{56,120},{... | collective-permute-start | bytes 786440 | tf_op jit(solution)/shard_map/ppermute | solution.py:414
  (24 other events, 166.4 us)
